TPU v7x, 1024 devices: a whole 4x8x16 slice. The times are simulated.
1024 devices in a mesh: dp: 64 (over x, y, core), mp: 16 (over z).
Axes of the slice: x: 4, y: 8, z: 16, core: 2. Of those that a mesh axis runs over, the one named last changes fastest.
Arguments:
- query_rows: bfloat16 [16384, 6144], P('dp', 'mp'), may hold values from -6 to 6
- key_rows: bfloat16 [16384, 6144], P('dp', 'mp'), may hold values from -6 to 6
- value_rows: bfloat16 [16384, 6144], P('dp', 'mp'), may hold values from -6 to 6
- proj_weight: bfloat16 [6144, 6144], P('mp'), may hold values from -0.078125 to 0.078125
- out_grad: bfloat16 [16384, 6144], P('dp', 'mp'), may hold values from -6 to 6
- image_starts: int32 [64, 256], replicated, may hold values from -1 to 128, as said below
Outputs:
- projected: bfloat16 [16384, 6144], P('dp', 'mp')
- grad_query: bfloat16 [16384, 6144], P('dp', 'mp')
- grad_key: bfloat16 [16384, 6144], P('dp', 'mp')
- grad_value: bfloat16 [16384, 6144], P('dp', 'mp')
Inputs may be any that keep to these rules, and one draw needn't show every extreme that they name: `image_starts`: each used row holds the index, within its pack, of the first row of its image; unused rows hold -1. A pack's used rows come first without gaps and its images are contiguous. Images begin only at rows 0, 64 and 128; one at 64 only in packs that use more than 128 rows. The data loader fills packs two at a time, splitting one batch of images between them, so packs t and t + 32 form a pair: one of them uses all of its first 128 rows, has an image beginning at row 128 that runs to its last used row, and uses some rows past it; the other uses fewer than 128 rows; together they use exactly 256 rows.
All inputs are finite; a program needn't handle non-finite values.
Results may differ from a plain program's by a relative error of at most 0.022.
Values may be sent and summed in bfloat16 or wider, within the bound.
No kernel may reach another device: no remote copies, remote signals or barrier semaphores. Data moves between devices by JAX's collectives and lax.ppermute only.
A program may use at most 32 MiB of HBM per device.

v0:
```python
import math

import jax
import jax.numpy as jnp
from jax import lax
from jax.sharding import PartitionSpec as P

HEAD_DIM = 128


def pack_pass(query_rows, key_rows, value_rows, out_grad, starts, proj_weight):
    row_count = query_rows.shape[0]
    head_count = proj_weight.shape[0] // HEAD_DIM
    root_dim = math.sqrt(HEAD_DIM)
    query_heads = query_rows.reshape(row_count, head_count, HEAD_DIM)
    key_heads = key_rows.reshape(row_count, head_count, HEAD_DIM)
    value_heads = value_rows.reshape(row_count, head_count, HEAD_DIM)
    same_image = starts[:, None] == starts[None, :]
    valid_rows = (starts >= 0)[:, None]
    scores = (
        jnp.einsum("qhd,khd->hqk", query_heads, key_heads, preferred_element_type=jnp.float32)
        / root_dim
    )
    scores = jnp.where(same_image[None], scores, -jnp.inf)
    maxima = jnp.max(scores, axis=2, keepdims=True)
    weights = jnp.exp(scores - maxima)
    probabilities = weights / jnp.sum(weights, axis=2, keepdims=True)
    rounded = probabilities.astype(jnp.bfloat16)
    attended = jnp.einsum(
        "hqk,khd->qhd", rounded, value_heads, preferred_element_type=jnp.float32
    ).reshape(row_count, -1)
    attended = jnp.where(valid_rows, attended, 0.0).astype(jnp.bfloat16)
    head_terms = jnp.dot(attended, proj_weight, preferred_element_type=jnp.float32)
    projected = lax.psum_scatter(
        head_terms.astype(jnp.bfloat16), "mp", scatter_dimension=1, tiled=True
    )
    grad_attended = lax.dot_general(
        lax.all_gather(out_grad, "mp", axis=1, tiled=True),
        proj_weight,
        (((1,), (1,)), ((), ())),
        preferred_element_type=jnp.float32,
    ).astype(jnp.bfloat16)
    grad_heads = grad_attended.reshape(row_count, head_count, HEAD_DIM)
    grad_value = jnp.einsum("hqk,qhd->khd", rounded, grad_heads, preferred_element_type=jnp.float32)
    grad_weights = jnp.einsum(
        "qhd,khd->hqk", grad_heads, value_heads, preferred_element_type=jnp.float32
    )
    correction = jnp.sum(probabilities * grad_weights, axis=2, keepdims=True)
    grad_scores = (probabilities * (grad_weights - correction) / root_dim).astype(jnp.bfloat16)
    grad_query = jnp.einsum(
        "hqk,khd->qhd", grad_scores, key_heads, preferred_element_type=jnp.float32
    )
    grad_key = jnp.einsum(
        "hqk,qhd->khd", grad_scores, query_heads, preferred_element_type=jnp.float32
    )

    def finish(gradient):
        return jnp.where(valid_rows, gradient.reshape(row_count, -1), 0.0).astype(jnp.bfloat16)

    return (projected, finish(grad_query), finish(grad_key), finish(grad_value))


def shards(query_rows, key_rows, value_rows, proj_weight, out_grad, image_starts):
    device_index = lax.axis_index("dp")
    own_starts = lax.dynamic_index_in_dim(image_starts, device_index, 0, keepdims=False)
    return pack_pass(query_rows, key_rows, value_rows, out_grad, own_starts, proj_weight)


def solution(mesh):
    placed = (P("dp", "mp"), P("dp", "mp"), P("dp", "mp"), P("mp", None), P("dp", "mp"), P())
    return jax.shard_map(
        shards,
        mesh=mesh,
        in_specs=placed,
        out_specs=(P("dp", "mp"), P("dp", "mp"), P("dp", "mp"), P("dp", "mp")),
        check_vma=False,
    )
```

profile of v0, /device:TPU:4, one launch (start us, length us, event | category | flops | bytes accessed | tf_op | source)
XLA Modules:
  0.0 187.1 jit_solution(4557154574370482926)
XLA Ops:
  7.2 0.0 copy-start
  7.2 0.0 all-gather.2.cloned.1.call-start
  7.2 0.7 all-gather.2.cloned.1.call-update
  7.9 0.0 reduce-scatter.4.cloned.1.call-start
  8.0 1.1 copy.42
  9.0 0.0 copy-start.1
  9.0 1.1 copy.43
  10.2 0.0 copy-start.3
  10.2 1.1 copy.46
  11.4 0.1 broadcast_compare_fusion
  11.5 1.3 fusion.31
  12.8 0.6 fusion.20
  13.4 0.8 copy.48
  14.2 0.0 copy-done.3
  14.2 4.3 %convolution_convert_fusion = bf16[256,6144]{1,0:T(8,128)(2,1)S(1)} fusion(bf16[384,6144]{1,0:T(8,128)(2,1)} %param.9, bf16[256,384]{1,0:T(8,128)(2,1)} %copy.48, pred[256]{0:T(512)(128)(4,1)S(1)} %broadcast_compare_fusion.1), kind=kOutput, calls=%fused_computation.2 | convolution fusion | flops 1209630720 | bytes 8061184 | tf_op jit(solution)/shard_map/dot_general | solution.py:33
  18.5 2.8 %copy.66 = bf16[256,6144]{0,1:T(8,128)(2,1)} copy(bf16[256,6144]{1,0:T(8,128)(2,1)S(1)} %convolution_convert_fusion) | data formatting | bytes 6291456
  21.4 0.0 reduce-scatter.4.cloned.1.call-update
  21.4 0.0 copy-start.2
  21.4 77.5 %all-gather.2.cloned.1.call-done = bf16[256,6144]{1,0:T(8,128)(2,1)} async-done(((bf16[256,384]{1,0:T(8,128)(2,1)}), bf16[256,6144]{1,0:T(8,128)(2,1)}) %all-gather.2.cloned.1.call-update) | async-done | bytes 3145744 | tf_op jit(solution)/shard_map/all_gather | solution.py:38
  98.9 5.1 %convolution_convert_fusion.1 = bf16[256,384]{1,0:T(8,128)(2,1)S(1)} fusion(bf16[256,6144]{1,0:T(8,128)(2,1)} %all-gather.2.cloned.1.call-done, bf16[384,6144]{1,0:T(8,128)(2,1)} %param.9), kind=kOutput, calls=%fused_computation.11 | convolution fusion | flops 1208057856 | bytes 8060928 | tf_op jit(solution)/shard_map/dot_general | solution.py:37
  104.0 0.0 copy-start.4
  104.0 0.1 copy.49
  104.2 0.3 fusion.32
  104.5 1.8 fusion.9
  106.3 0.2 copy.55
  106.5 1.8 fusion.10
  108.3 0.2 copy.53
  108.5 0.7 fusion.18
  109.1 0.2 copy.57
  109.3 1.0 select_convert_fusion
  110.3 68.3 %reduce-scatter.4.cloned.1.call-done = bf16[384,256]{1,0:T(8,128)(2,1)} async-done(((bf16[6144,256]{1,0:T(8,128)(2,1)}), bf16[384,256]{1,0:T(8,128)(2,1)}) %reduce-scatter.4.cloned.1.call-update) | async-done | bytes 196624
  178.5 1.7 copy.67
  (6 shorter events, 0.0 us)
Async XLA Ops:
  7.2 4.2 %copy-start = (s32[64,256]{1,0:T(8,128)S(1)}, s32[64,256]{1,0:T(8,128)}, u32[]{:S(2)}) copy-start(s32[64,256]{1,0:T(8,128)} %param.11) | copy-start | bytes 196612
  7.2 91.7 %all-gather.2.cloned.1.call-start = ((), (), s32[]{:S(2)}) async-start(), calls=%async_computation.1 | async-start | bytes 3342336 | tf_op jit(solution)/shard_map/all_gather | solution.py:38
  7.9 170.6 %reduce-scatter.4.cloned.1.call-start = ((), (), s32[]{:S(2)}) async-start(), calls=%async_computation.2 | async-start | bytes 3342336
  9.0 5.2 %copy-start.1 = (bf16[256,384]{0,1:T(8,128)(2,1)}, bf16[256,384]{0,1:T(8,128)(2,1)S(1)}, u32[]{:S(2)}) copy-start(bf16[256,384]{0,1:T(8,128)(2,1)S(1)} %copy.42) | copy-start | bytes 589828
  10.2 4.1 %copy-start.3 = (bf16[256,384]{0,1:T(8,128)(2,1)}, bf16[256,384]{0,1:T(8,128)(2,1)S(1)}, u32[]{:S(2)}) copy-start(bf16[256,384]{0,1:T(8,128)(2,1)S(1)} %copy.43) | copy-start | bytes 589828
  21.4 83.1 %copy-start.2 = (bf16[256,384]{0,1:T(8,128)(2,1)S(1)}, bf16[256,384]{0,1:T(8,128)(2,1)}, u32[]{:S(2)}) copy-start(bf16[256,384]{0,1:T(8,128)(2,1)} %copy-done.1) | copy-start | bytes 589828
  104.0 2.5 %copy-start.4 = (bf16[256,384]{0,1:T(8,128)(2,1)S(1)}, bf16[256,384]{0,1:T(8,128)(2,1)}, u32[]{:S(2)}) copy-start(bf16[256,384]{0,1:T(8,128)(2,1)} %copy-done.3) | copy-start | bytes 589828
Sparse Core Ops, SparseCore 0:
  10.7 88.1 all-gather.1
  102.3 76.1 reduce-scatter.3
where the time goes:
time: 187 us
  waiting for transfers between devices  146 us (78%)
  matrix products  15.9 us (9%)
  between operations  14.2 us (8%)
  local copies, waits for them, and re-layouts  9.41 us (5%)
    all_gather x1, waiting for transfers between devices, pack_pass(): lax.all_gather(out_grad, 'mp', axis=1, tiled=True)  77.5 us
    unnamed x3, waiting for transfers between devices  69 us
    unnamed x15, local copies, waits for them, and re-layouts  7.93 us
    dot_general x1, matrix products, pack_pass(): lax.dot_general(lax.all_gather(out_grad, 'mp', axis=1, tiled=True), proj_...  5.1 us
    dot_general x1, matrix products, pack_pass(): jnp.dot(attended, proj_weight, preferred_element_type=jnp.float32)  4.28 us
  transfers between devices with their start and end apart: 2, of which 2 were waited for; matrix products, arithmetic and copies ran while one was open for 13% of the time, Pallas kernels for 0%

commit v1 on v0

--- a/solution.py
+++ b/solution.py
@@ -6,12 +6,77 @@
 from jax.sharding import PartitionSpec as P
 
 HEAD_DIM = 128
+SLOT = 128
 
 
-def pack_pass(query_rows, key_rows, value_rows, out_grad, starts, proj_weight):
+def ring_pairs(dp_size, mp_size):
+    pairs = []
+    for dp in range(dp_size):
+        step = 1 if goes_right(dp, dp_size) else mp_size - 1
+        for z in range(mp_size):
+            pairs.append((dp * mp_size + z, dp * mp_size + (z + step) % mp_size))
+    return pairs
+
+
+def goes_right(dp, dp_size):
+    return (dp // (dp_size // 2) + dp) % 2 == 0
+
+
+def dot(a, b, dims=(((1,), (0,)), ((), ()))):
+    return lax.dot_general(a, b, dims, preferred_element_type=jnp.float32)
+
+
+def shards(query_rows, key_rows, value_rows, proj_weight, out_grad, image_starts):
+    dp_size, mp_size = lax.axis_size("dp"), lax.axis_size("mp")
+    half_ring = mp_size // 2
+    dp, z = lax.axis_index("dp"), lax.axis_index("mp")
+    ring_perm = ring_pairs(dp_size, mp_size)
+    swap_perm = [(i, (i + dp_size // 2) % dp_size) for i in range(dp_size)]
+    right = goes_right(dp, dp_size)
+    delta = jnp.where(right, 1, mp_size - 1)
+    starts = lax.dynamic_index_in_dim(image_starts, dp, 0, keepdims=False)
+    other_starts = lax.dynamic_index_in_dim(
+        image_starts, (dp + dp_size // 2) % dp_size, 0, keepdims=False
+    )
+    heavy = starts[SLOT - 1] >= 0
+    light_count = jnp.sum((jnp.where(heavy, other_starts, starts) >= 0).astype(jnp.int32))
+    from_light = (jnp.arange(SLOT) < light_count)[:, None]
+    flip = (jnp.arange(SLOT)[:, None] + jnp.arange(SLOT)[None, :] == SLOT - 1).astype(jnp.bfloat16)
+
+    def ring(rows):
+        return lax.ppermute(rows, ("dp", "mp"), ring_perm)
+
+    def swap(rows):
+        return lax.ppermute(rows, "dp", swap_perm)
+
+    def pack(own, other):
+        heavy_rows = jnp.where(heavy, own, other)
+        light_rows = jnp.where(heavy, other[:SLOT], own[:SLOT])
+        flipped = dot(flip, heavy_rows[SLOT:]).astype(jnp.bfloat16)
+        return jnp.concatenate([heavy_rows[:SLOT], jnp.where(from_light, light_rows, flipped)], 0)
+
+    def unpack(rows):
+        first = jnp.where(heavy, rows[:SLOT], rows[SLOT:])
+        return jnp.concatenate([first, dot(flip, rows[SLOT:]).astype(jnp.bfloat16)], 0)
+
+    def half_of(rows):
+        return jnp.where(right, rows[:SLOT], rows[SLOT:])
+
+    def place_half(rows):
+        zeros = jnp.zeros_like(rows)
+        return jnp.concatenate([jnp.where(right, rows, zeros), jnp.where(right, zeros, rows)], 0)
+
+    width = query_rows.shape[1]
+
+    def weight_block(index):
+        return lax.dynamic_slice_in_dim(proj_weight, (index % mp_size) * width, width, 1)
+
     row_count = query_rows.shape[0]
-    head_count = proj_weight.shape[0] // HEAD_DIM
+    head_count = width // HEAD_DIM
     root_dim = math.sqrt(HEAD_DIM)
+
+    other_grad = swap(out_grad)
+
     query_heads = query_rows.reshape(row_count, head_count, HEAD_DIM)
     key_heads = key_rows.reshape(row_count, head_count, HEAD_DIM)
     value_heads = value_rows.reshape(row_count, head_count, HEAD_DIM)
@@ -29,17 +94,44 @@
     attended = jnp.einsum(
         "hqk,khd->qhd", rounded, value_heads, preferred_element_type=jnp.float32
     ).reshape(row_count, -1)
-    attended = jnp.where(valid_rows, attended, 0.0).astype(jnp.bfloat16)
-    head_terms = jnp.dot(attended, proj_weight, preferred_element_type=jnp.float32)
-    projected = lax.psum_scatter(
-        head_terms.astype(jnp.bfloat16), "mp", scatter_dimension=1, tiled=True
+    attended = attended.astype(jnp.bfloat16)
+    other_attended = swap(attended)
+
+    pair_grad = pack(out_grad, other_grad)
+    pair_attended = pack(attended, other_attended)
+    partial = place_half(
+        dot(half_of(pair_grad), weight_block(z), (((1,), (1,)), ((), ())))
     )
-    grad_attended = lax.dot_general(
-        lax.all_gather(out_grad, "mp", axis=1, tiled=True),
-        proj_weight,
-        (((1,), (1,)), ((), ())),
-        preferred_element_type=jnp.float32,
-    ).astype(jnp.bfloat16)
+    terms = dot(pair_attended, proj_weight).astype(jnp.bfloat16)
+
+    def term(index):
+        return lax.dynamic_slice_in_dim(terms, (index % mp_size) * width, width, 1)
+
+    block = pair_grad
+    total = half_of(term(z + half_ring * delta))
+    for step in range(1, half_ring + 1):
+        block = ring(half_of(block) if step == half_ring else block)
+        received = ring(total)
+        product = dot(block, weight_block(z + step * (mp_size - delta)), (((1,), (1,)), ((), ())))
+        if step == half_ring:
+            product = place_half(product)
+        partial = partial + product
+        if step == 1:
+            received = place_half(received)
+        own = term(z + (half_ring - step) * delta)
+        if step == half_ring:
+            own = place_half(half_of(own))
+        total = received.astype(jnp.float32) + own.astype(jnp.float32)
+        if step < half_ring:
+            total = total.astype(jnp.bfloat16)
+
+    grad_pair = (partial + swap(partial.astype(jnp.bfloat16)).astype(jnp.float32)).astype(jnp.bfloat16)
+    grad_attended = unpack(grad_pair)
+    projected = unpack(
+        (total + swap(total.astype(jnp.bfloat16)).astype(jnp.float32)).astype(jnp.bfloat16)
+    )
+    projected = jnp.where(valid_rows, projected, 0)
+
     grad_heads = grad_attended.reshape(row_count, head_count, HEAD_DIM)
     grad_value = jnp.einsum("hqk,qhd->khd", rounded, grad_heads, preferred_element_type=jnp.float32)
     grad_weights = jnp.einsum(
@@ -60,12 +152,6 @@
     return (projected, finish(grad_query), finish(grad_key), finish(grad_value))
 
 
-def shards(query_rows, key_rows, value_rows, proj_weight, out_grad, image_starts):
-    device_index = lax.axis_index("dp")
-    own_starts = lax.dynamic_index_in_dim(image_starts, device_index, 0, keepdims=False)
-    return pack_pass(query_rows, key_rows, value_rows, out_grad, own_starts, proj_weight)
-
-
 def solution(mesh):
     placed = (P("dp", "mp"), P("dp", "mp"), P("dp", "mp"), P("mp", None), P("dp", "mp"), P())
     return jax.shard_map(

time: 187 us -> 127 us (0.68)
  the two profiles are of different devices: /device:TPU:4 before, /device:TPU:14 now
where the time goes in v1:
time: 127 us; the launch traced here: 126 us
  starting transfers between devices  91 us (72%)
  waiting for transfers between devices  11.7 us (9%)
  matrix products  11.4 us (9%)
  local copies, waits for them, and re-layouts  6.17 us (5%)
  other arithmetic  3.4 us (3%)
  between operations  2.3 us (2%)
    ppermute x16, starting transfers between devices, ring(): return lax.ppermute(rows, ('dp', 'mp'), ring_perm)  77.2 us
    ppermute x4, starting transfers between devices, swap(): return lax.ppermute(rows, 'dp', swap_perm)  13.8 us
    dot_general x14, matrix products, dot(): return lax.dot_general(a, b, dims, preferred_element_type=jnp.float32)  8.55 us
    ppermute x4, waiting for transfers between devices, swap(): return lax.ppermute(rows, 'dp', swap_perm)  6.16 us
    ppermute x16, waiting for transfers between devices, ring(): return lax.ppermute(rows, ('dp', 'mp'), ring_perm)  5.51 us
    unnamed x9, local copies, waits for them, and re-layouts  3.21 us
  transfers between devices with their start and end apart: 20, of which 6 were waited for; matrix products, arithmetic and copies ran while one was open for 10% of the time, Pallas kernels for 0%

profile of v1, /device:TPU:14, one launch (start us, length us, event | category | flops | bytes accessed | tf_op | source)
XLA Modules:
  0.0 126.0 jit_solution(18398853758758158214)
XLA Ops:
  0.6 3.4 %collective-permute-start.10 = (bf16[256,384]{1,0:T(8,128)(2,1)}, bf16[256,384]{1,0:T(8,128)(2,1)S(1)}, u32[]{:S(2)}, u32[]{:S(2)}) collective-permute-start(bf16[256,384]{1,0:T(8,128)(2,1)} %param.10), channel_id=1, source_target_pairs={{0,512},{16,528},{32,544},{48,560},{64,576},{80,592},{96,608},{112... | collective-permute-start | bytes 589832 | tf_op jit(solution)/shard_map/ppermute | solution.py:50
  4.1 1.1 copy.28
  5.2 1.1 copy.29
  7.1 1.1 copy.32
  9.4 4.0 %collective-permute-start = (bf16[256,384]{1,0:T(8,128)(2,1)S(1)}, bf16[256,384]{1,0:T(8,128)(2,1)S(1)}, u32[]{:S(2)}, u32[]{:S(2)}) collective-permute-start(bf16[256,384]{1,0:T(8,128)(2,1)S(1)} %copy.35), channel_id=1, source_target_pairs={{0,512},{16,528},{32,544},{48,560},{64,576},{80,592},{96,608},{112... | collective-permute-start | bytes 589832 | tf_op jit(solution)/shard_map/ppermute | solution.py:50
  13.7 1.3 %dynamic-slice = s32[1,1]{1,0:T(1,128)} dynamic-slice(s32[64,256]{1,0:T(8,128)} %param.11, s32[]{:T(128)S(6)} %select_n.265, s32[]{:T(128)S(6)} %add.335), dynamic_slice_sizes={1,1} | dynamic-slice | bytes 12 | tf_op jit(solution)/shard_map/slice | solution.py:41
  17.3 1.9 %collective-permute-done = bf16[256,384]{1,0:T(8,128)(2,1)S(1)} collective-permute-done((bf16[256,384]{1,0:T(8,128)(2,1)S(1)}, bf16[256,384]{1,0:T(8,128)(2,1)S(1)}, u32[]{:S(2)}, u32[]{:S(2)}) %collective-permute-start) | collective-permute-done | bytes 196640 | tf_op jit(solution)/shard_map/ppermute | solution.py:50
  19.4 1.2 broadcast_select_fusion.5
  20.8 4.3 %convolution_convert_fusion = bf16[256,6144]{1,0:T(8,128)(2,1)S(1)} fusion(bf16[384,6144]{1,0:T(8,128)(2,1)} %param.9, bf16[128,384]{1,0:T(8,128)(2,1)S(1)} %fusion.39, bf16[128,384]{1,0:T(8,128)(2,1)S(1)} %slice.83), kind=kOutput, calls=%fused_computation.2 | convolution fusion | flops 1209925632 | bytes 8060928 | tf_op jit(solution)/shard_map/dot_general | solution.py:26
  25.3 18.2 %collective-permute-start.1 = (bf16[128,384]{1,0:T(8,128)(2,1)S(1)}, bf16[128,384]{1,0:T(8,128)(2,1)S(1)}, u32[]{:S(2)}, u32[]{:S(2)}) collective-permute-start(bf16[128,384]{1,0:T(8,128)(2,1)S(1)} %get-tuple-element.6), channel_id=1, source_target_pairs={{0,1},{1,2},{2,3},{3,4},{4,5},{5,6},{6,7},{7,8},{8,9},{9,10},{10,1... | collective-permute-start | bytes 294920 | tf_op jit(solution)/shard_map/ppermute | solution.py:47
  43.5 2.5 %collective-permute-start.11 = (bf16[256,384]{1,0:T(8,128)(2,1)S(1)}, bf16[256,384]{1,0:T(8,128)(2,1)S(1)}, u32[]{:S(2)}, u32[]{:S(2)}) collective-permute-start(bf16[256,384]{1,0:T(8,128)(2,1)S(1)} %pad_maximum_fusion.1), channel_id=1, source_target_pairs={{0,1},{1,2},{2,3},{3,4},{4,5},{5,6},{6,7},{7,8},{8,9},{9,10},{10,1... | collective-permute-start | bytes 589832 | tf_op jit(solution)/shard_map/ppermute | solution.py:47
  46.1 5.2 %collective-permute-start.2 = (bf16[256,384]{1,0:T(8,128)(2,1)S(1)}, bf16[256,384]{1,0:T(8,128)(2,1)S(1)}, u32[]{:S(2)}, u32[]{:S(2)}) collective-permute-start(bf16[256,384]{1,0:T(8,128)(2,1)S(1)} %add_convert_fusion.8), channel_id=1, source_target_pairs={{0,1},{1,2},{2,3},{3,4},{4,5},{5,6},{6,7},{7,8},{8,9},{9,10},{10,1... | collective-permute-start | bytes 589832 | tf_op jit(solution)/shard_map/ppermute | solution.py:47
  51.3 3.4 %collective-permute-start.12 = (bf16[256,384]{1,0:T(8,128)(2,1)S(1)}, bf16[256,384]{1,0:T(8,128)(2,1)S(1)}, u32[]{:S(2)}, u32[]{:S(2)}) collective-permute-start(bf16[256,384]{1,0:T(8,128)(2,1)S(1)} %collective-permute-done.11), channel_id=1, source_target_pairs={{0,1},{1,2},{2,3},{3,4},{4,5},{5,6},{6,7},{7,8},{8,9},{9,10},{10,1... | collective-permute-start | bytes 589832 | tf_op jit(solution)/shard_map/ppermute | solution.py:47
  55.2 5.0 %collective-permute-start.3 = (bf16[256,384]{1,0:T(8,128)(2,1)S(1)}, bf16[256,384]{1,0:T(8,128)(2,1)S(1)}, u32[]{:S(2)}, u32[]{:S(2)}) collective-permute-start(bf16[256,384]{1,0:T(8,128)(2,1)S(1)} %add_convert_fusion.7), channel_id=1, source_target_pairs={{0,1},{1,2},{2,3},{3,4},{4,5},{5,6},{6,7},{7,8},{8,9},{9,10},{10,1... | collective-permute-start | bytes 589832 | tf_op jit(solution)/shard_map/ppermute | solution.py:47
  60.2 3.3 %collective-permute-start.13 = (bf16[256,384]{1,0:T(8,128)(2,1)S(1)}, bf16[256,384]{1,0:T(8,128)(2,1)S(1)}, u32[]{:S(2)}, u32[]{:S(2)}) collective-permute-start(bf16[256,384]{1,0:T(8,128)(2,1)S(1)} %collective-permute-done.12), channel_id=1, source_target_pairs={{0,1},{1,2},{2,3},{3,4},{4,5},{5,6},{6,7},{7,8},{8,9},{9,10},{10,1... | collective-permute-start | bytes 589832 | tf_op jit(solution)/shard_map/ppermute | solution.py:47
  63.9 5.1 %collective-permute-start.4 = (bf16[256,384]{1,0:T(8,128)(2,1)S(1)}, bf16[256,384]{1,0:T(8,128)(2,1)S(1)}, u32[]{:S(2)}, u32[]{:S(2)}) collective-permute-start(bf16[256,384]{1,0:T(8,128)(2,1)S(1)} %add_convert_fusion.6), channel_id=1, source_target_pairs={{0,1},{1,2},{2,3},{3,4},{4,5},{5,6},{6,7},{7,8},{8,9},{9,10},{10,1... | collective-permute-start | bytes 589832 | tf_op jit(solution)/shard_map/ppermute | solution.py:47
  69.0 3.3 %collective-permute-start.14 = (bf16[256,384]{1,0:T(8,128)(2,1)S(1)}, bf16[256,384]{1,0:T(8,128)(2,1)S(1)}, u32[]{:S(2)}, u32[]{:S(2)}) collective-permute-start(bf16[256,384]{1,0:T(8,128)(2,1)S(1)} %collective-permute-done.13), channel_id=1, source_target_pairs={{0,1},{1,2},{2,3},{3,4},{4,5},{5,6},{6,7},{7,8},{8,9},{9,10},{10,1... | collective-permute-start | bytes 589832 | tf_op jit(solution)/shard_map/ppermute | solution.py:47
  72.7 5.2 %collective-permute-start.5 = (bf16[256,384]{1,0:T(8,128)(2,1)S(1)}, bf16[256,384]{1,0:T(8,128)(2,1)S(1)}, u32[]{:S(2)}, u32[]{:S(2)}) collective-permute-start(bf16[256,384]{1,0:T(8,128)(2,1)S(1)} %add_convert_fusion.5), channel_id=1, source_target_pairs={{0,1},{1,2},{2,3},{3,4},{4,5},{5,6},{6,7},{7,8},{8,9},{9,10},{10,1... | collective-permute-start | bytes 589832 | tf_op jit(solution)/shard_map/ppermute | solution.py:47
  77.8 3.2 %collective-permute-start.15 = (bf16[256,384]{1,0:T(8,128)(2,1)S(1)}, bf16[256,384]{1,0:T(8,128)(2,1)S(1)}, u32[]{:S(2)}, u32[]{:S(2)}) collective-permute-start(bf16[256,384]{1,0:T(8,128)(2,1)S(1)} %collective-permute-done.14), channel_id=1, source_target_pairs={{0,1},{1,2},{2,3},{3,4},{4,5},{5,6},{6,7},{7,8},{8,9},{9,10},{10,1... | collective-permute-start | bytes 589832 | tf_op jit(solution)/shard_map/ppermute | solution.py:47
  81.4 5.2 %collective-permute-start.6 = (bf16[256,384]{1,0:T(8,128)(2,1)S(1)}, bf16[256,384]{1,0:T(8,128)(2,1)S(1)}, u32[]{:S(2)}, u32[]{:S(2)}) collective-permute-start(bf16[256,384]{1,0:T(8,128)(2,1)S(1)} %add_convert_fusion.4), channel_id=1, source_target_pairs={{0,1},{1,2},{2,3},{3,4},{4,5},{5,6},{6,7},{7,8},{8,9},{9,10},{10,1... | collective-permute-start | bytes 589832 | tf_op jit(solution)/shard_map/ppermute | solution.py:47
  86.7 3.1 %collective-permute-start.16 = (bf16[256,384]{1,0:T(8,128)(2,1)S(1)}, bf16[256,384]{1,0:T(8,128)(2,1)S(1)}, u32[]{:S(2)}, u32[]{:S(2)}) collective-permute-start(bf16[256,384]{1,0:T(8,128)(2,1)S(1)} %collective-permute-done.15), channel_id=1, source_target_pairs={{0,1},{1,2},{2,3},{3,4},{4,5},{5,6},{6,7},{7,8},{8,9},{9,10},{10,1... | collective-permute-start | bytes 589832 | tf_op jit(solution)/shard_map/ppermute | solution.py:47
  90.2 5.3 %collective-permute-start.7 = (bf16[256,384]{1,0:T(8,128)(2,1)S(1)}, bf16[256,384]{1,0:T(8,128)(2,1)S(1)}, u32[]{:S(2)}, u32[]{:S(2)}) collective-permute-start(bf16[256,384]{1,0:T(8,128)(2,1)S(1)} %add_convert_fusion.3), channel_id=1, source_target_pairs={{0,1},{1,2},{2,3},{3,4},{4,5},{5,6},{6,7},{7,8},{8,9},{9,10},{10,1... | collective-permute-start | bytes 589832 | tf_op jit(solution)/shard_map/ppermute | solution.py:47
  95.5 3.0 %collective-permute-start.17 = (bf16[256,384]{1,0:T(8,128)(2,1)S(1)}, bf16[256,384]{1,0:T(8,128)(2,1)S(1)}, u32[]{:S(2)}, u32[]{:S(2)}) collective-permute-start(bf16[256,384]{1,0:T(8,128)(2,1)S(1)} %collective-permute-done.16), channel_id=1, source_target_pairs={{0,1},{1,2},{2,3},{3,4},{4,5},{5,6},{6,7},{7,8},{8,9},{9,10},{10,1... | collective-permute-start | bytes 589832 | tf_op jit(solution)/shard_map/ppermute | solution.py:47
  98.9 4.2 %collective-permute-done.17 = bf16[256,384]{1,0:T(8,128)(2,1)S(1)} collective-permute-done((bf16[256,384]{1,0:T(8,128)(2,1)S(1)}, bf16[256,384]{1,0:T(8,128)(2,1)S(1)}, u32[]{:S(2)}, u32[]{:S(2)}) %collective-permute-start.17) | collective-permute-done | bytes 196640 | tf_op jit(solution)/shard_map/ppermute | solution.py:47
  103.1 4.2 %collective-permute-start.18 = (bf16[128,384]{1,0:T(8,128)(2,1)S(1)}, bf16[128,384]{1,0:T(8,128)(2,1)S(1)}, u32[]{:S(2)}, u32[]{:S(2)}) collective-permute-start(bf16[128,384]{1,0:T(8,128)(2,1)S(1)} %slice_select_fusion.1), channel_id=1, source_target_pairs={{0,1},{1,2},{2,3},{3,4},{4,5},{5,6},{6,7},{7,8},{8,9},{9,10},{10,1... | collective-permute-start | bytes 294920 | tf_op jit(solution)/shard_map/ppermute | solution.py:47
  107.4 1.9 %collective-permute-start.8 = (bf16[256,384]{1,0:T(8,128)(2,1)S(1)}, bf16[256,384]{1,0:T(8,128)(2,1)S(1)}, u32[]{:S(2)}, u32[]{:S(2)}) collective-permute-start(bf16[256,384]{1,0:T(8,128)(2,1)S(1)} %add_convert_fusion.2), channel_id=1, source_target_pairs={{0,1},{1,2},{2,3},{3,4},{4,5},{5,6},{6,7},{7,8},{8,9},{9,10},{10,1... | collective-permute-start | bytes 589832 | tf_op jit(solution)/shard_map/ppermute | solution.py:47
  110.2 3.8 %collective-permute-start.19 = (bf16[256,384]{1,0:T(8,128)(2,1)S(1)}, bf16[256,384]{1,0:T(8,128)(2,1)S(1)}, u32[]{:S(2)}, u32[]{:S(2)}) collective-permute-start(bf16[256,384]{1,0:T(8,128)(2,1)S(1)} %get-tuple-element.19), channel_id=1, source_target_pairs={{0,512},{16,528},{32,544},{48,560},{64,576},{80,592},{96,608},{112... | collective-permute-start | bytes 589832 | tf_op jit(solution)/shard_map/ppermute | solution.py:50
  114.0 1.0 collective-permute-done.8
  115.1 2.5 %collective-permute-start.9 = (bf16[256,384]{1,0:T(8,128)(2,1)S(1)}, bf16[256,384]{1,0:T(8,128)(2,1)S(1)}, u32[]{:S(2)}, u32[]{:S(2)}) collective-permute-start(bf16[256,384]{1,0:T(8,128)(2,1)S(1)} %fusion.18), channel_id=1, source_target_pairs={{0,512},{16,528},{32,544},{48,560},{64,576},{80,592},{96,608},{112... | collective-permute-start | bytes 589832 | tf_op jit(solution)/shard_map/ppermute | solution.py:50
  117.6 1.6 %collective-permute-done.19 = bf16[256,384]{1,0:T(8,128)(2,1)S(1)} collective-permute-done((bf16[256,384]{1,0:T(8,128)(2,1)S(1)}, bf16[256,384]{1,0:T(8,128)(2,1)S(1)}, u32[]{:S(2)}, u32[]{:S(2)}) %collective-permute-start.19) | collective-permute-done | bytes 196640 | tf_op jit(solution)/shard_map/ppermute | solution.py:50
  121.5 2.6 %collective-permute-done.9 = bf16[256,384]{1,0:T(8,128)(2,1)S(1)} collective-permute-done((bf16[256,384]{1,0:T(8,128)(2,1)S(1)}, bf16[256,384]{1,0:T(8,128)(2,1)S(1)}, u32[]{:S(2)}, u32[]{:S(2)}) %collective-permute-start.9) | collective-permute-done | bytes 196640 | tf_op jit(solution)/shard_map/ppermute | solution.py:50
  124.9 1.1 select_convert_fusion
  (73 shorter events, 10.2 us)
Async XLA Ops:
  0.6 16.6 %copy-start = (bf16[256,384]{1,0:T(8,128)(2,1)S(1)}, bf16[256,384]{1,0:T(8,128)(2,1)}, u32[]{:S(2)}) copy-start(bf16[256,384]{1,0:T(8,128)(2,1)} %param.10) | copy-start | bytes 589828
  0.6 16.6 %collective-permute-start.10 = (bf16[256,384]{1,0:T(8,128)(2,1)}, bf16[256,384]{1,0:T(8,128)(2,1)S(1)}, u32[]{:S(2)}, u32[]{:S(2)}) collective-permute-start(bf16[256,384]{1,0:T(8,128)(2,1)} %param.10), channel_id=1, source_target_pairs={{0,512},{16,528},{32,544},{48,560},{64,576},{80,592},{96,608},{112... | collective-permute-start | bytes 589832 | tf_op jit(solution)/shard_map/ppermute | solution.py:50
  9.4 9.8 %collective-permute-start = (bf16[256,384]{1,0:T(8,128)(2,1)S(1)}, bf16[256,384]{1,0:T(8,128)(2,1)S(1)}, u32[]{:S(2)}, u32[]{:S(2)}) collective-permute-start(bf16[256,384]{1,0:T(8,128)(2,1)S(1)} %copy.35), channel_id=1, source_target_pairs={{0,512},{16,528},{32,544},{48,560},{64,576},{80,592},{96,608},{112... | collective-permute-start | bytes 589832 | tf_op jit(solution)/shard_map/ppermute | solution.py:50
  20.6 34.1 %slice-start = ((s8[4718592]{0:T(1024)(128)(4,1)}), s8[4194304]{0:T(1024)(128)(4,1)S(1)}, s32[]{:S(2)}) async-start(s8[4718592]{0:T(1024)(128)(4,1)} %bitcast.41), calls=%async_computation | async-start | bytes 8388608
  20.8 34.0 %slice-start.1 = ((s8[4718592]{0:T(1024)(128)(4,1)}), s8[524288]{0:T(1024)(128)(4,1)S(1)}, s32[]{:S(2)}) async-start(s8[4718592]{0:T(1024)(128)(4,1)} %bitcast.41), calls=%async_computation.1 | async-start | bytes 1048576
  25.3 20.7 %collective-permute-start.1 = (bf16[128,384]{1,0:T(8,128)(2,1)S(1)}, bf16[128,384]{1,0:T(8,128)(2,1)S(1)}, u32[]{:S(2)}, u32[]{:S(2)}) collective-permute-start(bf16[128,384]{1,0:T(8,128)(2,1)S(1)} %get-tuple-element.6), channel_id=1, source_target_pairs={{0,1},{1,2},{2,3},{3,4},{4,5},{5,6},{6,7},{7,8},{8,9},{9,10},{10,1... | collective-permute-start | bytes 294920 | tf_op jit(solution)/shard_map/ppermute | solution.py:47
  43.5 7.8 %collective-permute-start.11 = (bf16[256,384]{1,0:T(8,128)(2,1)S(1)}, bf16[256,384]{1,0:T(8,128)(2,1)S(1)}, u32[]{:S(2)}, u32[]{:S(2)}) collective-permute-start(bf16[256,384]{1,0:T(8,128)(2,1)S(1)} %pad_maximum_fusion.1), channel_id=1, source_target_pairs={{0,1},{1,2},{2,3},{3,4},{4,5},{5,6},{6,7},{7,8},{8,9},{9,10},{10,1... | collective-permute-start | bytes 589832 | tf_op jit(solution)/shard_map/ppermute | solution.py:47
  46.1 9.0 %collective-permute-start.2 = (bf16[256,384]{1,0:T(8,128)(2,1)S(1)}, bf16[256,384]{1,0:T(8,128)(2,1)S(1)}, u32[]{:S(2)}, u32[]{:S(2)}) collective-permute-start(bf16[256,384]{1,0:T(8,128)(2,1)S(1)} %add_convert_fusion.8), channel_id=1, source_target_pairs={{0,1},{1,2},{2,3},{3,4},{4,5},{5,6},{6,7},{7,8},{8,9},{9,10},{10,1... | collective-permute-start | bytes 589832 | tf_op jit(solution)/shard_map/ppermute | solution.py:47
  51.3 8.8 %collective-permute-start.12 = (bf16[256,384]{1,0:T(8,128)(2,1)S(1)}, bf16[256,384]{1,0:T(8,128)(2,1)S(1)}, u32[]{:S(2)}, u32[]{:S(2)}) collective-permute-start(bf16[256,384]{1,0:T(8,128)(2,1)S(1)} %collective-permute-done.11), channel_id=1, source_target_pairs={{0,1},{1,2},{2,3},{3,4},{4,5},{5,6},{6,7},{7,8},{8,9},{9,10},{10,1... | collective-permute-start | bytes 589832 | tf_op jit(solution)/shard_map/ppermute | solution.py:47
  55.2 8.7 %collective-permute-start.3 = (bf16[256,384]{1,0:T(8,128)(2,1)S(1)}, bf16[256,384]{1,0:T(8,128)(2,1)S(1)}, u32[]{:S(2)}, u32[]{:S(2)}) collective-permute-start(bf16[256,384]{1,0:T(8,128)(2,1)S(1)} %add_convert_fusion.7), channel_id=1, source_target_pairs={{0,1},{1,2},{2,3},{3,4},{4,5},{5,6},{6,7},{7,8},{8,9},{9,10},{10,1... | collective-permute-start | bytes 589832 | tf_op jit(solution)/shard_map/ppermute | solution.py:47
  60.2 8.8 %collective-permute-start.13 = (bf16[256,384]{1,0:T(8,128)(2,1)S(1)}, bf16[256,384]{1,0:T(8,128)(2,1)S(1)}, u32[]{:S(2)}, u32[]{:S(2)}) collective-permute-start(bf16[256,384]{1,0:T(8,128)(2,1)S(1)} %collective-permute-done.12), channel_id=1, source_target_pairs={{0,1},{1,2},{2,3},{3,4},{4,5},{5,6},{6,7},{7,8},{8,9},{9,10},{10,1... | collective-permute-start | bytes 589832 | tf_op jit(solution)/shard_map/ppermute | solution.py:47
  63.9 8.7 %collective-permute-start.4 = (bf16[256,384]{1,0:T(8,128)(2,1)S(1)}, bf16[256,384]{1,0:T(8,128)(2,1)S(1)}, u32[]{:S(2)}, u32[]{:S(2)}) collective-permute-start(bf16[256,384]{1,0:T(8,128)(2,1)S(1)} %add_convert_fusion.6), channel_id=1, source_target_pairs={{0,1},{1,2},{2,3},{3,4},{4,5},{5,6},{6,7},{7,8},{8,9},{9,10},{10,1... | collective-permute-start | bytes 589832 | tf_op jit(solution)/shard_map/ppermute | solution.py:47
  69.0 8.8 %collective-permute-start.14 = (bf16[256,384]{1,0:T(8,128)(2,1)S(1)}, bf16[256,384]{1,0:T(8,128)(2,1)S(1)}, u32[]{:S(2)}, u32[]{:S(2)}) collective-permute-start(bf16[256,384]{1,0:T(8,128)(2,1)S(1)} %collective-permute-done.13), channel_id=1, source_target_pairs={{0,1},{1,2},{2,3},{3,4},{4,5},{5,6},{6,7},{7,8},{8,9},{9,10},{10,1... | collective-permute-start | bytes 589832 | tf_op jit(solution)/shard_map/ppermute | solution.py:47
  72.7 8.7 %collective-permute-start.5 = (bf16[256,384]{1,0:T(8,128)(2,1)S(1)}, bf16[256,384]{1,0:T(8,128)(2,1)S(1)}, u32[]{:S(2)}, u32[]{:S(2)}) collective-permute-start(bf16[256,384]{1,0:T(8,128)(2,1)S(1)} %add_convert_fusion.5), channel_id=1, source_target_pairs={{0,1},{1,2},{2,3},{3,4},{4,5},{5,6},{6,7},{7,8},{8,9},{9,10},{10,1... | collective-permute-start | bytes 589832 | tf_op jit(solution)/shard_map/ppermute | solution.py:47
  77.8 8.8 %collective-permute-start.15 = (bf16[256,384]{1,0:T(8,128)(2,1)S(1)}, bf16[256,384]{1,0:T(8,128)(2,1)S(1)}, u32[]{:S(2)}, u32[]{:S(2)}) collective-permute-start(bf16[256,384]{1,0:T(8,128)(2,1)S(1)} %collective-permute-done.14), channel_id=1, source_target_pairs={{0,1},{1,2},{2,3},{3,4},{4,5},{5,6},{6,7},{7,8},{8,9},{9,10},{10,1... | collective-permute-start | bytes 589832 | tf_op jit(solution)/shard_map/ppermute | solution.py:47
  81.4 8.7 %collective-permute-start.6 = (bf16[256,384]{1,0:T(8,128)(2,1)S(1)}, bf16[256,384]{1,0:T(8,128)(2,1)S(1)}, u32[]{:S(2)}, u32[]{:S(2)}) collective-permute-start(bf16[256,384]{1,0:T(8,128)(2,1)S(1)} %add_convert_fusion.4), channel_id=1, source_target_pairs={{0,1},{1,2},{2,3},{3,4},{4,5},{5,6},{6,7},{7,8},{8,9},{9,10},{10,1... | collective-permute-start | bytes 589832 | tf_op jit(solution)/shard_map/ppermute | solution.py:47
  86.7 8.8 %collective-permute-start.16 = (bf16[256,384]{1,0:T(8,128)(2,1)S(1)}, bf16[256,384]{1,0:T(8,128)(2,1)S(1)}, u32[]{:S(2)}, u32[]{:S(2)}) collective-permute-start(bf16[256,384]{1,0:T(8,128)(2,1)S(1)} %collective-permute-done.15), channel_id=1, source_target_pairs={{0,1},{1,2},{2,3},{3,4},{4,5},{5,6},{6,7},{7,8},{8,9},{9,10},{10,1... | collective-permute-start | bytes 589832 | tf_op jit(solution)/shard_map/ppermute | solution.py:47
  90.2 17.2 %collective-permute-start.7 = (bf16[256,384]{1,0:T(8,128)(2,1)S(1)}, bf16[256,384]{1,0:T(8,128)(2,1)S(1)}, u32[]{:S(2)}, u32[]{:S(2)}) collective-permute-start(bf16[256,384]{1,0:T(8,128)(2,1)S(1)} %add_convert_fusion.3), channel_id=1, source_target_pairs={{0,1},{1,2},{2,3},{3,4},{4,5},{5,6},{6,7},{7,8},{8,9},{9,10},{10,1... | collective-permute-start | bytes 589832 | tf_op jit(solution)/shard_map/ppermute | solution.py:47
  95.5 7.6 %collective-permute-start.17 = (bf16[256,384]{1,0:T(8,128)(2,1)S(1)}, bf16[256,384]{1,0:T(8,128)(2,1)S(1)}, u32[]{:S(2)}, u32[]{:S(2)}) collective-permute-start(bf16[256,384]{1,0:T(8,128)(2,1)S(1)} %collective-permute-done.16), channel_id=1, source_target_pairs={{0,1},{1,2},{2,3},{3,4},{4,5},{5,6},{6,7},{7,8},{8,9},{9,10},{10,1... | collective-permute-start | bytes 589832 | tf_op jit(solution)/shard_map/ppermute | solution.py:47
  103.1 6.5 %collective-permute-start.18 = (bf16[128,384]{1,0:T(8,128)(2,1)S(1)}, bf16[128,384]{1,0:T(8,128)(2,1)S(1)}, u32[]{:S(2)}, u32[]{:S(2)}) collective-permute-start(bf16[128,384]{1,0:T(8,128)(2,1)S(1)} %slice_select_fusion.1), channel_id=1, source_target_pairs={{0,1},{1,2},{2,3},{3,4},{4,5},{5,6},{6,7},{7,8},{8,9},{9,10},{10,1... | collective-permute-start | bytes 294920 | tf_op jit(solution)/shard_map/ppermute | solution.py:47
  107.4 7.6 %collective-permute-start.8 = (bf16[256,384]{1,0:T(8,128)(2,1)S(1)}, bf16[256,384]{1,0:T(8,128)(2,1)S(1)}, u32[]{:S(2)}, u32[]{:S(2)}) collective-permute-start(bf16[256,384]{1,0:T(8,128)(2,1)S(1)} %add_convert_fusion.2), channel_id=1, source_target_pairs={{0,1},{1,2},{2,3},{3,4},{4,5},{5,6},{6,7},{7,8},{8,9},{9,10},{10,1... | collective-permute-start | bytes 589832 | tf_op jit(solution)/shard_map/ppermute | solution.py:47
  110.2 9.1 %collective-permute-start.19 = (bf16[256,384]{1,0:T(8,128)(2,1)S(1)}, bf16[256,384]{1,0:T(8,128)(2,1)S(1)}, u32[]{:S(2)}, u32[]{:S(2)}) collective-permute-start(bf16[256,384]{1,0:T(8,128)(2,1)S(1)} %get-tuple-element.19), channel_id=1, source_target_pairs={{0,512},{16,528},{32,544},{48,560},{64,576},{80,592},{96,608},{112... | collective-permute-start | bytes 589832 | tf_op jit(solution)/shard_map/ppermute | solution.py:50
  115.1 9.1 %collective-permute-start.9 = (bf16[256,384]{1,0:T(8,128)(2,1)S(1)}, bf16[256,384]{1,0:T(8,128)(2,1)S(1)}, u32[]{:S(2)}, u32[]{:S(2)}) collective-permute-start(bf16[256,384]{1,0:T(8,128)(2,1)S(1)} %fusion.18), channel_id=1, source_target_pairs={{0,512},{16,528},{32,544},{48,560},{64,576},{80,592},{96,608},{112... | collective-permute-start | bytes 589832 | tf_op jit(solution)/shard_map/ppermute | solution.py:50

commit v2 on v1

--- a/solution.py
+++ b/solution.py
@@ -9,10 +9,10 @@
 SLOT = 128
 
 
-def ring_pairs(dp_size, mp_size):
+def ring_pairs(dp_size, mp_size, distance):
     pairs = []
     for dp in range(dp_size):
-        step = 1 if goes_right(dp, dp_size) else mp_size - 1
+        step = distance if goes_right(dp, dp_size) else mp_size - distance
         for z in range(mp_size):
             pairs.append((dp * mp_size + z, dp * mp_size + (z + step) % mp_size))
     return pairs
@@ -28,9 +28,11 @@
 
 def shards(query_rows, key_rows, value_rows, proj_weight, out_grad, image_starts):
     dp_size, mp_size = lax.axis_size("dp"), lax.axis_size("mp")
-    half_ring = mp_size // 2
+    near = mp_size // 4
+    far = near + 1
     dp, z = lax.axis_index("dp"), lax.axis_index("mp")
-    ring_perm = ring_pairs(dp_size, mp_size)
+    hop_perm = ring_pairs(dp_size, mp_size, 1)
+    jump_perm = ring_pairs(dp_size, mp_size, far)
     swap_perm = [(i, (i + dp_size // 2) % dp_size) for i in range(dp_size)]
     right = goes_right(dp, dp_size)
     delta = jnp.where(right, 1, mp_size - 1)
@@ -43,8 +45,11 @@
     from_light = (jnp.arange(SLOT) < light_count)[:, None]
     flip = (jnp.arange(SLOT)[:, None] + jnp.arange(SLOT)[None, :] == SLOT - 1).astype(jnp.bfloat16)
 
-    def ring(rows):
-        return lax.ppermute(rows, ("dp", "mp"), ring_perm)
+    def hop(rows):
+        return lax.ppermute(rows, ("dp", "mp"), hop_perm)
+
+    def jump(rows):
+        return lax.ppermute(rows, ("dp", "mp"), jump_perm)
 
     def swap(rows):
         return lax.ppermute(rows, "dp", swap_perm)
@@ -104,26 +109,40 @@
     )
     terms = dot(pair_attended, proj_weight).astype(jnp.bfloat16)
 
-    def term(index):
+    def term(distance):
+        index = z + distance * delta
         return lax.dynamic_slice_in_dim(terms, (index % mp_size) * width, width, 1)
 
-    block = pair_grad
-    total = half_of(term(z + half_ring * delta))
-    for step in range(1, half_ring + 1):
-        block = ring(half_of(block) if step == half_ring else block)
-        received = ring(total)
-        product = dot(block, weight_block(z + step * (mp_size - delta)), (((1,), (1,)), ((), ())))
-        if step == half_ring:
-            product = place_half(product)
-        partial = partial + product
-        if step == 1:
-            received = place_half(received)
-        own = term(z + (half_ring - step) * delta)
-        if step == half_ring:
-            own = place_half(half_of(own))
-        total = received.astype(jnp.float32) + own.astype(jnp.float32)
-        if step < half_ring:
-            total = total.astype(jnp.bfloat16)
+    def product(block, distance):
+        return dot(
+            block, weight_block(z + distance * (mp_size - delta)), (((1,), (1,)), ((), ()))
+        )
+
+    def plus(received, distance):
+        total = received.astype(jnp.float32) + term(distance).astype(jnp.float32)
+        return total.astype(jnp.bfloat16)
+
+    rows = 2 * SLOT
+    near_block, far_block = hop(pair_grad), jump(pair_grad)
+    sums = hop(jnp.concatenate([term(near), half_of(term(near + far - 1))], 0))
+    sums = [sums[:rows], place_half(sums[rows:])]
+    for step in range(1, near):
+        last = step == near - 1
+        partial = partial + product(near_block, step) + product(far_block, far + step - 1)
+        moved = hop(jnp.concatenate([near_block, half_of(far_block) if last else far_block], 0))
+        near_block, far_block = moved[:rows], moved[rows:]
+        sums = [plus(sums[0], near - step), plus(sums[1], near + far - 1 - step)]
+        if last:
+            sums = [hop(sums[0]), jump(sums[1])]
+        else:
+            sums = hop(jnp.concatenate(sums, 0))
+            sums = [sums[:rows], sums[rows:]]
+    partial = partial + product(near_block, near) + place_half(product(far_block, near + far - 1))
+    total = (
+        sums[0].astype(jnp.float32)
+        + sums[1].astype(jnp.float32)
+        + place_half(half_of(term(0)).astype(jnp.float32))
+    )
 
     grad_pair = (partial + swap(partial.astype(jnp.bfloat16)).astype(jnp.float32)).astype(jnp.bfloat16)
     grad_attended = unpack(grad_pair)

time: 127 us -> 122 us (0.961)
  the two profiles are of different devices: /device:TPU:14 before, /device:TPU:8 now
where the time goes in v2:
time: 122 us; the launch traced here: 121 us
  starting transfers between devices  53.4 us (44%)
  waiting for transfers between devices  45.5 us (37%)
  matrix products  10.5 us (9%)
  local copies, waits for them, and re-layouts  6.23 us (5%)
  other arithmetic  3.48 us (3%)
  between operations  2.23 us (2%)
    ppermute x8, waiting for transfers between devices, hop(): return lax.ppermute(rows, ('dp', 'mp'), hop_perm)  23.4 us
    ppermute x8, starting transfers between devices, hop(): return lax.ppermute(rows, ('dp', 'mp'), hop_perm)  20.1 us
    ppermute x2, starting transfers between devices, jump(): return lax.ppermute(rows, ('dp', 'mp'), jump_perm)  17.8 us
    ppermute x4, starting transfers between devices, swap(): return lax.ppermute(rows, 'dp', swap_perm)  15.5 us
    ppermute x2, waiting for transfers between devices, jump(): return lax.ppermute(rows, ('dp', 'mp'), jump_perm)  15.2 us
    dot_general x14, matrix products, dot(): return lax.dot_general(a, b, dims, preferred_element_type=jnp.float32)  7.61 us
    ppermute x4, waiting for transfers between devices, swap(): return lax.ppermute(rows, 'dp', swap_perm)  6.85 us
    unnamed x9, local copies, waits for them, and re-layouts  3.21 us
  transfers between devices with their start and end apart: 14, of which 10 were waited for; matrix products, arithmetic and copies ran while one was open for 14% of the time, Pallas kernels for 0%

profile of v2, /device:TPU:8, one launch (start us, length us, event | category | flops | bytes accessed | tf_op | source)
XLA Modules:
  0.0 121.2 jit_solution(11110829508644180073)
XLA Ops:
  0.6 5.1 %collective-permute-start.7 = (bf16[256,384]{1,0:T(8,128)(2,1)}, bf16[256,384]{1,0:T(8,128)(2,1)S(1)}, u32[]{:S(2)}, u32[]{:S(2)}) collective-permute-start(bf16[256,384]{1,0:T(8,128)(2,1)} %param.10), channel_id=1, source_target_pairs={{0,512},{16,528},{32,544},{48,560},{64,576},{80,592},{96,608},{112... | collective-permute-start | bytes 589832 | tf_op jit(solution)/shard_map/ppermute | solution.py:55
  5.7 0.7 constant_dynamic-slice_fusion.1
  6.6 1.1 copy.28
  7.6 1.1 copy.29
  8.7 1.1 copy.32
  11.0 2.4 %collective-permute-start = (bf16[256,384]{1,0:T(8,128)(2,1)S(1)}, bf16[256,384]{1,0:T(8,128)(2,1)S(1)}, u32[]{:S(2)}, u32[]{:S(2)}) collective-permute-start(bf16[256,384]{1,0:T(8,128)(2,1)S(1)} %copy.35), channel_id=1, source_target_pairs={{0,512},{16,528},{32,544},{48,560},{64,576},{80,592},{96,608},{112... | collective-permute-start | bytes 589832 | tf_op jit(solution)/shard_map/ppermute | solution.py:55
  13.7 1.3 %dynamic-slice = s32[1,1]{1,0:T(1,128)} dynamic-slice(s32[64,256]{1,0:T(8,128)} %param.11, s32[]{:T(128)S(6)} %select_n.265, s32[]{:T(128)S(6)} %add.335), dynamic_slice_sizes={1,1} | dynamic-slice | bytes 12 | tf_op jit(solution)/shard_map/slice | solution.py:43
  17.5 12.7 %collective-permute-start.9 = (bf16[256,384]{1,0:T(8,128)(2,1)S(1)}, bf16[256,384]{1,0:T(8,128)(2,1)S(1)}, u32[]{:S(2)}, u32[]{:S(2)}) collective-permute-start(bf16[256,384]{1,0:T(8,128)(2,1)S(1)} %pad_maximum_fusion.5), channel_id=1, source_target_pairs={{0,5},{1,6},{2,7},{3,8},{4,9},{5,10},{6,11},{7,12},{8,13},{9,14},{... | collective-permute-start | bytes 589832 | tf_op jit(solution)/shard_map/ppermute | solution.py:52
  30.2 4.3 %collective-permute-start.8 = (bf16[256,384]{1,0:T(8,128)(2,1)S(1)}, bf16[256,384]{1,0:T(8,128)(2,1)S(1)}, u32[]{:S(2)}, u32[]{:S(2)}) collective-permute-start(bf16[256,384]{1,0:T(8,128)(2,1)S(1)} %pad_maximum_fusion.5), channel_id=1, source_target_pairs={{0,1},{1,2},{2,3},{3,4},{4,5},{5,6},{6,7},{7,8},{8,9},{9,10},{10,1... | collective-permute-start | bytes 589832 | tf_op jit(solution)/shard_map/ppermute | solution.py:49
  34.8 4.3 %convolution_convert_fusion = bf16[256,6144]{1,0:T(8,128)(2,1)S(1)} fusion(bf16[384,6144]{1,0:T(8,128)(2,1)} %param.9, bf16[128,384]{1,0:T(8,128)(2,1)S(1)} %fusion.53, bf16[128,384]{1,0:T(8,128)(2,1)S(1)} %slice.134), kind=kOutput, calls=%fused_computation.2 | convolution fusion | flops 1209925632 | bytes 8060928 | tf_op jit(solution)/shard_map/dot_general | solution.py:26
  39.2 4.3 %collective-permute-start.1 = (bf16[384,384]{1,0:T(8,128)(2,1)S(1)}, bf16[384,384]{1,0:T(8,128)(2,1)S(1)}, u32[]{:S(2)}, u32[]{:S(2)}) collective-permute-start(bf16[384,384]{1,0:T(8,128)(2,1)S(1)} %pad_maximum_fusion.3), channel_id=1, source_target_pairs={{0,1},{1,2},{2,3},{3,4},{4,5},{5,6},{6,7},{7,8},{8,9},{9,10},{10,1... | collective-permute-start | bytes 884744 | tf_op jit(solution)/shard_map/ppermute | solution.py:49
  43.9 6.0 %collective-permute-done.8 = bf16[256,384]{1,0:T(8,128)(2,1)S(1)} collective-permute-done((bf16[256,384]{1,0:T(8,128)(2,1)S(1)}, bf16[256,384]{1,0:T(8,128)(2,1)S(1)}, u32[]{:S(2)}, u32[]{:S(2)}) %collective-permute-start.8) | collective-permute-done | bytes 196640 | tf_op jit(solution)/shard_map/ppermute | solution.py:49
  49.9 1.9 %collective-permute-start.10 = (bf16[512,384]{1,0:T(8,128)(2,1)S(1)}, bf16[512,384]{1,0:T(8,128)(2,1)S(1)}, u32[]{:S(2)}, u32[]{:S(2)}) collective-permute-start(bf16[512,384]{1,0:T(8,128)(2,1)S(1)} %pad_maximum_fusion.2), channel_id=1, source_target_pairs={{0,1},{1,2},{2,3},{3,4},{4,5},{5,6},{6,7},{7,8},{8,9},{9,10},{10,1... | collective-permute-start | bytes 1179656 | tf_op jit(solution)/shard_map/ppermute | solution.py:49
  52.1 0.9 collective-permute-done.1
  53.2 1.9 %collective-permute-start.2 = (bf16[512,384]{1,0:T(8,128)(2,1)S(1)}, bf16[512,384]{1,0:T(8,128)(2,1)S(1)}, u32[]{:S(2)}, u32[]{:S(2)}) collective-permute-start(bf16[512,384]{1,0:T(8,128)(2,1)S(1)} %pad_maximum_fusion), channel_id=1, source_target_pairs={{0,1},{1,2},{2,3},{3,4},{4,5},{5,6},{6,7},{7,8},{8,9},{9,10},{10,1... | collective-permute-start | bytes 1179656 | tf_op jit(solution)/shard_map/ppermute | solution.py:49
  55.2 6.8 %collective-permute-done.10 = bf16[512,384]{1,0:T(8,128)(2,1)S(1)} collective-permute-done((bf16[512,384]{1,0:T(8,128)(2,1)S(1)}, bf16[512,384]{1,0:T(8,128)(2,1)S(1)}, u32[]{:S(2)}, u32[]{:S(2)}) %collective-permute-start.10) | collective-permute-done | bytes 393248 | tf_op jit(solution)/shard_map/ppermute | solution.py:49
  61.9 1.9 %collective-permute-start.11 = (bf16[512,384]{1,0:T(8,128)(2,1)S(1)}, bf16[512,384]{1,0:T(8,128)(2,1)S(1)}, u32[]{:S(2)}, u32[]{:S(2)}) collective-permute-start(bf16[512,384]{1,0:T(8,128)(2,1)S(1)} %collective-permute-done.10), channel_id=1, source_target_pairs={{0,1},{1,2},{2,3},{3,4},{4,5},{5,6},{6,7},{7,8},{8,9},{9,10},{10,1... | collective-permute-start | bytes 1179656 | tf_op jit(solution)/shard_map/ppermute | solution.py:49
  64.5 1.7 %collective-permute-done.2 = bf16[512,384]{1,0:T(8,128)(2,1)S(1)} collective-permute-done((bf16[512,384]{1,0:T(8,128)(2,1)S(1)}, bf16[512,384]{1,0:T(8,128)(2,1)S(1)}, u32[]{:S(2)}, u32[]{:S(2)}) %collective-permute-start.2) | collective-permute-done | bytes 393248 | tf_op jit(solution)/shard_map/ppermute | solution.py:49
  66.3 1.9 %collective-permute-start.3 = (bf16[512,384]{1,0:T(8,128)(2,1)S(1)}, bf16[512,384]{1,0:T(8,128)(2,1)S(1)}, u32[]{:S(2)}, u32[]{:S(2)}) collective-permute-start(bf16[512,384]{1,0:T(8,128)(2,1)S(1)} %pad_maximum_fusion.1), channel_id=1, source_target_pairs={{0,1},{1,2},{2,3},{3,4},{4,5},{5,6},{6,7},{7,8},{8,9},{9,10},{10,1... | collective-permute-start | bytes 1179656 | tf_op jit(solution)/shard_map/ppermute | solution.py:49
  68.6 4.2 %collective-permute-done.11 = bf16[512,384]{1,0:T(8,128)(2,1)S(1)} collective-permute-done((bf16[512,384]{1,0:T(8,128)(2,1)S(1)}, bf16[512,384]{1,0:T(8,128)(2,1)S(1)}, u32[]{:S(2)}, u32[]{:S(2)}) %collective-permute-start.11) | collective-permute-done | bytes 393248 | tf_op jit(solution)/shard_map/ppermute | solution.py:49
  72.9 1.9 %collective-permute-start.12 = (bf16[384,384]{1,0:T(8,128)(2,1)S(1)}, bf16[384,384]{1,0:T(8,128)(2,1)S(1)}, u32[]{:S(2)}, u32[]{:S(2)}) collective-permute-start(bf16[384,384]{1,0:T(8,128)(2,1)S(1)} %pad_maximum_fusion.4), channel_id=1, source_target_pairs={{0,1},{1,2},{2,3},{3,4},{4,5},{5,6},{6,7},{7,8},{8,9},{9,10},{10,1... | collective-permute-start | bytes 884744 | tf_op jit(solution)/shard_map/ppermute | solution.py:49
  74.8 2.4 %collective-permute-done.3 = bf16[512,384]{1,0:T(8,128)(2,1)S(1)} collective-permute-done((bf16[512,384]{1,0:T(8,128)(2,1)S(1)}, bf16[512,384]{1,0:T(8,128)(2,1)S(1)}, u32[]{:S(2)}, u32[]{:S(2)}) %collective-permute-start.3) | collective-permute-done | bytes 393248 | tf_op jit(solution)/shard_map/ppermute | solution.py:49
  77.3 1.9 %collective-permute-start.4 = (bf16[256,384]{1,0:T(8,128)(2,1)S(1)}, bf16[256,384]{1,0:T(8,128)(2,1)S(1)}, u32[]{:S(2)}, u32[]{:S(2)}) collective-permute-start(bf16[256,384]{1,0:T(8,128)(2,1)S(1)} %get-tuple-element.4), channel_id=1, source_target_pairs={{0,1},{1,2},{2,3},{3,4},{4,5},{5,6},{6,7},{7,8},{8,9},{9,10},{10,1... | collective-permute-start | bytes 589832 | tf_op jit(solution)/shard_map/ppermute | solution.py:49
  79.3 5.1 %collective-permute-start.5 = (bf16[256,384]{1,0:T(8,128)(2,1)S(1)}, bf16[256,384]{1,0:T(8,128)(2,1)S(1)}, u32[]{:S(2)}, u32[]{:S(2)}) collective-permute-start(bf16[256,384]{1,0:T(8,128)(2,1)S(1)} %get-tuple-element.5), channel_id=1, source_target_pairs={{0,5},{1,6},{2,7},{3,8},{4,9},{5,10},{6,11},{7,12},{8,13},{9,14},{... | collective-permute-start | bytes 589832 | tf_op jit(solution)/shard_map/ppermute | solution.py:52
  84.6 1.5 %collective-permute-done.4 = bf16[256,384]{1,0:T(8,128)(2,1)S(1)} collective-permute-done((bf16[256,384]{1,0:T(8,128)(2,1)S(1)}, bf16[256,384]{1,0:T(8,128)(2,1)S(1)}, u32[]{:S(2)}, u32[]{:S(2)}) %collective-permute-start.4) | collective-permute-done | bytes 196640 | tf_op jit(solution)/shard_map/ppermute | solution.py:49
  86.1 15.2 %collective-permute-done.5 = bf16[256,384]{1,0:T(8,128)(2,1)S(1)} collective-permute-done((bf16[256,384]{1,0:T(8,128)(2,1)S(1)}, bf16[256,384]{1,0:T(8,128)(2,1)S(1)}, u32[]{:S(2)}, u32[]{:S(2)}) %collective-permute-start.5) | collective-permute-done | bytes 196640 | tf_op jit(solution)/shard_map/ppermute | solution.py:52
  101.3 6.1 %collective-permute-start.6 = (bf16[256,384]{1,0:T(8,128)(2,1)S(1)}, bf16[256,384]{1,0:T(8,128)(2,1)S(1)}, u32[]{:S(2)}, u32[]{:S(2)}) collective-permute-start(bf16[256,384]{1,0:T(8,128)(2,1)S(1)} %fusion.58), channel_id=1, source_target_pairs={{0,512},{16,528},{32,544},{48,560},{64,576},{80,592},{96,608},{112... | collective-permute-start | bytes 589832 | tf_op jit(solution)/shard_map/ppermute | solution.py:55
  108.3 1.9 %collective-permute-start.13 = (bf16[256,384]{1,0:T(8,128)(2,1)S(1)}, bf16[256,384]{1,0:T(8,128)(2,1)S(1)}, u32[]{:S(2)}, u32[]{:S(2)}) collective-permute-start(bf16[256,384]{1,0:T(8,128)(2,1)S(1)} %get-tuple-element.24), channel_id=1, source_target_pairs={{0,512},{16,528},{32,544},{48,560},{64,576},{80,592},{96,608},{112... | collective-permute-start | bytes 589832 | tf_op jit(solution)/shard_map/ppermute | solution.py:55
  110.3 0.8 collective-permute-done.6
  111.4 6.0 %collective-permute-done.13 = bf16[256,384]{1,0:T(8,128)(2,1)S(1)} collective-permute-done((bf16[256,384]{1,0:T(8,128)(2,1)S(1)}, bf16[256,384]{1,0:T(8,128)(2,1)S(1)}, u32[]{:S(2)}, u32[]{:S(2)}) %collective-permute-start.13) | collective-permute-done | bytes 196640 | tf_op jit(solution)/shard_map/ppermute | solution.py:55
  118.1 0.7 fusion.46
  120.2 1.1 select_convert_fusion
  (65 shorter events, 9.0 us)
Async XLA Ops:
  0.6 16.6 %copy-start = (bf16[256,384]{1,0:T(8,128)(2,1)S(1)}, bf16[256,384]{1,0:T(8,128)(2,1)}, u32[]{:S(2)}) copy-start(bf16[256,384]{1,0:T(8,128)(2,1)} %param.10) | copy-start | bytes 589828
  0.6 16.6 %collective-permute-start.7 = (bf16[256,384]{1,0:T(8,128)(2,1)}, bf16[256,384]{1,0:T(8,128)(2,1)S(1)}, u32[]{:S(2)}, u32[]{:S(2)}) collective-permute-start(bf16[256,384]{1,0:T(8,128)(2,1)} %param.10), channel_id=1, source_target_pairs={{0,512},{16,528},{32,544},{48,560},{64,576},{80,592},{96,608},{112... | collective-permute-start | bytes 589832 | tf_op jit(solution)/shard_map/ppermute | solution.py:55
  11.0 23.5 %collective-permute-start = (bf16[256,384]{1,0:T(8,128)(2,1)S(1)}, bf16[256,384]{1,0:T(8,128)(2,1)S(1)}, u32[]{:S(2)}, u32[]{:S(2)}) collective-permute-start(bf16[256,384]{1,0:T(8,128)(2,1)S(1)} %copy.35), channel_id=1, source_target_pairs={{0,512},{16,528},{32,544},{48,560},{64,576},{80,592},{96,608},{112... | collective-permute-start | bytes 589832 | tf_op jit(solution)/shard_map/ppermute | solution.py:55
  17.5 26.4 %collective-permute-start.9 = (bf16[256,384]{1,0:T(8,128)(2,1)S(1)}, bf16[256,384]{1,0:T(8,128)(2,1)S(1)}, u32[]{:S(2)}, u32[]{:S(2)}) collective-permute-start(bf16[256,384]{1,0:T(8,128)(2,1)S(1)} %pad_maximum_fusion.5), channel_id=1, source_target_pairs={{0,5},{1,6},{2,7},{3,8},{4,9},{5,10},{6,11},{7,12},{8,13},{9,14},{... | collective-permute-start | bytes 589832 | tf_op jit(solution)/shard_map/ppermute | solution.py:52
  30.2 19.6 %collective-permute-start.8 = (bf16[256,384]{1,0:T(8,128)(2,1)S(1)}, bf16[256,384]{1,0:T(8,128)(2,1)S(1)}, u32[]{:S(2)}, u32[]{:S(2)}) collective-permute-start(bf16[256,384]{1,0:T(8,128)(2,1)S(1)} %pad_maximum_fusion.5), channel_id=1, source_target_pairs={{0,1},{1,2},{2,3},{3,4},{4,5},{5,6},{6,7},{7,8},{8,9},{9,10},{10,1... | collective-permute-start | bytes 589832 | tf_op jit(solution)/shard_map/ppermute | solution.py:49
  34.6 9.0 %slice-start = ((s8[4718592]{0:T(1024)(128)(4,1)}), s8[4194304]{0:T(1024)(128)(4,1)S(1)}, s32[]{:S(2)}) async-start(s8[4718592]{0:T(1024)(128)(4,1)} %bitcast.35), calls=%async_computation | async-start | bytes 8388608
  34.8 8.8 %slice-start.1 = ((s8[4718592]{0:T(1024)(128)(4,1)}), s8[524288]{0:T(1024)(128)(4,1)S(1)}, s32[]{:S(2)}) async-start(s8[4718592]{0:T(1024)(128)(4,1)} %bitcast.35), calls=%async_computation.1 | async-start | bytes 1048576
  39.2 13.8 %collective-permute-start.1 = (bf16[384,384]{1,0:T(8,128)(2,1)S(1)}, bf16[384,384]{1,0:T(8,128)(2,1)S(1)}, u32[]{:S(2)}, u32[]{:S(2)}) collective-permute-start(bf16[384,384]{1,0:T(8,128)(2,1)S(1)} %pad_maximum_fusion.3), channel_id=1, source_target_pairs={{0,1},{1,2},{2,3},{3,4},{4,5},{5,6},{6,7},{7,8},{8,9},{9,10},{10,1... | collective-permute-start | bytes 884744 | tf_op jit(solution)/shard_map/ppermute | solution.py:49
  49.9 12.0 %collective-permute-start.10 = (bf16[512,384]{1,0:T(8,128)(2,1)S(1)}, bf16[512,384]{1,0:T(8,128)(2,1)S(1)}, u32[]{:S(2)}, u32[]{:S(2)}) collective-permute-start(bf16[512,384]{1,0:T(8,128)(2,1)S(1)} %pad_maximum_fusion.2), channel_id=1, source_target_pairs={{0,1},{1,2},{2,3},{3,4},{4,5},{5,6},{6,7},{7,8},{8,9},{9,10},{10,1... | collective-permute-start | bytes 1179656 | tf_op jit(solution)/shard_map/ppermute | solution.py:49
  53.2 12.9 %collective-permute-start.2 = (bf16[512,384]{1,0:T(8,128)(2,1)S(1)}, bf16[512,384]{1,0:T(8,128)(2,1)S(1)}, u32[]{:S(2)}, u32[]{:S(2)}) collective-permute-start(bf16[512,384]{1,0:T(8,128)(2,1)S(1)} %pad_maximum_fusion), channel_id=1, source_target_pairs={{0,1},{1,2},{2,3},{3,4},{4,5},{5,6},{6,7},{7,8},{8,9},{9,10},{10,1... | collective-permute-start | bytes 1179656 | tf_op jit(solution)/shard_map/ppermute | solution.py:49
  61.9 10.9 %collective-permute-start.11 = (bf16[512,384]{1,0:T(8,128)(2,1)S(1)}, bf16[512,384]{1,0:T(8,128)(2,1)S(1)}, u32[]{:S(2)}, u32[]{:S(2)}) collective-permute-start(bf16[512,384]{1,0:T(8,128)(2,1)S(1)} %collective-permute-done.10), channel_id=1, source_target_pairs={{0,1},{1,2},{2,3},{3,4},{4,5},{5,6},{6,7},{7,8},{8,9},{9,10},{10,1... | collective-permute-start | bytes 1179656 | tf_op jit(solution)/shard_map/ppermute | solution.py:49
  66.3 10.9 %collective-permute-start.3 = (bf16[512,384]{1,0:T(8,128)(2,1)S(1)}, bf16[512,384]{1,0:T(8,128)(2,1)S(1)}, u32[]{:S(2)}, u32[]{:S(2)}) collective-permute-start(bf16[512,384]{1,0:T(8,128)(2,1)S(1)} %pad_maximum_fusion.1), channel_id=1, source_target_pairs={{0,1},{1,2},{2,3},{3,4},{4,5},{5,6},{6,7},{7,8},{8,9},{9,10},{10,1... | collective-permute-start | bytes 1179656 | tf_op jit(solution)/shard_map/ppermute | solution.py:49
  72.9 34.5 %collective-permute-start.12 = (bf16[384,384]{1,0:T(8,128)(2,1)S(1)}, bf16[384,384]{1,0:T(8,128)(2,1)S(1)}, u32[]{:S(2)}, u32[]{:S(2)}) collective-permute-start(bf16[384,384]{1,0:T(8,128)(2,1)S(1)} %pad_maximum_fusion.4), channel_id=1, source_target_pairs={{0,1},{1,2},{2,3},{3,4},{4,5},{5,6},{6,7},{7,8},{8,9},{9,10},{10,1... | collective-permute-start | bytes 884744 | tf_op jit(solution)/shard_map/ppermute | solution.py:49
  77.3 8.8 %collective-permute-start.4 = (bf16[256,384]{1,0:T(8,128)(2,1)S(1)}, bf16[256,384]{1,0:T(8,128)(2,1)S(1)}, u32[]{:S(2)}, u32[]{:S(2)}) collective-permute-start(bf16[256,384]{1,0:T(8,128)(2,1)S(1)} %get-tuple-element.4), channel_id=1, source_target_pairs={{0,1},{1,2},{2,3},{3,4},{4,5},{5,6},{6,7},{7,8},{8,9},{9,10},{10,1... | collective-permute-start | bytes 589832 | tf_op jit(solution)/shard_map/ppermute | solution.py:49
  79.3 22.0 %collective-permute-start.5 = (bf16[256,384]{1,0:T(8,128)(2,1)S(1)}, bf16[256,384]{1,0:T(8,128)(2,1)S(1)}, u32[]{:S(2)}, u32[]{:S(2)}) collective-permute-start(bf16[256,384]{1,0:T(8,128)(2,1)S(1)} %get-tuple-element.5), channel_id=1, source_target_pairs={{0,5},{1,6},{2,7},{3,8},{4,9},{5,10},{6,11},{7,12},{8,13},{9,14},{... | collective-permute-start | bytes 589832 | tf_op jit(solution)/shard_map/ppermute | solution.py:52
  101.3 9.7 %collective-permute-start.6 = (bf16[256,384]{1,0:T(8,128)(2,1)S(1)}, bf16[256,384]{1,0:T(8,128)(2,1)S(1)}, u32[]{:S(2)}, u32[]{:S(2)}) collective-permute-start(bf16[256,384]{1,0:T(8,128)(2,1)S(1)} %fusion.58), channel_id=1, source_target_pairs={{0,512},{16,528},{32,544},{48,560},{64,576},{80,592},{96,608},{112... | collective-permute-start | bytes 589832 | tf_op jit(solution)/shard_map/ppermute | solution.py:55
  108.3 9.1 %collective-permute-start.13 = (bf16[256,384]{1,0:T(8,128)(2,1)S(1)}, bf16[256,384]{1,0:T(8,128)(2,1)S(1)}, u32[]{:S(2)}, u32[]{:S(2)}) collective-permute-start(bf16[256,384]{1,0:T(8,128)(2,1)S(1)} %get-tuple-element.24), channel_id=1, source_target_pairs={{0,512},{16,528},{32,544},{48,560},{64,576},{80,592},{96,608},{112... | collective-permute-start | bytes 589832 | tf_op jit(solution)/shard_map/ppermute | solution.py:55

commit v3 on v2

v3 whole, which is shorter than its diff:
```python
import functools
import math

import jax
import jax.numpy as jnp
from jax import lax
from jax.experimental import pallas as pl
from jax.experimental.pallas import tpu as pltpu
from jax.sharding import PartitionSpec as P

HEAD_DIM = 128
SLOT = 128
ROWS = 256
VMEM_LIMIT = 20 * 1024 * 1024
FRONT_LIMIT = 58 * 1024 * 1024
IN_VMEM = pl.BlockSpec(memory_space=pltpu.VMEM)


def ring_pairs(dp_size, mp_size, distance):
    pairs = []
    for dp in range(dp_size):
        step = distance if goes_right(dp, dp_size) else mp_size - distance
        for z in range(mp_size):
            pairs.append((dp * mp_size + z, dp * mp_size + (z + step) % mp_size))
    return pairs


def goes_right(dp, dp_size):
    half = dp_size // 2
    if isinstance(dp, int):
        return (dp // half + dp) % 2 == 0
    return lax.rem(lax.div(dp, half) + dp, 2) == 0


def dot(a, b, dims=(1, 0)):
    return lax.dot_general(
        a, b, (((dims[0],), (dims[1],)), ((), ())), preferred_element_type=jnp.float32
    )


def call(kernel, outs, operands, specs=None, scratch=(), flops=0, name=None, limit=VMEM_LIMIT):
    moved = sum(math.prod(a.shape) * a.dtype.itemsize for a in (*operands, *outs))
    return pl.pallas_call(
        kernel,
        out_shape=outs,
        in_specs=specs or [IN_VMEM] * len(operands),
        out_specs=[IN_VMEM] * len(outs),
        scratch_shapes=list(scratch),
        compiler_params=pltpu.CompilerParams(vmem_limit_bytes=limit),
        cost_estimate=pl.CostEstimate(flops=flops, bytes_accessed=moved, transcendentals=0),
        name=name,
    )(*operands)


def starts_of(starts_ref):
    return starts_ref[0:1, :], starts_ref[1:2, :]


def as_column(row):
    size = row.shape[1]
    on_diagonal = lax.broadcasted_iota(jnp.int32, (size, size), 0) == lax.broadcasted_iota(
        jnp.int32, (size, size), 1
    )
    return jnp.sum(jnp.where(on_diagonal, row, 0), axis=1, keepdims=True)


def is_heavy(own):
    lanes = lax.broadcasted_iota(jnp.int32, own.shape, 1)
    return jnp.sum(jnp.where(lanes == SLOT - 1, own, 0)) >= 0


def flip_matrix():
    total = lax.broadcasted_iota(jnp.int32, (SLOT, SLOT), 0) + lax.broadcasted_iota(
        jnp.int32, (SLOT, SLOT), 1
    )
    return jnp.where(total == SLOT - 1, 1.0, 0.0).astype(jnp.bfloat16)


def packed_slots(own_starts, other_starts, own_ref, other_ref):
    heavy = is_heavy(own_starts)
    light_starts = jnp.where(heavy, other_starts, own_starts)
    light_count = jnp.sum((light_starts >= 0).astype(jnp.int32))
    from_light = lax.broadcasted_iota(jnp.int32, (SLOT, 1), 0) < light_count
    own_first, other_first = own_ref[:SLOT, :], other_ref[:SLOT, :]
    first = jnp.where(heavy, own_first, other_first)
    light = jnp.where(heavy, other_first, own_first)
    second = jnp.where(heavy, own_ref[SLOT:, :], other_ref[SLOT:, :])
    flipped = dot(flip_matrix(), second)
    second_slot = jnp.where(from_light, light.astype(jnp.float32), flipped).astype(jnp.bfloat16)
    return first, second_slot


def started(moves, sems):
    copies = [pltpu.make_async_copy(*move, sems.at[at]) for at, move in enumerate(moves)]
    for copy in copies:
        copy.start()
    return copies


def pack_kernel(own_hbm, other_hbm, starts_hbm, out_ref, own_ref, other_ref, starts_ref, sems):
    moves = [(starts_hbm, starts_ref), (own_hbm, own_ref), (other_hbm, other_ref)]
    for copy in started(moves, sems):
        copy.wait()
    first, second = packed_slots(*starts_of(starts_ref), own_ref, other_ref)
    out_ref[:SLOT, :] = first
    out_ref[SLOT:, :] = second


def pack_terms_kernel(
    dp_size,
    own_hbm,
    other_hbm,
    starts_hbm,
    held_hbm,
    out_ref,
    terms_ref,
    own_ref,
    other_ref,
    starts_ref,
    held_ref,
    sems,
):
    moves = [
        (starts_hbm, starts_ref),
        (own_hbm, own_ref),
        (other_hbm, other_ref),
        (held_hbm, held_ref),
    ]
    copies = started(moves, sems)
    right = goes_right(lax.axis_index("dp"), dp_size)
    for copy in copies[:3]:
        copy.wait()
    first, second = packed_slots(*starts_of(starts_ref), own_ref, other_ref)
    out_ref[:SLOT, :] = first
    out_ref[SLOT:, :] = second
    half = jnp.where(right, first, second)
    copies[3].wait()
    terms_ref[:SLOT, :] = dot(first, held_ref[0]).astype(jnp.bfloat16)
    terms_ref[SLOT:ROWS, :] = dot(second, held_ref[0]).astype(jnp.bfloat16)
    terms_ref[ROWS:, :] = dot(half, held_ref[1]).astype(jnp.bfloat16)


def probabilities_of(query, key, same_image):
    scores = dot(query, key, (1, 1)) / math.sqrt(HEAD_DIM)
    scores = jnp.where(same_image, scores, -jnp.inf)
    weights = jnp.exp(scores - jnp.max(scores, axis=1, keepdims=True))
    return weights * (1.0 / jnp.sum(weights, axis=1, keepdims=True))


def forward_kernel(
    dp_size,
    mp_size,
    distances,
    query_hbm,
    key_hbm,
    value_hbm,
    weight_hbm,
    starts_ref,
    out_ref,
    held_ref,
    pair_starts_ref,
    query_ref,
    key_ref,
    value_ref,
    sems,
):
    width = query_ref.shape[1]
    dp, z = lax.axis_index("dp"), lax.axis_index("mp")
    right = goes_right(dp, dp_size)
    moves = [
        (query_hbm, query_ref),
        (key_hbm, key_ref),
        (value_hbm, value_ref),
    ]
    for slot, distance in enumerate(distances):
        index = lax.rem(z + jnp.where(right, distance, mp_size - distance), mp_size)
        columns = pl.ds(pl.multiple_of(index * width, 128), width)
        moves.append((weight_hbm.at[:, columns], held_ref.at[slot]))
    copies = started(moves, sems)
    own = starts_ref[pl.ds(dp, 1), :]
    pair_starts_ref[0:1, :] = own
    pair_starts_ref[1:2, :] = starts_ref[pl.ds(lax.rem(dp + dp_size // 2, dp_size), 1), :]
    same_image = as_column(own) == own
    for copy in copies[:3]:
        copy.wait()
    for head in range(width // HEAD_DIM):
        at = slice(head * HEAD_DIM, (head + 1) * HEAD_DIM)
        rounded = probabilities_of(query_ref[:, at], key_ref[:, at], same_image).astype(jnp.bfloat16)
        out_ref[:, at] = dot(rounded, value_ref[:, at]).astype(jnp.bfloat16)
    for copy in copies[3:]:
        copy.wait()


def unpacked(heavy, first, second):
    own_first = jnp.where(heavy, first, second)
    return own_first, dot(flip_matrix(), second.astype(jnp.bfloat16))


def backward_kernel(
    query_ref,
    key_ref,
    value_ref,
    partial_ref,
    other_ref,
    starts_ref,
    grad_query_ref,
    grad_key_ref,
    grad_value_ref,
    grad_ref,
):
    own, _ = starts_of(starts_ref)
    column = as_column(own)
    same_image = column == own
    valid = column >= 0
    pair = partial_ref[...] + other_ref[...].astype(jnp.float32)
    low, high = unpacked(is_heavy(own), pair[:SLOT], pair[SLOT:])
    grad_ref[:SLOT, :] = low.astype(jnp.bfloat16)
    grad_ref[SLOT:, :] = high.astype(jnp.bfloat16)
    for head in range(query_ref.shape[1] // HEAD_DIM):
        at = slice(head * HEAD_DIM, (head + 1) * HEAD_DIM)
        query, key, value, grad = query_ref[:, at], key_ref[:, at], value_ref[:, at], grad_ref[:, at]
        probabilities = probabilities_of(query, key, same_image)
        rounded = probabilities.astype(jnp.bfloat16)
        grad_value = dot(rounded, grad, (0, 0))
        grad_weights = dot(grad, value, (1, 1))
        correction = jnp.sum(probabilities * grad_weights, axis=1, keepdims=True)
        grad_scores = (probabilities * (grad_weights - correction) / math.sqrt(HEAD_DIM)).astype(
            jnp.bfloat16
        )
        grad_query = dot(grad_scores, key)
        grad_key = dot(grad_scores, query, (0, 0))
        grad_query_ref[:, at] = jnp.where(valid, grad_query, 0.0).astype(jnp.bfloat16)
        grad_key_ref[:, at] = jnp.where(valid, grad_key, 0.0).astype(jnp.bfloat16)
        grad_value_ref[:, at] = jnp.where(valid, grad_value, 0.0).astype(jnp.bfloat16)


def finish_kernel(total_ref, other_ref, starts_ref, out_ref):
    own, _ = starts_of(starts_ref)
    valid = as_column(own) >= 0
    pair = total_ref[...] + other_ref[...].astype(jnp.float32)
    low, high = unpacked(is_heavy(own), pair[:SLOT], pair[SLOT:])
    out_ref[:SLOT, :] = jnp.where(valid[:SLOT], low, 0.0).astype(jnp.bfloat16)
    out_ref[SLOT:, :] = jnp.where(valid[SLOT:], high, 0.0).astype(jnp.bfloat16)


def shards(query_rows, key_rows, value_rows, proj_weight, out_grad, image_starts):
    dp_size, mp_size = lax.axis_size("dp"), lax.axis_size("mp")
    width = query_rows.shape[1]
    near = mp_size // 4
    far = near + 1
    dp, z = lax.axis_index("dp"), lax.axis_index("mp")
    hop_perm = ring_pairs(dp_size, mp_size, 1)
    jump_perm = ring_pairs(dp_size, mp_size, far)
    swap_perm = [(i, (i + dp_size // 2) % dp_size) for i in range(dp_size)]
    right = goes_right(dp, dp_size)
    delta = jnp.where(right, 1, mp_size - 1)
    rows_type = jax.ShapeDtypeStruct((ROWS, width), jnp.bfloat16)
    half_type = jax.ShapeDtypeStruct((ROWS + SLOT, width), jnp.bfloat16)

    def hop(rows):
        return lax.ppermute(rows, ("dp", "mp"), hop_perm)

    def jump(rows):
        return lax.ppermute(rows, ("dp", "mp"), jump_perm)

    def swap(rows):
        return lax.ppermute(rows, "dp", swap_perm)

    def half_of(rows):
        return jnp.where(right, rows[:SLOT], rows[SLOT:])

    def place_half(rows):
        zeros = jnp.zeros_like(rows)
        return jnp.concatenate([jnp.where(right, rows, zeros), jnp.where(right, zeros, rows)], 0)

    def block_of(array, index):
        return lax.dynamic_slice_in_dim(array, lax.rem(index, mp_size) * width, width, 1)

    other_out_grad = swap(out_grad)
    in_hbm = pl.BlockSpec(memory_space=pltpu.HBM)
    in_any = pl.BlockSpec(memory_space=pl.ANY)
    held_type = jax.ShapeDtypeStruct((2, width, width), jnp.bfloat16)
    starts_type = jax.ShapeDtypeStruct((2, ROWS), jnp.int32)
    row_buffer = pltpu.VMEM((ROWS, width), jnp.bfloat16)
    starts_buffer = pltpu.VMEM((2, ROWS), jnp.int32)
    attended, held, starts = call(
        functools.partial(forward_kernel, dp_size, mp_size, (near, near + far - 1)),
        [rows_type, held_type, starts_type],
        (query_rows, key_rows, value_rows, proj_weight, image_starts),
        specs=[in_hbm] * 4 + [IN_VMEM],
        scratch=[row_buffer] * 3 + [pltpu.SemaphoreType.DMA((5,))],
        flops=4 * ROWS * ROWS * width,
        name="attention_forward",
        limit=FRONT_LIMIT,
    )
    other_attended = swap(attended)
    (pair_grad,) = call(
        pack_kernel,
        [rows_type],
        (out_grad, other_out_grad, starts),
        specs=[in_hbm, in_any, in_hbm],
        scratch=[row_buffer] * 2 + [starts_buffer, pltpu.SemaphoreType.DMA((3,))],
        name="pack_out_grad",
        limit=FRONT_LIMIT,
    )
    near_block, far_block = hop(pair_grad), jump(pair_grad)
    pair_attended, first_terms = call(
        functools.partial(pack_terms_kernel, dp_size),
        [rows_type, half_type],
        (attended, other_attended, starts, held),
        specs=[in_hbm, in_any, in_hbm, in_hbm],
        scratch=[row_buffer] * 2
        + [
            starts_buffer,
            pltpu.VMEM((2, width, width), jnp.bfloat16),
            pltpu.SemaphoreType.DMA((4,)),
        ],
        name="pack_attended",
        limit=FRONT_LIMIT,
    )
    sums = hop(first_terms)
    sums = [sums[:ROWS], place_half(sums[ROWS:])]

    def term(distance):
        return dot(pair_attended, block_of(proj_weight, z + distance * delta))

    def product(block, distance):
        return dot(block, block_of(proj_weight, z + distance * (mp_size - delta)), (1, 1))

    def plus(received, distance):
        return (received.astype(jnp.float32) + term(distance)).astype(jnp.bfloat16)

    partial = place_half(product(half_of(pair_grad), 0))
    for step in range(1, near):
        last = step == near - 1
        partial = partial + product(near_block, step) + product(far_block, far + step - 1)
        moved = hop(jnp.concatenate([near_block, half_of(far_block) if last else far_block], 0))
        near_block, far_block = moved[:ROWS], moved[ROWS:]
        sums = [plus(sums[0], near - step), plus(sums[1], near + far - 1 - step)]
        if last:
            sums = [hop(sums[0]), jump(sums[1])]
        else:
            sums = hop(jnp.concatenate(sums, 0))
            sums = [sums[:ROWS], sums[ROWS:]]
    partial = partial + product(near_block, near) + place_half(product(far_block, near + far - 1))
    near_sum, partial = lax.optimization_barrier((sums[0], partial))
    other_partial = swap(partial.astype(jnp.bfloat16))
    last_sum, other_partial = lax.optimization_barrier((sums[1], other_partial))
    total = (
        near_sum.astype(jnp.float32)
        + last_sum.astype(jnp.float32)
        + place_half(dot(half_of(pair_attended), block_of(proj_weight, z)))
    )
    other_total = swap(total.astype(jnp.bfloat16))
    grads = call(
        backward_kernel,
        [rows_type] * 3,
        (query_rows, key_rows, value_rows, partial, other_partial, starts),
        scratch=[pltpu.VMEM((ROWS, width), jnp.bfloat16)],
        flops=12 * ROWS * ROWS * width,
        name="attention_backward",
    )
    (projected,) = call(
        finish_kernel,
        [rows_type],
        (total, other_total, starts),
        name="finish_projected",
    )
    return (projected, *grads)


def solution(mesh):
    placed = (P("dp", "mp"), P("dp", "mp"), P("dp", "mp"), P("mp", None), P("dp", "mp"), P())
    return jax.shard_map(
        shards,
        mesh=mesh,
        in_specs=placed,
        out_specs=(P("dp", "mp"), P("dp", "mp"), P("dp", "mp"), P("dp", "mp")),
        check_vma=False,
    )
```

time: 122 us -> 113 us (0.926)
  the two profiles are of different devices: /device:TPU:8 before, /device:TPU:54 now
where the time goes in v3:
time: 113 us
  starting transfers between devices  68.8 us (61%)
  waiting for transfers between devices  19.9 us (18%)
  Pallas kernels  12.5 us (11%)
  matrix products  8.48 us (8%)
  local copies, waits for them, and re-layouts  1.4 us (1%)
  between operations  1.24 us (1%)
    ppermute x8, starting transfers between devices, hop(): return lax.ppermute(rows, ('dp', 'mp'), hop_perm)  47.8 us
    ppermute x2, waiting for transfers between devices, jump(): return lax.ppermute(rows, ('dp', 'mp'), jump_perm)  13.9 us
    pallas_call x5, Pallas kernels, call(): pl.pallas_call(kernel, out_shape=outs, in_specs=specs or [IN_VMEM] * len(...  12.5 us
    ppermute x4, starting transfers between devices, swap(): return lax.ppermute(rows, 'dp', swap_perm)  12.4 us
    ppermute x2, starting transfers between devices, jump(): return lax.ppermute(rows, ('dp', 'mp'), jump_perm)  8.57 us
    dot_general x16, matrix products, dot(): lax.dot_general(a, b, (((dims[0],), (dims[1],)), ((), ())), preferred_ele...  8.48 us
    ppermute x4, waiting for transfers between devices, swap(): return lax.ppermute(rows, 'dp', swap_perm)  3.77 us
  transfers between devices with their start and end apart: 14, of which 5 were waited for; matrix products, arithmetic and copies ran while one was open for 8% of the time, Pallas kernels for 10%

profile of v3, /device:TPU:54, one launch (start us, length us, event | category | flops | bytes accessed | tf_op | source)
XLA Modules:
  0.0 112.6 jit_solution(5704648906974456519)
XLA Ops:
  0.6 3.3 %collective-permute-start.5 = (bf16[256,384]{1,0:T(8,128)(2,1)}, bf16[256,384]{1,0:T(8,128)(2,1)S(1)}, u32[]{:S(2)}, u32[]{:S(2)}) collective-permute-start(bf16[256,384]{1,0:T(8,128)(2,1)} %own_hbm.1), channel_id=1, source_target_pairs={{0,512},{16,528},{32,544},{48,560},{64,576},{80,592},{96,608},{112... | collective-permute-start | bytes 589832 | tf_op jit(solution)/shard_map/ppermute | solution.py:267
  4.0 3.9 %attention_forward.1 = (bf16[256,384]{1,0:T(8,128)(2,1)}, bf16[2,384,384]{2,1,0:T(8,128)(2,1)}, s32[2,256]{1,0:T(2,128)}) custom-call(bf16[256,384]{1,0:T(8,128)(2,1)} %query_ref.1, bf16[256,384]{1,0:T(8,128)(2,1)} %key_ref.1, bf16[256,384]{1,0:T(8,128)(2,1)} %value_ref.1, bf16[384,6144]{1,0:T(8,128)(2,1)} %weight_hbm.1, s32[64,256]{1,0:T(8,128)} %starts_ref.1), custom_call_target="tpu_custom_call" | custom-call | flops 100663296 | bytes 6162432 | tf_op jit(solution)/shard_map/attention_forward/pallas_call | solution.py:43
  7.9 4.0 %collective-permute-start = (bf16[256,384]{1,0:T(8,128)(2,1)}, bf16[256,384]{1,0:T(8,128)(2,1)S(1)}, u32[]{:S(2)}, u32[]{:S(2)}) collective-permute-start(bf16[256,384]{1,0:T(8,128)(2,1)} %get-tuple-element.16.own_hbm), channel_id=1, source_target_pairs={{0,512},{16,528},{32,544},{48,560},{64,576},{80,592},{96,608},{112... | collective-permute-start | bytes 589832 | tf_op jit(solution)/shard_map/ppermute | solution.py:267
  12.1 0.7 copy-done.6
  12.8 2.4 %pack_out_grad.1 = bf16[256,384]{1,0:T(8,128)(2,1)} custom-call(bf16[256,384]{1,0:T(8,128)(2,1)} %own_hbm.1, bf16[256,384]{1,0:T(8,128)(2,1)} %copy-done.6, s32[2,256]{1,0:T(2,128)} %get-tuple-element.17.starts_hbm.starts_ref), custom_call_target="tpu_custom_call" | custom-call | bytes 591872 | tf_op jit(solution)/shard_map/pack_out_grad/pallas_call | solution.py:43
  15.2 18.2 %collective-permute-start.6 = (bf16[256,384]{1,0:T(8,128)(2,1)}, bf16[256,384]{1,0:T(8,128)(2,1)S(1)}, u32[]{:S(2)}, u32[]{:S(2)}) collective-permute-start(bf16[256,384]{1,0:T(8,128)(2,1)} %pack_out_grad.1), channel_id=1, source_target_pairs={{0,1},{1,2},{2,3},{3,4},{4,5},{5,6},{6,7},{7,8},{8,9},{9,10},{10,1... | collective-permute-start | bytes 589832 | tf_op jit(solution)/shard_map/ppermute | solution.py:261
  33.4 3.6 %collective-permute-start.7 = (bf16[256,384]{1,0:T(8,128)(2,1)}, bf16[256,384]{1,0:T(8,128)(2,1)S(1)}, u32[]{:S(2)}, u32[]{:S(2)}) collective-permute-start(bf16[256,384]{1,0:T(8,128)(2,1)} %pack_out_grad.1), channel_id=1, source_target_pairs={{0,5},{1,6},{2,7},{3,8},{4,9},{5,10},{6,11},{7,12},{8,13},{9,14},{... | collective-permute-start | bytes 589832 | tf_op jit(solution)/shard_map/ppermute | solution.py:264
  37.1 0.7 copy-done.7
  37.8 2.4 %pack_attended.1 = (bf16[256,384]{1,0:T(8,128)(2,1)}, bf16[384,384]{1,0:T(8,128)(2,1)}) custom-call(bf16[256,384]{1,0:T(8,128)(2,1)} %get-tuple-element.16.own_hbm, bf16[256,384]{1,0:T(8,128)(2,1)} %copy-done.7, s32[2,256]{1,0:T(2,128)} %get-tuple-element.17.starts_hbm.starts_ref, bf16[2,384,384]{2,1,0:T(8,128)(2,1)} %get-tuple-element.18.held_hbm), custom_call_target="tpu_custom_call" | custom-call | bytes 1476608 | tf_op jit(solution)/shard_map/pack_attended/pallas_call | solution.py:43
  40.2 2.6 %collective-permute-start.1 = (bf16[384,384]{1,0:T(8,128)(2,1)}, bf16[384,384]{1,0:T(8,128)(2,1)S(1)}, u32[]{:S(2)}, u32[]{:S(2)}) collective-permute-start(bf16[384,384]{1,0:T(8,128)(2,1)} %get-tuple-element.19), channel_id=1, source_target_pairs={{0,1},{1,2},{2,3},{3,4},{4,5},{5,6},{6,7},{7,8},{8,9},{9,10},{10,1... | collective-permute-start | bytes 884744 | tf_op jit(solution)/shard_map/ppermute | solution.py:261
  42.8 1.3 %broadcast_select_fusion.5 = (f32[128,384]{1,0:T(8,128)S(1)}, f32[128,384]{1,0:T(8,128)S(1)}) fusion(pred[]{:T(512)S(6)} %eq.3, bf16[384,6144]{1,0:T(8,128)(2,1)} %weight_hbm.1, s32[]{:T(128)S(6)} %select_n.110, bf16[256,384]{1,0:T(8,128)(2,1)} %pack_out_grad.1), kind=kOutput, calls=%fused_computation.65 | convolution fusion | flops 37896192 | bytes 886272 | tf_op jit(solution)/shard_map/dot_general | solution.py:36
  44.1 3.5 %collective-permute-done.7 = bf16[256,384]{1,0:T(8,128)(2,1)S(1)} collective-permute-done((bf16[256,384]{1,0:T(8,128)(2,1)}, bf16[256,384]{1,0:T(8,128)(2,1)S(1)}, u32[]{:S(2)}, u32[]{:S(2)}) %collective-permute-start.7) | collective-permute-done | bytes 196640 | tf_op jit(solution)/shard_map/ppermute | solution.py:264
  47.7 4.9 %collective-permute-start.8 = (bf16[512,384]{1,0:T(8,128)(2,1)S(1)}, bf16[512,384]{1,0:T(8,128)(2,1)S(1)}, u32[]{:S(2)}, u32[]{:S(2)}) collective-permute-start(bf16[512,384]{1,0:T(8,128)(2,1)S(1)} %pad_maximum_fusion.2), channel_id=1, source_target_pairs={{0,1},{1,2},{2,3},{3,4},{4,5},{5,6},{6,7},{7,8},{8,9},{9,10},{10,1... | collective-permute-start | bytes 1179656 | tf_op jit(solution)/shard_map/ppermute | solution.py:261
  52.6 1.3 %fusion.21 = f32[256,384]{1,0:T(8,128)S(1)} fusion(bf16[256,384]{1,0:T(8,128)(2,1)S(1)} %collective-permute-done.7, bf16[384,6144]{1,0:T(8,128)(2,1)} %weight_hbm.1, s32[]{:T(128)S(6)} %select_n.114), kind=kOutput, calls=%fused_computation.32 | convolution fusion | flops 75497472 | bytes 884740 | tf_op jit(solution)/shard_map/dot_general | solution.py:36
  53.9 1.3 %add_convert_fusion.4 = bf16[256,384]{1,0:T(8,128)(2,1)S(1)} fusion(bf16[256,384]{1,0:T(8,128)(2,1)} %get-tuple-element.20, bf16[384,6144]{1,0:T(8,128)(2,1)} %weight_hbm.1, s32[]{:T(128)S(6)} %select_n.105, bf16[128,384]{1,0:T(8,128)(2,1)S(1)} %get-tuple-element.31, bf16[128,384]{1,0:T(8,128)(2,1)S(1)} %get-tuple-element.30), kind=kOutput, calls=%fused_computation.16 | convolution fusion | flops 76087296 | bytes 884740 | tf_op jit(solution)/shard_map/dot_general | solution.py:36
  55.2 1.2 %add_convert_fusion.5 = bf16[256,384]{1,0:T(8,128)(2,1)S(1)} fusion(bf16[256,384]{1,0:T(8,128)(2,1)} %get-tuple-element.20, bf16[384,6144]{1,0:T(8,128)(2,1)S(1)} %copy-done.4, s32[]{:T(128)S(6)} %select_n.101, bf16[384,384]{1,0:T(8,128)(2,1)S(1)} %collective-permute-done.1), kind=kOutput, calls=%fused_computation.17 | convolution fusion | flops 75792384 | bytes 884740 | tf_op jit(solution)/shard_map/dot_general | solution.py:36
  56.5 3.9 %collective-permute-start.2 = (bf16[512,384]{1,0:T(8,128)(2,1)S(1)}, bf16[512,384]{1,0:T(8,128)(2,1)S(1)}, u32[]{:S(2)}, u32[]{:S(2)}) collective-permute-start(bf16[512,384]{1,0:T(8,128)(2,1)S(1)} %pad_maximum_fusion), channel_id=1, source_target_pairs={{0,1},{1,2},{2,3},{3,4},{4,5},{5,6},{6,7},{7,8},{8,9},{9,10},{10,1... | collective-permute-start | bytes 1179656 | tf_op jit(solution)/shard_map/ppermute | solution.py:261
  60.5 3.7 %collective-permute-start.9 = (bf16[512,384]{1,0:T(8,128)(2,1)S(1)}, bf16[512,384]{1,0:T(8,128)(2,1)S(1)}, u32[]{:S(2)}, u32[]{:S(2)}) collective-permute-start(bf16[512,384]{1,0:T(8,128)(2,1)S(1)} %collective-permute-done.8), channel_id=1, source_target_pairs={{0,1},{1,2},{2,3},{3,4},{4,5},{5,6},{6,7},{7,8},{8,9},{9,10},{10,1... | collective-permute-start | bytes 1179656 | tf_op jit(solution)/shard_map/ppermute | solution.py:261
  64.8 0.3 fusion.2
  65.1 1.1 collective-permute-done.2
  66.8 5.2 %collective-permute-start.3 = (bf16[512,384]{1,0:T(8,128)(2,1)S(1)}, bf16[512,384]{1,0:T(8,128)(2,1)S(1)}, u32[]{:S(2)}, u32[]{:S(2)}) collective-permute-start(bf16[512,384]{1,0:T(8,128)(2,1)S(1)} %pad_maximum_fusion.1), channel_id=1, source_target_pairs={{0,1},{1,2},{2,3},{3,4},{4,5},{5,6},{6,7},{7,8},{8,9},{9,10},{10,1... | collective-permute-start | bytes 1179656 | tf_op jit(solution)/shard_map/ppermute | solution.py:261
  72.1 3.7 %collective-permute-start.10 = (bf16[384,384]{1,0:T(8,128)(2,1)S(1)}, bf16[384,384]{1,0:T(8,128)(2,1)S(1)}, u32[]{:S(2)}, u32[]{:S(2)}) collective-permute-start(bf16[384,384]{1,0:T(8,128)(2,1)S(1)} %pad_maximum_fusion.3), channel_id=1, source_target_pairs={{0,1},{1,2},{2,3},{3,4},{4,5},{5,6},{6,7},{7,8},{8,9},{9,10},{10,1... | collective-permute-start | bytes 884744 | tf_op jit(solution)/shard_map/ppermute | solution.py:261
  76.1 1.1 collective-permute-done.3
  77.5 5.6 %collective-permute-start.4 = (bf16[256,384]{1,0:T(8,128)(2,1)S(1)}, bf16[256,384]{1,0:T(8,128)(2,1)S(1)}, u32[]{:S(2)}, u32[]{:S(2)}) collective-permute-start(bf16[256,384]{1,0:T(8,128)(2,1)S(1)} %add_convert_fusion.1), channel_id=1, source_target_pairs={{0,1},{1,2},{2,3},{3,4},{4,5},{5,6},{6,7},{7,8},{8,9},{9,10},{10,1... | collective-permute-start | bytes 589832 | tf_op jit(solution)/shard_map/ppermute | solution.py:261
  83.4 4.9 %collective-permute-start.11 = (bf16[256,384]{1,0:T(8,128)(2,1)S(1)}, bf16[256,384]{1,0:T(8,128)(2,1)S(1)}, u32[]{:S(2)}, u32[]{:S(2)}) collective-permute-start(bf16[256,384]{1,0:T(8,128)(2,1)S(1)} %add_convert_fusion), channel_id=1, source_target_pairs={{0,5},{1,6},{2,7},{3,8},{4,9},{5,10},{6,11},{7,12},{8,13},{9,14},{... | collective-permute-start | bytes 589832 | tf_op jit(solution)/shard_map/ppermute | solution.py:264
  88.9 0.3 fusion.5.partial_ref
  89.3 2.7 %collective-permute-start.12 = (bf16[256,384]{1,0:T(8,128)(2,1)S(1)}, bf16[256,384]{1,0:T(8,128)(2,1)S(1)}, u32[]{:S(2)}, u32[]{:S(2)}) collective-permute-start(bf16[256,384]{1,0:T(8,128)(2,1)S(1)} %convert_element_type.61), channel_id=1, source_target_pairs={{0,512},{16,528},{32,544},{48,560},{64,576},{80,592},{96,608},{112... | collective-permute-start | bytes 589832 | tf_op jit(solution)/shard_map/ppermute | solution.py:267
  92.2 10.4 %collective-permute-done.11 = bf16[256,384]{1,0:T(8,128)(2,1)S(1)} collective-permute-done((bf16[256,384]{1,0:T(8,128)(2,1)S(1)}, bf16[256,384]{1,0:T(8,128)(2,1)S(1)}, u32[]{:S(2)}, u32[]{:S(2)}) %collective-permute-start.11) | collective-permute-done | bytes 196640 | tf_op jit(solution)/shard_map/ppermute | solution.py:264
  102.7 2.4 %collective-permute-start.13 = (bf16[256,384]{1,0:T(8,128)(2,1)S(1)}, bf16[256,384]{1,0:T(8,128)(2,1)S(1)}, u32[]{:S(2)}, u32[]{:S(2)}) collective-permute-start(bf16[256,384]{1,0:T(8,128)(2,1)S(1)} %get-tuple-element.28), channel_id=1, source_target_pairs={{0,512},{16,528},{32,544},{48,560},{64,576},{80,592},{96,608},{112... | collective-permute-start | bytes 589832 | tf_op jit(solution)/shard_map/ppermute | solution.py:267
  105.1 2.8 %attention_backward.1 = (bf16[256,384]{1,0:T(8,128)(2,1)}, bf16[256,384]{1,0:T(8,128)(2,1)}, bf16[256,384]{1,0:T(8,128)(2,1)}) custom-call(bf16[256,384]{1,0:T(8,128)(2,1)S(1)} %copy-done, bf16[256,384]{1,0:T(8,128)(2,1)S(1)} %copy-done.1, bf16[256,384]{1,0:T(8,128)(2,1)S(1)} %copy-done.2, f32[256,384]{1,0:T(8,128)S(1)} %fusion.5.partial_ref, ...), custom_call_target="tpu_custom_call" | custom-call | flops 301989888 | bytes 1771520 | tf_op jit(solution)/shard_map/attention_backward/pallas_call | solution.py:43
  108.0 3.8 %collective-permute-done.13.other_ref = bf16[256,384]{1,0:T(8,128)(2,1)S(1)} collective-permute-done((bf16[256,384]{1,0:T(8,128)(2,1)S(1)}, bf16[256,384]{1,0:T(8,128)(2,1)S(1)}, u32[]{:S(2)}, u32[]{:S(2)}) %collective-permute-start.13) | collective-permute-done | bytes 196640 | tf_op jit(solution)/shard_map/ppermute | solution.py:267
  111.7 0.9 finish_projected.1
  (42 shorter events, 3.2 us)
Async XLA Ops:
  0.6 11.4 %collective-permute-start.5 = (bf16[256,384]{1,0:T(8,128)(2,1)}, bf16[256,384]{1,0:T(8,128)(2,1)S(1)}, u32[]{:S(2)}, u32[]{:S(2)}) collective-permute-start(bf16[256,384]{1,0:T(8,128)(2,1)} %own_hbm.1), channel_id=1, source_target_pairs={{0,512},{16,528},{32,544},{48,560},{64,576},{80,592},{96,608},{112... | collective-permute-start | bytes 589832 | tf_op jit(solution)/shard_map/ppermute | solution.py:267
  7.9 29.2 %collective-permute-start = (bf16[256,384]{1,0:T(8,128)(2,1)}, bf16[256,384]{1,0:T(8,128)(2,1)S(1)}, u32[]{:S(2)}, u32[]{:S(2)}) collective-permute-start(bf16[256,384]{1,0:T(8,128)(2,1)} %get-tuple-element.16.own_hbm), channel_id=1, source_target_pairs={{0,512},{16,528},{32,544},{48,560},{64,576},{80,592},{96,608},{112... | collective-permute-start | bytes 589832 | tf_op jit(solution)/shard_map/ppermute | solution.py:267
  12.0 43.2 %copy-start.4 = (bf16[384,6144]{1,0:T(8,128)(2,1)S(1)}, bf16[384,6144]{1,0:T(8,128)(2,1)}, u32[]{:S(2)}) copy-start(bf16[384,6144]{1,0:T(8,128)(2,1)} %weight_hbm.1) | copy-start | bytes 14155780
  12.1 0.7 copy-start.6
  15.2 28.9 %collective-permute-start.6 = (bf16[256,384]{1,0:T(8,128)(2,1)}, bf16[256,384]{1,0:T(8,128)(2,1)S(1)}, u32[]{:S(2)}, u32[]{:S(2)}) collective-permute-start(bf16[256,384]{1,0:T(8,128)(2,1)} %pack_out_grad.1), channel_id=1, source_target_pairs={{0,1},{1,2},{2,3},{3,4},{4,5},{5,6},{6,7},{7,8},{8,9},{9,10},{10,1... | collective-permute-start | bytes 589832 | tf_op jit(solution)/shard_map/ppermute | solution.py:261
  33.4 14.2 %collective-permute-start.7 = (bf16[256,384]{1,0:T(8,128)(2,1)}, bf16[256,384]{1,0:T(8,128)(2,1)S(1)}, u32[]{:S(2)}, u32[]{:S(2)}) collective-permute-start(bf16[256,384]{1,0:T(8,128)(2,1)} %pack_out_grad.1), channel_id=1, source_target_pairs={{0,5},{1,6},{2,7},{3,8},{4,9},{5,10},{6,11},{7,12},{8,13},{9,14},{... | collective-permute-start | bytes 589832 | tf_op jit(solution)/shard_map/ppermute | solution.py:264
  37.1 0.7 copy-start.7
  40.2 26.0 %copy-start.5 = (bf16[256,384]{1,0:T(8,128)(2,1)S(1)}, bf16[256,384]{1,0:T(8,128)(2,1)}, u32[]{:S(2)}) copy-start(bf16[256,384]{1,0:T(8,128)(2,1)} %get-tuple-element.20) | copy-start | bytes 589828
  40.2 13.6 %collective-permute-start.1 = (bf16[384,384]{1,0:T(8,128)(2,1)}, bf16[384,384]{1,0:T(8,128)(2,1)S(1)}, u32[]{:S(2)}, u32[]{:S(2)}) collective-permute-start(bf16[384,384]{1,0:T(8,128)(2,1)} %get-tuple-element.19), channel_id=1, source_target_pairs={{0,1},{1,2},{2,3},{3,4},{4,5},{5,6},{6,7},{7,8},{8,9},{9,10},{10,1... | collective-permute-start | bytes 884744 | tf_op jit(solution)/shard_map/ppermute | solution.py:261
  47.7 12.8 %collective-permute-start.8 = (bf16[512,384]{1,0:T(8,128)(2,1)S(1)}, bf16[512,384]{1,0:T(8,128)(2,1)S(1)}, u32[]{:S(2)}, u32[]{:S(2)}) collective-permute-start(bf16[512,384]{1,0:T(8,128)(2,1)S(1)} %pad_maximum_fusion.2), channel_id=1, source_target_pairs={{0,1},{1,2},{2,3},{3,4},{4,5},{5,6},{6,7},{7,8},{8,9},{9,10},{10,1... | collective-permute-start | bytes 1179656 | tf_op jit(solution)/shard_map/ppermute | solution.py:261
  56.5 9.7 %collective-permute-start.2 = (bf16[512,384]{1,0:T(8,128)(2,1)S(1)}, bf16[512,384]{1,0:T(8,128)(2,1)S(1)}, u32[]{:S(2)}, u32[]{:S(2)}) collective-permute-start(bf16[512,384]{1,0:T(8,128)(2,1)S(1)} %pad_maximum_fusion), channel_id=1, source_target_pairs={{0,1},{1,2},{2,3},{3,4},{4,5},{5,6},{6,7},{7,8},{8,9},{9,10},{10,1... | collective-permute-start | bytes 1179656 | tf_op jit(solution)/shard_map/ppermute | solution.py:261
  60.5 11.5 %collective-permute-start.9 = (bf16[512,384]{1,0:T(8,128)(2,1)S(1)}, bf16[512,384]{1,0:T(8,128)(2,1)S(1)}, u32[]{:S(2)}, u32[]{:S(2)}) collective-permute-start(bf16[512,384]{1,0:T(8,128)(2,1)S(1)} %collective-permute-done.8), channel_id=1, source_target_pairs={{0,1},{1,2},{2,3},{3,4},{4,5},{5,6},{6,7},{7,8},{8,9},{9,10},{10,1... | collective-permute-start | bytes 1179656 | tf_op jit(solution)/shard_map/ppermute | solution.py:261
  66.8 10.4 %collective-permute-start.3 = (bf16[512,384]{1,0:T(8,128)(2,1)S(1)}, bf16[512,384]{1,0:T(8,128)(2,1)S(1)}, u32[]{:S(2)}, u32[]{:S(2)}) collective-permute-start(bf16[512,384]{1,0:T(8,128)(2,1)S(1)} %pad_maximum_fusion.1), channel_id=1, source_target_pairs={{0,1},{1,2},{2,3},{3,4},{4,5},{5,6},{6,7},{7,8},{8,9},{9,10},{10,1... | collective-permute-start | bytes 1179656 | tf_op jit(solution)/shard_map/ppermute | solution.py:261
  72.1 33.0 %copy-start = (bf16[256,384]{1,0:T(8,128)(2,1)S(1)}, bf16[256,384]{1,0:T(8,128)(2,1)}, u32[]{:S(2)}) copy-start(bf16[256,384]{1,0:T(8,128)(2,1)} %query_ref.1) | copy-start | bytes 589828
  72.1 33.0 %copy-start.1 = (bf16[256,384]{1,0:T(8,128)(2,1)S(1)}, bf16[256,384]{1,0:T(8,128)(2,1)}, u32[]{:S(2)}) copy-start(bf16[256,384]{1,0:T(8,128)(2,1)} %key_ref.1) | copy-start | bytes 589828
  72.1 33.0 %copy-start.2 = (bf16[256,384]{1,0:T(8,128)(2,1)S(1)}, bf16[256,384]{1,0:T(8,128)(2,1)}, u32[]{:S(2)}) copy-start(bf16[256,384]{1,0:T(8,128)(2,1)} %value_ref.1) | copy-start | bytes 589828
  72.1 33.0 %copy-start.3 = (s32[2,256]{1,0:T(2,128)S(1)}, s32[2,256]{1,0:T(2,128)}, u32[]{:S(2)}) copy-start(s32[2,256]{1,0:T(2,128)} %get-tuple-element.17.starts_hbm.starts_ref) | copy-start | bytes 6148
  72.1 16.2 %collective-permute-start.10 = (bf16[384,384]{1,0:T(8,128)(2,1)S(1)}, bf16[384,384]{1,0:T(8,128)(2,1)S(1)}, u32[]{:S(2)}, u32[]{:S(2)}) collective-permute-start(bf16[384,384]{1,0:T(8,128)(2,1)S(1)} %pad_maximum_fusion.3), channel_id=1, source_target_pairs={{0,1},{1,2},{2,3},{3,4},{4,5},{5,6},{6,7},{7,8},{8,9},{9,10},{10,1... | collective-permute-start | bytes 884744 | tf_op jit(solution)/shard_map/ppermute | solution.py:261
  77.5 11.7 %collective-permute-start.4 = (bf16[256,384]{1,0:T(8,128)(2,1)S(1)}, bf16[256,384]{1,0:T(8,128)(2,1)S(1)}, u32[]{:S(2)}, u32[]{:S(2)}) collective-permute-start(bf16[256,384]{1,0:T(8,128)(2,1)S(1)} %add_convert_fusion.1), channel_id=1, source_target_pairs={{0,1},{1,2},{2,3},{3,4},{4,5},{5,6},{6,7},{7,8},{8,9},{9,10},{10,1... | collective-permute-start | bytes 589832 | tf_op jit(solution)/shard_map/ppermute | solution.py:261
  83.4 19.2 %collective-permute-start.11 = (bf16[256,384]{1,0:T(8,128)(2,1)S(1)}, bf16[256,384]{1,0:T(8,128)(2,1)S(1)}, u32[]{:S(2)}, u32[]{:S(2)}) collective-permute-start(bf16[256,384]{1,0:T(8,128)(2,1)S(1)} %add_convert_fusion), channel_id=1, source_target_pairs={{0,5},{1,6},{2,7},{3,8},{4,9},{5,10},{6,11},{7,12},{8,13},{9,14},{... | collective-permute-start | bytes 589832 | tf_op jit(solution)/shard_map/ppermute | solution.py:264
  89.3 13.3 %collective-permute-start.12 = (bf16[256,384]{1,0:T(8,128)(2,1)S(1)}, bf16[256,384]{1,0:T(8,128)(2,1)S(1)}, u32[]{:S(2)}, u32[]{:S(2)}) collective-permute-start(bf16[256,384]{1,0:T(8,128)(2,1)S(1)} %convert_element_type.61), channel_id=1, source_target_pairs={{0,512},{16,528},{32,544},{48,560},{64,576},{80,592},{96,608},{112... | collective-permute-start | bytes 589832 | tf_op jit(solution)/shard_map/ppermute | solution.py:267
  102.7 9.1 %collective-permute-start.13 = (bf16[256,384]{1,0:T(8,128)(2,1)S(1)}, bf16[256,384]{1,0:T(8,128)(2,1)S(1)}, u32[]{:S(2)}, u32[]{:S(2)}) collective-permute-start(bf16[256,384]{1,0:T(8,128)(2,1)S(1)} %get-tuple-element.28), channel_id=1, source_target_pairs={{0,512},{16,528},{32,544},{48,560},{64,576},{80,592},{96,608},{112... | collective-permute-start | bytes 589832 | tf_op jit(solution)/shard_map/ppermute | solution.py:267

commit v4 on v3

--- a/solution.py
+++ b/solution.py
@@ -90,17 +90,7 @@
     return first, second_slot
 
 
-def started(moves, sems):
-    copies = [pltpu.make_async_copy(*move, sems.at[at]) for at, move in enumerate(moves)]
-    for copy in copies:
-        copy.start()
-    return copies
-
-
-def pack_kernel(own_hbm, other_hbm, starts_hbm, out_ref, own_ref, other_ref, starts_ref, sems):
-    moves = [(starts_hbm, starts_ref), (own_hbm, own_ref), (other_hbm, other_ref)]
-    for copy in started(moves, sems):
-        copy.wait()
+def pack_kernel(own_ref, other_ref, starts_ref, out_ref):
     first, second = packed_slots(*starts_of(starts_ref), own_ref, other_ref)
     out_ref[:SLOT, :] = first
     out_ref[SLOT:, :] = second
@@ -108,36 +98,64 @@
 
 def pack_terms_kernel(
     dp_size,
-    own_hbm,
-    other_hbm,
-    starts_hbm,
-    held_hbm,
-    out_ref,
-    terms_ref,
+    mp_size,
+    distances,
     own_ref,
     other_ref,
     starts_ref,
-    held_ref,
-    sems,
+    weight_ref,
+    earlier_ref,
+    out_ref,
+    terms_ref,
 ):
-    moves = [
-        (starts_hbm, starts_ref),
-        (own_hbm, own_ref),
-        (other_hbm, other_ref),
-        (held_hbm, held_ref),
-    ]
-    copies = started(moves, sems)
+    del earlier_ref
     right = goes_right(lax.axis_index("dp"), dp_size)
-    for copy in copies[:3]:
-        copy.wait()
     first, second = packed_slots(*starts_of(starts_ref), own_ref, other_ref)
     out_ref[:SLOT, :] = first
     out_ref[SLOT:, :] = second
     half = jnp.where(right, first, second)
-    copies[3].wait()
-    terms_ref[:SLOT, :] = dot(first, held_ref[0]).astype(jnp.bfloat16)
-    terms_ref[SLOT:ROWS, :] = dot(second, held_ref[0]).astype(jnp.bfloat16)
-    terms_ref[ROWS:, :] = dot(half, held_ref[1]).astype(jnp.bfloat16)
+
+    near_weight, far_weight = weights_at(dp_size, mp_size, distances, weight_ref)
+    terms_ref[:SLOT, :] = dot(first, near_weight).astype(jnp.bfloat16)
+    terms_ref[SLOT:ROWS, :] = dot(second, near_weight).astype(jnp.bfloat16)
+    terms_ref[ROWS:, :] = dot(half, far_weight).astype(jnp.bfloat16)
+
+
+def weights_at(dp_size, mp_size, distances, weight_ref):
+    width = weight_ref.shape[0]
+    right = goes_right(lax.axis_index("dp"), dp_size)
+    found = []
+    for distance in distances:
+        ahead = jnp.where(right, distance, mp_size - distance)
+        index = lax.rem(lax.axis_index("mp") + ahead, mp_size)
+        found.append(weight_ref[:, pl.ds(pl.multiple_of(index * width, 128), width)])
+    return found
+
+
+def add_terms_kernel(dp_size, mp_size, distances, sums_ref, rows_ref, weight_ref, *out_refs):
+    near_weight, far_weight = weights_at(dp_size, mp_size, distances, weight_ref)
+    near_term, far_term = dot(rows_ref[...], near_weight), dot(rows_ref[...], far_weight)
+    near_sum = sums_ref[:ROWS, :].astype(jnp.float32) + near_term
+    if sums_ref.shape[0] == 2 * ROWS:
+        far_sum = sums_ref[ROWS:, :].astype(jnp.float32) + far_term
+    else:
+        right = goes_right(lax.axis_index("dp"), dp_size)
+        half = sums_ref[ROWS:, :].astype(jnp.float32)
+        first = jnp.where(right, half, 0.0) + far_term[:SLOT]
+        second = jnp.where(right, 0.0, half) + far_term[SLOT:]
+        far_sum = jnp.concatenate([first, second], 0)
+    if len(out_refs) == 2:
+        out_refs[0][...] = near_sum.astype(jnp.bfloat16)
+        out_refs[1][...] = far_sum.astype(jnp.bfloat16)
+    else:
+        out_refs[0][:ROWS, :] = near_sum.astype(jnp.bfloat16)
+        out_refs[0][ROWS:, :] = far_sum.astype(jnp.bfloat16)
+
+
+def join_kernel(near_ref, far_ref, earlier_ref, out_ref):
+    del earlier_ref
+    out_ref[:ROWS, :] = near_ref[...]
+    out_ref[ROWS:, :] = far_ref[...]
 
 
 def probabilities_of(query, key, same_image):
@@ -147,48 +165,17 @@
     return weights * (1.0 / jnp.sum(weights, axis=1, keepdims=True))
 
 
-def forward_kernel(
-    dp_size,
-    mp_size,
-    distances,
-    query_hbm,
-    key_hbm,
-    value_hbm,
-    weight_hbm,
-    starts_ref,
-    out_ref,
-    held_ref,
-    pair_starts_ref,
-    query_ref,
-    key_ref,
-    value_ref,
-    sems,
-):
+def forward_kernel(dp_size, query_ref, key_ref, value_ref, starts_ref, out_ref, pair_starts_ref):
     width = query_ref.shape[1]
-    dp, z = lax.axis_index("dp"), lax.axis_index("mp")
-    right = goes_right(dp, dp_size)
-    moves = [
-        (query_hbm, query_ref),
-        (key_hbm, key_ref),
-        (value_hbm, value_ref),
-    ]
-    for slot, distance in enumerate(distances):
-        index = lax.rem(z + jnp.where(right, distance, mp_size - distance), mp_size)
-        columns = pl.ds(pl.multiple_of(index * width, 128), width)
-        moves.append((weight_hbm.at[:, columns], held_ref.at[slot]))
-    copies = started(moves, sems)
+    dp = lax.axis_index("dp")
     own = starts_ref[pl.ds(dp, 1), :]
     pair_starts_ref[0:1, :] = own
     pair_starts_ref[1:2, :] = starts_ref[pl.ds(lax.rem(dp + dp_size // 2, dp_size), 1), :]
     same_image = as_column(own) == own
-    for copy in copies[:3]:
-        copy.wait()
     for head in range(width // HEAD_DIM):
         at = slice(head * HEAD_DIM, (head + 1) * HEAD_DIM)
         rounded = probabilities_of(query_ref[:, at], key_ref[:, at], same_image).astype(jnp.bfloat16)
         out_ref[:, at] = dot(rounded, value_ref[:, at]).astype(jnp.bfloat16)
-    for copy in copies[3:]:
-        copy.wait()
 
 
 def unpacked(heavy, first, second):
@@ -277,75 +264,66 @@
         return lax.dynamic_slice_in_dim(array, lax.rem(index, mp_size) * width, width, 1)
 
     other_out_grad = swap(out_grad)
-    in_hbm = pl.BlockSpec(memory_space=pltpu.HBM)
     in_any = pl.BlockSpec(memory_space=pl.ANY)
-    held_type = jax.ShapeDtypeStruct((2, width, width), jnp.bfloat16)
-    starts_type = jax.ShapeDtypeStruct((2, ROWS), jnp.int32)
-    row_buffer = pltpu.VMEM((ROWS, width), jnp.bfloat16)
-    starts_buffer = pltpu.VMEM((2, ROWS), jnp.int32)
-    attended, held, starts = call(
-        functools.partial(forward_kernel, dp_size, mp_size, (near, near + far - 1)),
-        [rows_type, held_type, starts_type],
-        (query_rows, key_rows, value_rows, proj_weight, image_starts),
-        specs=[in_hbm] * 4 + [IN_VMEM],
-        scratch=[row_buffer] * 3 + [pltpu.SemaphoreType.DMA((5,))],
+    attended, starts = call(
+        functools.partial(forward_kernel, dp_size),
+        [rows_type, jax.ShapeDtypeStruct((2, ROWS), jnp.int32)],
+        (query_rows, key_rows, value_rows, image_starts),
         flops=4 * ROWS * ROWS * width,
         name="attention_forward",
-        limit=FRONT_LIMIT,
     )
     other_attended = swap(attended)
     (pair_grad,) = call(
-        pack_kernel,
-        [rows_type],
-        (out_grad, other_out_grad, starts),
-        specs=[in_hbm, in_any, in_hbm],
-        scratch=[row_buffer] * 2 + [starts_buffer, pltpu.SemaphoreType.DMA((3,))],
-        name="pack_out_grad",
-        limit=FRONT_LIMIT,
+        pack_kernel, [rows_type], (out_grad, other_out_grad, starts), name="pack_out_grad"
     )
     near_block, far_block = hop(pair_grad), jump(pair_grad)
     pair_attended, first_terms = call(
-        functools.partial(pack_terms_kernel, dp_size),
+        functools.partial(pack_terms_kernel, dp_size, mp_size, (near, near + far - 1)),
         [rows_type, half_type],
-        (attended, other_attended, starts, held),
-        specs=[in_hbm, in_any, in_hbm, in_hbm],
-        scratch=[row_buffer] * 2
-        + [
-            starts_buffer,
-            pltpu.VMEM((2, width, width), jnp.bfloat16),
-            pltpu.SemaphoreType.DMA((4,)),
-        ],
+        (attended, other_attended, starts, proj_weight, pair_grad),
+        specs=[IN_VMEM] * 4 + [in_any],
         name="pack_attended",
-        limit=FRONT_LIMIT,
-    )
-    sums = hop(first_terms)
-    sums = [sums[:ROWS], place_half(sums[ROWS:])]
-
-    def term(distance):
-        return dot(pair_attended, block_of(proj_weight, z + distance * delta))
+    )
 
     def product(block, distance):
         return dot(block, block_of(proj_weight, z + distance * (mp_size - delta)), (1, 1))
 
-    def plus(received, distance):
-        return (received.astype(jnp.float32) + term(distance)).astype(jnp.bfloat16)
+    def add_terms(sums, step):
+        distances = (near - step, near + far - 1 - step)
+        joined = jax.ShapeDtypeStruct((2 * ROWS, width), jnp.bfloat16)
+        return call(
+            functools.partial(add_terms_kernel, dp_size, mp_size, distances),
+            [rows_type, rows_type] if step == near - 1 else [joined],
+            (sums, pair_attended, proj_weight),
+            flops=4 * ROWS * width * width,
+            name="add_terms",
+        )
+
+    sums = hop(first_terms)
+    for step in range(1, near - 1):
+        sums = hop(*add_terms(sums, step))
+        if step == 1:
+            (moved,) = call(
+                join_kernel,
+                [jax.ShapeDtypeStruct((2 * ROWS, width), jnp.bfloat16)],
+                (near_block, far_block, first_terms),
+                specs=[IN_VMEM] * 2 + [in_any],
+                name="join_out_grad",
+            )
+    near_sum, last_sum = add_terms(sums, near - 1)
+    last_sum, near_sum = jump(last_sum), hop(near_sum)
 
     partial = place_half(product(half_of(pair_grad), 0))
     for step in range(1, near):
-        last = step == near - 1
+        near_block, far_block = moved[:ROWS], moved[ROWS:]
         partial = partial + product(near_block, step) + product(far_block, far + step - 1)
-        moved = hop(jnp.concatenate([near_block, half_of(far_block) if last else far_block], 0))
-        near_block, far_block = moved[:ROWS], moved[ROWS:]
-        sums = [plus(sums[0], near - step), plus(sums[1], near + far - 1 - step)]
-        if last:
-            sums = [hop(sums[0]), jump(sums[1])]
-        else:
-            sums = hop(jnp.concatenate(sums, 0))
-            sums = [sums[:ROWS], sums[ROWS:]]
+        if step == near - 1:
+            moved = jnp.concatenate([near_block, half_of(far_block)], 0)
+        moved = hop(moved)
+    near_block, far_block = moved[:ROWS], moved[ROWS:]
     partial = partial + product(near_block, near) + place_half(product(far_block, near + far - 1))
-    near_sum, partial = lax.optimization_barrier((sums[0], partial))
     other_partial = swap(partial.astype(jnp.bfloat16))
-    last_sum, other_partial = lax.optimization_barrier((sums[1], other_partial))
+    last_sum, other_partial = lax.optimization_barrier((last_sum, other_partial))
     total = (
         near_sum.astype(jnp.float32)
         + last_sum.astype(jnp.float32)

time: 113 us -> 108 us (0.956)
  the two profiles are of different devices: /device:TPU:54 before, /device:TPU:32 now
where the time goes in v4:
time: 108 us
  starting transfers between devices  57.8 us (54%)
  waiting for transfers between devices  32.1 us (30%)
  local copies, waits for them, and re-layouts  6.91 us (6%)
  Pallas kernels  6.78 us (6%)
  matrix products  2.85 us (3%)
  between operations  1.08 us (1%)
    ppermute x8, starting transfers between devices, hop(): return lax.ppermute(rows, ('dp', 'mp'), hop_perm)  24.5 us
    ppermute x8, waiting for transfers between devices, hop(): return lax.ppermute(rows, ('dp', 'mp'), hop_perm)  19.8 us
    ppermute x4, starting transfers between devices, swap(): return lax.ppermute(rows, 'dp', swap_perm)  18.6 us
    ppermute x2, starting transfers between devices, jump(): return lax.ppermute(rows, ('dp', 'mp'), jump_perm)  14.6 us
    ppermute x2, waiting for transfers between devices, jump(): return lax.ppermute(rows, ('dp', 'mp'), jump_perm)  9.16 us
    unnamed x20, local copies, waits for them, and re-layouts  6.89 us
    pallas_call x9, Pallas kernels, call(): pl.pallas_call(kernel, out_shape=outs, in_specs=specs or [IN_VMEM] * len(...  6.78 us
    ppermute x4, waiting for transfers between devices, swap(): return lax.ppermute(rows, 'dp', swap_perm)  3.16 us
  transfers between devices with their start and end apart: 14, of which 9 were waited for; matrix products, arithmetic and copies ran while one was open for 3% of the time, Pallas kernels for 5%

profile of v4, /device:TPU:32, one launch (start us, length us, event | category | flops | bytes accessed | tf_op | source)
XLA Modules:
  0.0 107.7 jit_solution(9935169144099142084)
XLA Ops:
  0.6 4.9 %collective-permute-start.1 = (bf16[256,384]{1,0:T(8,128)(2,1)}, bf16[256,384]{1,0:T(8,128)(2,1)S(1)}, u32[]{:S(2)}, u32[]{:S(2)}) collective-permute-start(bf16[256,384]{1,0:T(8,128)(2,1)} %own_ref.1), channel_id=1, source_target_pairs={{0,512},{16,528},{32,544},{48,560},{64,576},{80,592},{96,608},{112... | collective-permute-start | bytes 589832 | tf_op jit(solution)/shard_map/ppermute | solution.py:254
  5.6 0.9 copy-done.2
  6.5 0.9 copy-done.4
  7.4 0.9 copy-done.6
  8.4 0.8 copy-done.9
  9.2 1.0 attention_forward.1
  10.2 2.4 %collective-permute-start = (bf16[256,384]{1,0:T(8,128)(2,1)S(1)}, bf16[256,384]{1,0:T(8,128)(2,1)S(1)}, u32[]{:S(2)}, u32[]{:S(2)}) collective-permute-start(bf16[256,384]{1,0:T(8,128)(2,1)S(1)} %get-tuple-element.15.own_ref), channel_id=1, source_target_pairs={{0,512},{16,528},{32,544},{48,560},{64,576},{80,592},{96,608},{112... | collective-permute-start | bytes 589832 | tf_op jit(solution)/shard_map/ppermute | solution.py:254
  12.7 0.9 copy-done.8
  13.9 4.3 %collective-permute-start.7 = (bf16[256,384]{1,0:T(8,128)(2,1)S(1)}, bf16[256,384]{1,0:T(8,128)(2,1)S(1)}, u32[]{:S(2)}, u32[]{:S(2)}) collective-permute-start(bf16[256,384]{1,0:T(8,128)(2,1)S(1)} %pack_out_grad.1.earlier_ref), channel_id=1, source_target_pairs={{0,1},{1,2},{2,3},{3,4},{4,5},{5,6},{6,7},{7,8},{8,9},{9,10},{10,1... | collective-permute-start | bytes 589832 | tf_op jit(solution)/shard_map/ppermute | solution.py:248
  18.2 12.7 %collective-permute-start.8 = (bf16[256,384]{1,0:T(8,128)(2,1)S(1)}, bf16[256,384]{1,0:T(8,128)(2,1)S(1)}, u32[]{:S(2)}, u32[]{:S(2)}) collective-permute-start(bf16[256,384]{1,0:T(8,128)(2,1)S(1)} %pack_out_grad.1.earlier_ref), channel_id=1, source_target_pairs={{0,5},{1,6},{2,7},{3,8},{4,9},{5,10},{6,11},{7,12},{8,13},{9,14},{... | collective-permute-start | bytes 589832 | tf_op jit(solution)/shard_map/ppermute | solution.py:251
  31.0 2.3 %copy-done = bf16[384,6144]{1,0:T(8,128)(2,1)S(1)} copy-done((bf16[384,6144]{1,0:T(8,128)(2,1)S(1)}, bf16[384,6144]{1,0:T(8,128)(2,1)}, u32[]{:S(2)}) %copy-start) | copy-done | bytes 4718616
  33.4 0.6 pack_attended.1
  33.9 4.6 %collective-permute-start.2 = (bf16[384,384]{1,0:T(8,128)(2,1)S(1)}, bf16[384,384]{1,0:T(8,128)(2,1)S(1)}, u32[]{:S(2)}, u32[]{:S(2)}) collective-permute-start(bf16[384,384]{1,0:T(8,128)(2,1)S(1)} %get-tuple-element.17.earlier_ref), channel_id=1, source_target_pairs={{0,1},{1,2},{2,3},{3,4},{4,5},{5,6},{6,7},{7,8},{8,9},{9,10},{10,1... | collective-permute-start | bytes 884744 | tf_op jit(solution)/shard_map/ppermute | solution.py:248
  38.5 2.3 %collective-permute-done.8.far_ref = bf16[256,384]{1,0:T(8,128)(2,1)S(1)} collective-permute-done((bf16[256,384]{1,0:T(8,128)(2,1)S(1)}, bf16[256,384]{1,0:T(8,128)(2,1)S(1)}, u32[]{:S(2)}, u32[]{:S(2)}) %collective-permute-start.8) | collective-permute-done | bytes 196640 | tf_op jit(solution)/shard_map/ppermute | solution.py:251
  40.9 4.3 %collective-permute-start.9 = (bf16[512,384]{1,0:T(8,128)(2,1)S(1)}, bf16[512,384]{1,0:T(8,128)(2,1)S(1)}, u32[]{:S(2)}, u32[]{:S(2)}) collective-permute-start(bf16[512,384]{1,0:T(8,128)(2,1)S(1)} %join_out_grad.1), channel_id=1, source_target_pairs={{0,1},{1,2},{2,3},{3,4},{4,5},{5,6},{6,7},{7,8},{8,9},{9,10},{10,1... | collective-permute-start | bytes 1179656 | tf_op jit(solution)/shard_map/ppermute | solution.py:248
  45.8 4.1 %collective-permute-done.2.sums_ref = bf16[384,384]{1,0:T(8,128)(2,1)S(1)} collective-permute-done((bf16[384,384]{1,0:T(8,128)(2,1)S(1)}, bf16[384,384]{1,0:T(8,128)(2,1)S(1)}, u32[]{:S(2)}, u32[]{:S(2)}) %collective-permute-start.2) | collective-permute-done | bytes 294944 | tf_op jit(solution)/shard_map/ppermute | solution.py:248
  50.2 3.2 %collective-permute-start.3 = (bf16[512,384]{1,0:T(8,128)(2,1)S(1)}, bf16[512,384]{1,0:T(8,128)(2,1)S(1)}, u32[]{:S(2)}, u32[]{:S(2)}) collective-permute-start(bf16[512,384]{1,0:T(8,128)(2,1)S(1)} %add_terms.3), channel_id=1, source_target_pairs={{0,1},{1,2},{2,3},{3,4},{4,5},{5,6},{6,7},{7,8},{8,9},{9,10},{10,1... | collective-permute-start | bytes 1179656 | tf_op jit(solution)/shard_map/ppermute | solution.py:248
  53.5 7.3 %collective-permute-done.9 = bf16[512,384]{1,0:T(8,128)(2,1)S(1)} collective-permute-done((bf16[512,384]{1,0:T(8,128)(2,1)S(1)}, bf16[512,384]{1,0:T(8,128)(2,1)S(1)}, u32[]{:S(2)}, u32[]{:S(2)}) %collective-permute-start.9) | collective-permute-done | bytes 393248 | tf_op jit(solution)/shard_map/ppermute | solution.py:248
  60.7 1.9 %collective-permute-start.10 = (bf16[512,384]{1,0:T(8,128)(2,1)S(1)}, bf16[512,384]{1,0:T(8,128)(2,1)S(1)}, u32[]{:S(2)}, u32[]{:S(2)}) collective-permute-start(bf16[512,384]{1,0:T(8,128)(2,1)S(1)} %collective-permute-done.9), channel_id=1, source_target_pairs={{0,1},{1,2},{2,3},{3,4},{4,5},{5,6},{6,7},{7,8},{8,9},{9,10},{10,1... | collective-permute-start | bytes 1179656 | tf_op jit(solution)/shard_map/ppermute | solution.py:248
  63.3 1.7 %collective-permute-done.3.sums_ref = bf16[512,384]{1,0:T(8,128)(2,1)S(1)} collective-permute-done((bf16[512,384]{1,0:T(8,128)(2,1)S(1)}, bf16[512,384]{1,0:T(8,128)(2,1)S(1)}, u32[]{:S(2)}, u32[]{:S(2)}) %collective-permute-start.3) | collective-permute-done | bytes 393248 | tf_op jit(solution)/shard_map/ppermute | solution.py:248
  65.3 1.9 %collective-permute-start.4 = (bf16[512,384]{1,0:T(8,128)(2,1)S(1)}, bf16[512,384]{1,0:T(8,128)(2,1)S(1)}, u32[]{:S(2)}, u32[]{:S(2)}) collective-permute-start(bf16[512,384]{1,0:T(8,128)(2,1)S(1)} %add_terms.4), channel_id=1, source_target_pairs={{0,1},{1,2},{2,3},{3,4},{4,5},{5,6},{6,7},{7,8},{8,9},{9,10},{10,1... | collective-permute-start | bytes 1179656 | tf_op jit(solution)/shard_map/ppermute | solution.py:248
  67.3 4.3 %collective-permute-done.10 = bf16[512,384]{1,0:T(8,128)(2,1)S(1)} collective-permute-done((bf16[512,384]{1,0:T(8,128)(2,1)S(1)}, bf16[512,384]{1,0:T(8,128)(2,1)S(1)}, u32[]{:S(2)}, u32[]{:S(2)}) %collective-permute-start.10) | collective-permute-done | bytes 393248 | tf_op jit(solution)/shard_map/ppermute | solution.py:248
  71.7 1.9 %collective-permute-start.11 = (bf16[384,384]{1,0:T(8,128)(2,1)S(1)}, bf16[384,384]{1,0:T(8,128)(2,1)S(1)}, u32[]{:S(2)}, u32[]{:S(2)}) collective-permute-start(bf16[384,384]{1,0:T(8,128)(2,1)S(1)} %pad_maximum_fusion), channel_id=1, source_target_pairs={{0,1},{1,2},{2,3},{3,4},{4,5},{5,6},{6,7},{7,8},{8,9},{9,10},{10,1... | collective-permute-start | bytes 884744 | tf_op jit(solution)/shard_map/ppermute | solution.py:248
  74.3 1.9 %collective-permute-done.4.sums_ref = bf16[512,384]{1,0:T(8,128)(2,1)S(1)} collective-permute-done((bf16[512,384]{1,0:T(8,128)(2,1)S(1)}, bf16[512,384]{1,0:T(8,128)(2,1)S(1)}, u32[]{:S(2)}, u32[]{:S(2)}) %collective-permute-start.4) | collective-permute-done | bytes 393248 | tf_op jit(solution)/shard_map/ppermute | solution.py:248
  76.6 1.9 %collective-permute-start.6 = (bf16[256,384]{1,0:T(8,128)(2,1)S(1)}, bf16[256,384]{1,0:T(8,128)(2,1)S(1)}, u32[]{:S(2)}, u32[]{:S(2)}) collective-permute-start(bf16[256,384]{1,0:T(8,128)(2,1)S(1)} %get-tuple-element.20), channel_id=1, source_target_pairs={{0,5},{1,6},{2,7},{3,8},{4,9},{5,10},{6,11},{7,12},{8,13},{9,14},{... | collective-permute-start | bytes 589832 | tf_op jit(solution)/shard_map/ppermute | solution.py:251
  78.6 2.4 %collective-permute-start.5 = (bf16[256,384]{1,0:T(8,128)(2,1)S(1)}, bf16[256,384]{1,0:T(8,128)(2,1)S(1)}, u32[]{:S(2)}, u32[]{:S(2)}) collective-permute-start(bf16[256,384]{1,0:T(8,128)(2,1)S(1)} %get-tuple-element.19), channel_id=1, source_target_pairs={{0,1},{1,2},{2,3},{3,4},{4,5},{5,6},{6,7},{7,8},{8,9},{9,10},{10,1... | collective-permute-start | bytes 589832 | tf_op jit(solution)/shard_map/ppermute | solution.py:248
  82.4 8.3 %collective-permute-start.12 = (bf16[256,384]{1,0:T(8,128)(2,1)S(1)}, bf16[256,384]{1,0:T(8,128)(2,1)S(1)}, u32[]{:S(2)}, u32[]{:S(2)}) collective-permute-start(bf16[256,384]{1,0:T(8,128)(2,1)S(1)} %get-tuple-element.34), channel_id=1, source_target_pairs={{0,512},{16,528},{32,544},{48,560},{64,576},{80,592},{96,608},{112... | collective-permute-start | bytes 589832 | tf_op jit(solution)/shard_map/ppermute | solution.py:254
  90.9 6.8 %collective-permute-done.6 = bf16[256,384]{1,0:T(8,128)(2,1)S(1)} collective-permute-done((bf16[256,384]{1,0:T(8,128)(2,1)S(1)}, bf16[256,384]{1,0:T(8,128)(2,1)S(1)}, u32[]{:S(2)}, u32[]{:S(2)}) %collective-permute-start.6) | collective-permute-done | bytes 196640 | tf_op jit(solution)/shard_map/ppermute | solution.py:251
  97.8 3.0 %collective-permute-start.13 = (bf16[256,384]{1,0:T(8,128)(2,1)S(1)}, bf16[256,384]{1,0:T(8,128)(2,1)S(1)}, u32[]{:S(2)}, u32[]{:S(2)}) collective-permute-start(bf16[256,384]{1,0:T(8,128)(2,1)S(1)} %get-tuple-element.26), channel_id=1, source_target_pairs={{0,512},{16,528},{32,544},{48,560},{64,576},{80,592},{96,608},{112... | collective-permute-start | bytes 589832 | tf_op jit(solution)/shard_map/ppermute | solution.py:254
  100.9 2.8 %attention_backward.1 = (bf16[256,384]{1,0:T(8,128)(2,1)}, bf16[256,384]{1,0:T(8,128)(2,1)}, bf16[256,384]{1,0:T(8,128)(2,1)}) custom-call(bf16[256,384]{1,0:T(8,128)(2,1)S(1)} %copy-done.3, bf16[256,384]{1,0:T(8,128)(2,1)S(1)} %copy-done.5, bf16[256,384]{1,0:T(8,128)(2,1)S(1)} %copy-done.7, f32[256,384]{1,0:T(8,128)S(1)} %get-tuple-element.35.partial_ref, ...), custom_call_target="tpu_custom_call" | custom-call | flops 301989888 | bytes 1771520 | tf_op jit(solution)/shard_map/attention_backward/pallas_call | solution.py:43
  103.7 3.2 %collective-permute-done.13.other_ref = bf16[256,384]{1,0:T(8,128)(2,1)S(1)} collective-permute-done((bf16[256,384]{1,0:T(8,128)(2,1)S(1)}, bf16[256,384]{1,0:T(8,128)(2,1)S(1)}, u32[]{:S(2)}, u32[]{:S(2)}) %collective-permute-start.13) | collective-permute-done | bytes 196640 | tf_op jit(solution)/shard_map/ppermute | solution.py:254
  106.8 0.9 finish_projected.1
  (39 shorter events, 5.1 us)
Async XLA Ops:
  0.6 12.0 %collective-permute-start.1 = (bf16[256,384]{1,0:T(8,128)(2,1)}, bf16[256,384]{1,0:T(8,128)(2,1)S(1)}, u32[]{:S(2)}, u32[]{:S(2)}) collective-permute-start(bf16[256,384]{1,0:T(8,128)(2,1)} %own_ref.1), channel_id=1, source_target_pairs={{0,512},{16,528},{32,544},{48,560},{64,576},{80,592},{96,608},{112... | collective-permute-start | bytes 589832 | tf_op jit(solution)/shard_map/ppermute | solution.py:254
  5.6 0.9 copy-start.2
  6.5 0.9 copy-start.4
  7.4 0.9 copy-start.6
  8.4 0.8 copy-start.9
  10.2 20.8 %collective-permute-start = (bf16[256,384]{1,0:T(8,128)(2,1)S(1)}, bf16[256,384]{1,0:T(8,128)(2,1)S(1)}, u32[]{:S(2)}, u32[]{:S(2)}) collective-permute-start(bf16[256,384]{1,0:T(8,128)(2,1)S(1)} %get-tuple-element.15.own_ref), channel_id=1, source_target_pairs={{0,512},{16,528},{32,544},{48,560},{64,576},{80,592},{96,608},{112... | collective-permute-start | bytes 589832 | tf_op jit(solution)/shard_map/ppermute | solution.py:254
  12.7 0.9 copy-start.8
  13.9 24.6 %collective-permute-start.7 = (bf16[256,384]{1,0:T(8,128)(2,1)S(1)}, bf16[256,384]{1,0:T(8,128)(2,1)S(1)}, u32[]{:S(2)}, u32[]{:S(2)}) collective-permute-start(bf16[256,384]{1,0:T(8,128)(2,1)S(1)} %pack_out_grad.1.earlier_ref), channel_id=1, source_target_pairs={{0,1},{1,2},{2,3},{3,4},{4,5},{5,6},{6,7},{7,8},{8,9},{9,10},{10,1... | collective-permute-start | bytes 589832 | tf_op jit(solution)/shard_map/ppermute | solution.py:248
  18.2 22.6 %collective-permute-start.8 = (bf16[256,384]{1,0:T(8,128)(2,1)S(1)}, bf16[256,384]{1,0:T(8,128)(2,1)S(1)}, u32[]{:S(2)}, u32[]{:S(2)}) collective-permute-start(bf16[256,384]{1,0:T(8,128)(2,1)S(1)} %pack_out_grad.1.earlier_ref), channel_id=1, source_target_pairs={{0,5},{1,6},{2,7},{3,8},{4,9},{5,10},{6,11},{7,12},{8,13},{9,14},{... | collective-permute-start | bytes 589832 | tf_op jit(solution)/shard_map/ppermute | solution.py:251
  31.0 2.3 %copy-start = (bf16[384,6144]{1,0:T(8,128)(2,1)S(1)}, bf16[384,6144]{1,0:T(8,128)(2,1)}, u32[]{:S(2)}) copy-start(bf16[384,6144]{1,0:T(8,128)(2,1)} %weight_ref.7) | copy-start | bytes 14155780
  33.4 11.8 %copy-start.1 = (bf16[384,6144]{1,0:T(8,128)(2,1)S(1)}, bf16[384,6144]{1,0:T(8,128)(2,1)}, u32[]{:S(2)}) copy-start(bf16[384,6144]{1,0:T(8,128)(2,1)} %weight_ref.7) | copy-start | bytes 14155780
  33.9 15.9 %collective-permute-start.2 = (bf16[384,384]{1,0:T(8,128)(2,1)S(1)}, bf16[384,384]{1,0:T(8,128)(2,1)S(1)}, u32[]{:S(2)}, u32[]{:S(2)}) collective-permute-start(bf16[384,384]{1,0:T(8,128)(2,1)S(1)} %get-tuple-element.17.earlier_ref), channel_id=1, source_target_pairs={{0,1},{1,2},{2,3},{3,4},{4,5},{5,6},{6,7},{7,8},{8,9},{9,10},{10,1... | collective-permute-start | bytes 884744 | tf_op jit(solution)/shard_map/ppermute | solution.py:248
  40.9 19.9 %collective-permute-start.9 = (bf16[512,384]{1,0:T(8,128)(2,1)S(1)}, bf16[512,384]{1,0:T(8,128)(2,1)S(1)}, u32[]{:S(2)}, u32[]{:S(2)}) collective-permute-start(bf16[512,384]{1,0:T(8,128)(2,1)S(1)} %join_out_grad.1), channel_id=1, source_target_pairs={{0,1},{1,2},{2,3},{3,4},{4,5},{5,6},{6,7},{7,8},{8,9},{9,10},{10,1... | collective-permute-start | bytes 1179656 | tf_op jit(solution)/shard_map/ppermute | solution.py:248
  50.2 14.7 %collective-permute-start.3 = (bf16[512,384]{1,0:T(8,128)(2,1)S(1)}, bf16[512,384]{1,0:T(8,128)(2,1)S(1)}, u32[]{:S(2)}, u32[]{:S(2)}) collective-permute-start(bf16[512,384]{1,0:T(8,128)(2,1)S(1)} %add_terms.3), channel_id=1, source_target_pairs={{0,1},{1,2},{2,3},{3,4},{4,5},{5,6},{6,7},{7,8},{8,9},{9,10},{10,1... | collective-permute-start | bytes 1179656 | tf_op jit(solution)/shard_map/ppermute | solution.py:248
  60.7 10.9 %collective-permute-start.10 = (bf16[512,384]{1,0:T(8,128)(2,1)S(1)}, bf16[512,384]{1,0:T(8,128)(2,1)S(1)}, u32[]{:S(2)}, u32[]{:S(2)}) collective-permute-start(bf16[512,384]{1,0:T(8,128)(2,1)S(1)} %collective-permute-done.9), channel_id=1, source_target_pairs={{0,1},{1,2},{2,3},{3,4},{4,5},{5,6},{6,7},{7,8},{8,9},{9,10},{10,1... | collective-permute-start | bytes 1179656 | tf_op jit(solution)/shard_map/ppermute | solution.py:248
  65.3 10.9 %collective-permute-start.4 = (bf16[512,384]{1,0:T(8,128)(2,1)S(1)}, bf16[512,384]{1,0:T(8,128)(2,1)S(1)}, u32[]{:S(2)}, u32[]{:S(2)}) collective-permute-start(bf16[512,384]{1,0:T(8,128)(2,1)S(1)} %add_terms.4), channel_id=1, source_target_pairs={{0,1},{1,2},{2,3},{3,4},{4,5},{5,6},{6,7},{7,8},{8,9},{9,10},{10,1... | collective-permute-start | bytes 1179656 | tf_op jit(solution)/shard_map/ppermute | solution.py:248
  71.7 9.8 %collective-permute-start.11 = (bf16[384,384]{1,0:T(8,128)(2,1)S(1)}, bf16[384,384]{1,0:T(8,128)(2,1)S(1)}, u32[]{:S(2)}, u32[]{:S(2)}) collective-permute-start(bf16[384,384]{1,0:T(8,128)(2,1)S(1)} %pad_maximum_fusion), channel_id=1, source_target_pairs={{0,1},{1,2},{2,3},{3,4},{4,5},{5,6},{6,7},{7,8},{8,9},{9,10},{10,1... | collective-permute-start | bytes 884744 | tf_op jit(solution)/shard_map/ppermute | solution.py:248
  74.3 26.6 %copy-start.3 = (bf16[256,384]{1,0:T(8,128)(2,1)S(1)}, bf16[256,384]{1,0:T(8,128)(2,1)}, u32[]{:S(2)}) copy-start(bf16[256,384]{1,0:T(8,128)(2,1)} %query_ref.3) | copy-start | bytes 589828
  74.3 26.6 %copy-start.5 = (bf16[256,384]{1,0:T(8,128)(2,1)S(1)}, bf16[256,384]{1,0:T(8,128)(2,1)}, u32[]{:S(2)}) copy-start(bf16[256,384]{1,0:T(8,128)(2,1)} %key_ref.3) | copy-start | bytes 589828
  74.3 26.6 %copy-start.7 = (bf16[256,384]{1,0:T(8,128)(2,1)S(1)}, bf16[256,384]{1,0:T(8,128)(2,1)}, u32[]{:S(2)}) copy-start(bf16[256,384]{1,0:T(8,128)(2,1)} %value_ref.3) | copy-start | bytes 589828
  76.6 21.1 %collective-permute-start.6 = (bf16[256,384]{1,0:T(8,128)(2,1)S(1)}, bf16[256,384]{1,0:T(8,128)(2,1)S(1)}, u32[]{:S(2)}, u32[]{:S(2)}) collective-permute-start(bf16[256,384]{1,0:T(8,128)(2,1)S(1)} %get-tuple-element.20), channel_id=1, source_target_pairs={{0,5},{1,6},{2,7},{3,8},{4,9},{5,10},{6,11},{7,12},{8,13},{9,14},{... | collective-permute-start | bytes 589832 | tf_op jit(solution)/shard_map/ppermute | solution.py:251
  78.6 19.2 %collective-permute-start.5 = (bf16[256,384]{1,0:T(8,128)(2,1)S(1)}, bf16[256,384]{1,0:T(8,128)(2,1)S(1)}, u32[]{:S(2)}, u32[]{:S(2)}) collective-permute-start(bf16[256,384]{1,0:T(8,128)(2,1)S(1)} %get-tuple-element.19), channel_id=1, source_target_pairs={{0,1},{1,2},{2,3},{3,4},{4,5},{5,6},{6,7},{7,8},{8,9},{9,10},{10,1... | collective-permute-start | bytes 589832 | tf_op jit(solution)/shard_map/ppermute | solution.py:248
  82.4 15.3 %collective-permute-start.12 = (bf16[256,384]{1,0:T(8,128)(2,1)S(1)}, bf16[256,384]{1,0:T(8,128)(2,1)S(1)}, u32[]{:S(2)}, u32[]{:S(2)}) collective-permute-start(bf16[256,384]{1,0:T(8,128)(2,1)S(1)} %get-tuple-element.34), channel_id=1, source_target_pairs={{0,512},{16,528},{32,544},{48,560},{64,576},{80,592},{96,608},{112... | collective-permute-start | bytes 589832 | tf_op jit(solution)/shard_map/ppermute | solution.py:254
  97.8 9.1 %collective-permute-start.13 = (bf16[256,384]{1,0:T(8,128)(2,1)S(1)}, bf16[256,384]{1,0:T(8,128)(2,1)S(1)}, u32[]{:S(2)}, u32[]{:S(2)}) collective-permute-start(bf16[256,384]{1,0:T(8,128)(2,1)S(1)} %get-tuple-element.26), channel_id=1, source_target_pairs={{0,512},{16,528},{32,544},{48,560},{64,576},{80,592},{96,608},{112... | collective-permute-start | bytes 589832 | tf_op jit(solution)/shard_map/ppermute | solution.py:254

commit v5 on v4

--- a/solution.py
+++ b/solution.py
@@ -12,7 +12,7 @@
 SLOT = 128
 ROWS = 256
 VMEM_LIMIT = 20 * 1024 * 1024
-FRONT_LIMIT = 58 * 1024 * 1024
+FRONT_LIMIT = 54600 * 1024
 IN_VMEM = pl.BlockSpec(memory_space=pltpu.VMEM)
 
 
@@ -97,16 +97,7 @@
 
 
 def pack_terms_kernel(
-    dp_size,
-    mp_size,
-    distances,
-    own_ref,
-    other_ref,
-    starts_ref,
-    weight_ref,
-    earlier_ref,
-    out_ref,
-    terms_ref,
+    dp_size, own_ref, other_ref, starts_ref, held_ref, earlier_ref, out_ref, terms_ref
 ):
     del earlier_ref
     right = goes_right(lax.axis_index("dp"), dp_size)
@@ -114,11 +105,9 @@
     out_ref[:SLOT, :] = first
     out_ref[SLOT:, :] = second
     half = jnp.where(right, first, second)
-
-    near_weight, far_weight = weights_at(dp_size, mp_size, distances, weight_ref)
-    terms_ref[:SLOT, :] = dot(first, near_weight).astype(jnp.bfloat16)
-    terms_ref[SLOT:ROWS, :] = dot(second, near_weight).astype(jnp.bfloat16)
-    terms_ref[ROWS:, :] = dot(half, far_weight).astype(jnp.bfloat16)
+    terms_ref[:SLOT, :] = dot(first, held_ref[0]).astype(jnp.bfloat16)
+    terms_ref[SLOT:ROWS, :] = dot(second, held_ref[0]).astype(jnp.bfloat16)
+    terms_ref[ROWS:, :] = dot(half, held_ref[1]).astype(jnp.bfloat16)
 
 
 def weights_at(dp_size, mp_size, distances, weight_ref):
@@ -165,17 +154,56 @@
     return weights * (1.0 / jnp.sum(weights, axis=1, keepdims=True))
 
 
-def forward_kernel(dp_size, query_ref, key_ref, value_ref, starts_ref, out_ref, pair_starts_ref):
+def forward_kernel(
+    dp_size,
+    mp_size,
+    distances,
+    query_hbm,
+    key_hbm,
+    value_hbm,
+    out_grad_hbm,
+    weight_hbm,
+    starts_hbm,
+    out_ref,
+    out_grad_ref,
+    held_ref,
+    pair_starts_ref,
+    query_ref,
+    key_ref,
+    value_ref,
+    starts_ref,
+    sems,
+):
     width = query_ref.shape[1]
-    dp = lax.axis_index("dp")
+    dp, z = lax.axis_index("dp"), lax.axis_index("mp")
+    right = goes_right(dp, dp_size)
+    moves = [
+        (starts_hbm, starts_ref),
+        (query_hbm, query_ref),
+        (key_hbm, key_ref),
+        (value_hbm, value_ref),
+        (out_grad_hbm, out_grad_ref),
+    ]
+    for slot, distance in enumerate(distances):
+        index = lax.rem(z + jnp.where(right, distance, mp_size - distance), mp_size)
+        columns = pl.ds(pl.multiple_of(index * width, 128), width)
+        moves.append((weight_hbm.at[:, columns], held_ref.at[slot]))
+    copies = [pltpu.make_async_copy(*move, sems.at[at]) for at, move in enumerate(moves)]
+    for copy in copies:
+        copy.start()
+    copies[0].wait()
     own = starts_ref[pl.ds(dp, 1), :]
     pair_starts_ref[0:1, :] = own
     pair_starts_ref[1:2, :] = starts_ref[pl.ds(lax.rem(dp + dp_size // 2, dp_size), 1), :]
+    for copy in copies[1:4]:
+        copy.wait()
     same_image = as_column(own) == own
     for head in range(width // HEAD_DIM):
         at = slice(head * HEAD_DIM, (head + 1) * HEAD_DIM)
         rounded = probabilities_of(query_ref[:, at], key_ref[:, at], same_image).astype(jnp.bfloat16)
         out_ref[:, at] = dot(rounded, value_ref[:, at]).astype(jnp.bfloat16)
+    for copy in copies[4:]:
+        copy.wait()
 
 
 def unpacked(heavy, first, second):
@@ -265,22 +293,33 @@
 
     other_out_grad = swap(out_grad)
     in_any = pl.BlockSpec(memory_space=pl.ANY)
-    attended, starts = call(
-        functools.partial(forward_kernel, dp_size),
-        [rows_type, jax.ShapeDtypeStruct((2, ROWS), jnp.int32)],
-        (query_rows, key_rows, value_rows, image_starts),
+    in_hbm = pl.BlockSpec(memory_space=pltpu.HBM)
+    row_buffer = pltpu.VMEM((ROWS, width), jnp.bfloat16)
+    attended, own_out_grad, held, starts = call(
+        functools.partial(forward_kernel, dp_size, mp_size, (near, near + far - 1)),
+        [
+            rows_type,
+            rows_type,
+            jax.ShapeDtypeStruct((2, width, width), jnp.bfloat16),
+            jax.ShapeDtypeStruct((2, ROWS), jnp.int32),
+        ],
+        (query_rows, key_rows, value_rows, out_grad, proj_weight, image_starts),
+        specs=[in_hbm] * 6,
+        scratch=[row_buffer] * 3
+        + [pltpu.VMEM(image_starts.shape, jnp.int32), pltpu.SemaphoreType.DMA((7,))],
         flops=4 * ROWS * ROWS * width,
         name="attention_forward",
+        limit=FRONT_LIMIT,
     )
     other_attended = swap(attended)
     (pair_grad,) = call(
-        pack_kernel, [rows_type], (out_grad, other_out_grad, starts), name="pack_out_grad"
+        pack_kernel, [rows_type], (own_out_grad, other_out_grad, starts), name="pack_out_grad"
     )
     near_block, far_block = hop(pair_grad), jump(pair_grad)
     pair_attended, first_terms = call(
-        functools.partial(pack_terms_kernel, dp_size, mp_size, (near, near + far - 1)),
+        functools.partial(pack_terms_kernel, dp_size),
         [rows_type, half_type],
-        (attended, other_attended, starts, proj_weight, pair_grad),
+        (attended, other_attended, starts, held, pair_grad),
         specs=[IN_VMEM] * 4 + [in_any],
         name="pack_attended",
     )

time: 108 us -> 109 us (level)
  the two profiles are of different devices: /device:TPU:32 before, /device:TPU:36 now
where the time goes in v5:
time: 109 us; the launch traced here: 108 us
  starting transfers between devices  68.9 us (63%)
  waiting for transfers between devices  19.9 us (18%)
  Pallas kernels  8.89 us (8%)
  matrix products  4.73 us (4%)
  local copies, waits for them, and re-layouts  4.26 us (4%)
  between operations  1.11 us (1%)
    ppermute x8, starting transfers between devices, hop(): return lax.ppermute(rows, ('dp', 'mp'), hop_perm)  44.6 us
    ppermute x2, starting transfers between devices, jump(): return lax.ppermute(rows, ('dp', 'mp'), jump_perm)  13.1 us
    ppermute x4, starting transfers between devices, swap(): return lax.ppermute(rows, 'dp', swap_perm)  11.2 us
    ppermute x4, waiting for transfers between devices, swap(): return lax.ppermute(rows, 'dp', swap_perm)  11.2 us
    pallas_call x9, Pallas kernels, call(): pl.pallas_call(kernel, out_shape=outs, in_specs=specs or [IN_VMEM] * len(...  8.89 us
    ppermute x2, waiting for transfers between devices, jump(): return lax.ppermute(rows, ('dp', 'mp'), jump_perm)  5.34 us
    dot_general x10, matrix products, dot(): lax.dot_general(a, b, (((dims[0],), (dims[1],)), ((), ())), preferred_ele...  4.73 us
    unnamed x12, local copies, waits for them, and re-layouts  4.24 us
  transfers between devices with their start and end apart: 14, of which 6 were waited for; matrix products, arithmetic and copies ran while one was open for 4% of the time, Pallas kernels for 7%

profile of v5, /device:TPU:36, one launch (start us, length us, event | category | flops | bytes accessed | tf_op | source)
XLA Modules:
  0.0 107.9 jit_solution(1171327276824519787)
XLA Ops:
  0.6 2.4 %collective-permute-start.1 = (bf16[256,384]{1,0:T(8,128)(2,1)}, bf16[256,384]{1,0:T(8,128)(2,1)S(1)}, u32[]{:S(2)}, u32[]{:S(2)}) collective-permute-start(bf16[256,384]{1,0:T(8,128)(2,1)} %out_grad_hbm.1), channel_id=1, source_target_pairs={{0,512},{16,528},{32,544},{48,560},{64,576},{80,592},{96,608},{112... | collective-permute-start | bytes 589832 | tf_op jit(solution)/shard_map/ppermute | solution.py:282
  3.1 0.8 copy-done.5
  3.9 3.1 %attention_forward.1 = (bf16[256,384]{1,0:T(8,128)(2,1)S(1)}, bf16[256,384]{1,0:T(8,128)(2,1)S(1)}, bf16[2,384,384]{2,1,0:T(8,128)(2,1)}, s32[2,256]{1,0:T(2,128)S(1)}) custom-call(bf16[256,384]{1,0:T(8,128)(2,1)} %query_ref.1, bf16[256,384]{1,0:T(8,128)(2,1)} %key_ref.1, bf16[256,384]{1,0:T(8,128)(2,1)} %value_ref.1, bf16[256,384]{1,0:T(8,128)(2,1)} %out_grad_hbm.1, ...), custom_call_target="tpu_custom_call" | custom-call | flops 100663296 | bytes 6555648 | tf_op jit(solution)/shard_map/attention_forward/pallas_call | solution.py:43
  7.0 4.9 %collective-permute-start = (bf16[256,384]{1,0:T(8,128)(2,1)S(1)}, bf16[256,384]{1,0:T(8,128)(2,1)S(1)}, u32[]{:S(2)}, u32[]{:S(2)}) collective-permute-start(bf16[256,384]{1,0:T(8,128)(2,1)S(1)} %get-tuple-element.17.own_ref), channel_id=1, source_target_pairs={{0,512},{16,528},{32,544},{48,560},{64,576},{80,592},{96,608},{112... | collective-permute-start | bytes 589832 | tf_op jit(solution)/shard_map/ppermute | solution.py:282
  12.3 18.2 %collective-permute-start.7 = (bf16[256,384]{1,0:T(8,128)(2,1)S(1)}, bf16[256,384]{1,0:T(8,128)(2,1)S(1)}, u32[]{:S(2)}, u32[]{:S(2)}) collective-permute-start(bf16[256,384]{1,0:T(8,128)(2,1)S(1)} %pack_out_grad.1.earlier_ref), channel_id=1, source_target_pairs={{0,1},{1,2},{2,3},{3,4},{4,5},{5,6},{6,7},{7,8},{8,9},{9,10},{10,1... | collective-permute-start | bytes 589832 | tf_op jit(solution)/shard_map/ppermute | solution.py:276
  30.5 3.6 %collective-permute-start.8 = (bf16[256,384]{1,0:T(8,128)(2,1)S(1)}, bf16[256,384]{1,0:T(8,128)(2,1)S(1)}, u32[]{:S(2)}, u32[]{:S(2)}) collective-permute-start(bf16[256,384]{1,0:T(8,128)(2,1)S(1)} %pack_out_grad.1.earlier_ref), channel_id=1, source_target_pairs={{0,5},{1,6},{2,7},{3,8},{4,9},{5,10},{6,11},{7,12},{8,13},{9,14},{... | collective-permute-start | bytes 589832 | tf_op jit(solution)/shard_map/ppermute | solution.py:279
  34.2 1.1 copy-done.4
  35.3 0.6 pack_attended.1
  35.9 2.5 %collective-permute-start.2 = (bf16[384,384]{1,0:T(8,128)(2,1)S(1)}, bf16[384,384]{1,0:T(8,128)(2,1)S(1)}, u32[]{:S(2)}, u32[]{:S(2)}) collective-permute-start(bf16[384,384]{1,0:T(8,128)(2,1)S(1)} %get-tuple-element.21.earlier_ref), channel_id=1, source_target_pairs={{0,1},{1,2},{2,3},{3,4},{4,5},{5,6},{6,7},{7,8},{8,9},{9,10},{10,1... | collective-permute-start | bytes 884744 | tf_op jit(solution)/shard_map/ppermute | solution.py:276
  38.3 5.3 %collective-permute-done.8.far_ref = bf16[256,384]{1,0:T(8,128)(2,1)S(1)} collective-permute-done((bf16[256,384]{1,0:T(8,128)(2,1)S(1)}, bf16[256,384]{1,0:T(8,128)(2,1)S(1)}, u32[]{:S(2)}, u32[]{:S(2)}) %collective-permute-start.8) | collective-permute-done | bytes 196640 | tf_op jit(solution)/shard_map/ppermute | solution.py:279
  43.7 5.7 %collective-permute-start.9 = (bf16[512,384]{1,0:T(8,128)(2,1)S(1)}, bf16[512,384]{1,0:T(8,128)(2,1)S(1)}, u32[]{:S(2)}, u32[]{:S(2)}) collective-permute-start(bf16[512,384]{1,0:T(8,128)(2,1)S(1)} %join_out_grad.1), channel_id=1, source_target_pairs={{0,1},{1,2},{2,3},{3,4},{4,5},{5,6},{6,7},{7,8},{8,9},{9,10},{10,1... | collective-permute-start | bytes 1179656 | tf_op jit(solution)/shard_map/ppermute | solution.py:276
  49.4 1.2 %broadcast_select_fusion.5 = (f32[128,384]{1,0:T(8,128)S(1)}, f32[128,384]{1,0:T(8,128)S(1)}) fusion(pred[]{:T(512)S(6)} %eq.3, bf16[384,6144]{1,0:T(8,128)(2,1)} %weight_ref.5, s32[]{:T(128)S(6)} %select_n.76, bf16[256,384]{1,0:T(8,128)(2,1)S(1)} %pack_out_grad.1.earlier_ref), kind=kOutput, calls=%fused_computation.46 | convolution fusion | flops 37896192 | bytes 886272 | tf_op jit(solution)/shard_map/dot_general | solution.py:36
  50.6 1.3 %fusion.17 = f32[256,384]{1,0:T(8,128)S(1)} fusion(bf16[384,6144]{1,0:T(8,128)(2,1)} %weight_ref.5, s32[]{:T(128)S(6)} %select_n.81, bf16[512,384]{1,0:T(8,128)(2,1)S(1)} %join_out_grad.1), kind=kOutput, calls=%fused_computation.21 | convolution fusion | flops 75497472 | bytes 884740 | tf_op jit(solution)/shard_map/dot_general | solution.py:36
  51.9 2.3 %copy-done = bf16[384,6144]{1,0:T(8,128)(2,1)S(1)} copy-done((bf16[384,6144]{1,0:T(8,128)(2,1)S(1)}, bf16[384,6144]{1,0:T(8,128)(2,1)}, u32[]{:S(2)}) %copy-start) | copy-done | bytes 4718616
  54.2 0.4 add_terms.3
  54.6 2.8 %collective-permute-start.3 = (bf16[512,384]{1,0:T(8,128)(2,1)S(1)}, bf16[512,384]{1,0:T(8,128)(2,1)S(1)}, u32[]{:S(2)}, u32[]{:S(2)}) collective-permute-start(bf16[512,384]{1,0:T(8,128)(2,1)S(1)} %add_terms.3), channel_id=1, source_target_pairs={{0,1},{1,2},{2,3},{3,4},{4,5},{5,6},{6,7},{7,8},{8,9},{9,10},{10,1... | collective-permute-start | bytes 1179656 | tf_op jit(solution)/shard_map/ppermute | solution.py:276
  57.4 4.9 %collective-permute-start.10 = (bf16[512,384]{1,0:T(8,128)(2,1)S(1)}, bf16[512,384]{1,0:T(8,128)(2,1)S(1)}, u32[]{:S(2)}, u32[]{:S(2)}) collective-permute-start(bf16[512,384]{1,0:T(8,128)(2,1)S(1)} %collective-permute-done.9), channel_id=1, source_target_pairs={{0,1},{1,2},{2,3},{3,4},{4,5},{5,6},{6,7},{7,8},{8,9},{9,10},{10,1... | collective-permute-start | bytes 1179656 | tf_op jit(solution)/shard_map/ppermute | solution.py:276
  62.9 1.4 %collective-permute-done.3.sums_ref = bf16[512,384]{1,0:T(8,128)(2,1)S(1)} collective-permute-done((bf16[512,384]{1,0:T(8,128)(2,1)S(1)}, bf16[512,384]{1,0:T(8,128)(2,1)S(1)}, u32[]{:S(2)}, u32[]{:S(2)}) %collective-permute-start.3) | collective-permute-done | bytes 393248 | tf_op jit(solution)/shard_map/ppermute | solution.py:276
  64.3 0.4 add_terms.4
  64.7 4.1 %collective-permute-start.4 = (bf16[512,384]{1,0:T(8,128)(2,1)S(1)}, bf16[512,384]{1,0:T(8,128)(2,1)S(1)}, u32[]{:S(2)}, u32[]{:S(2)}) collective-permute-start(bf16[512,384]{1,0:T(8,128)(2,1)S(1)} %add_terms.4), channel_id=1, source_target_pairs={{0,1},{1,2},{2,3},{3,4},{4,5},{5,6},{6,7},{7,8},{8,9},{9,10},{10,1... | collective-permute-start | bytes 1179656 | tf_op jit(solution)/shard_map/ppermute | solution.py:276
  68.9 4.6 %collective-permute-start.11 = (bf16[384,384]{1,0:T(8,128)(2,1)S(1)}, bf16[384,384]{1,0:T(8,128)(2,1)S(1)}, u32[]{:S(2)}, u32[]{:S(2)}) collective-permute-start(bf16[384,384]{1,0:T(8,128)(2,1)S(1)} %pad_maximum_fusion), channel_id=1, source_target_pairs={{0,1},{1,2},{2,3},{3,4},{4,5},{5,6},{6,7},{7,8},{8,9},{9,10},{10,1... | collective-permute-start | bytes 884744 | tf_op jit(solution)/shard_map/ppermute | solution.py:276
  74.4 0.4 add_terms.5
  74.8 9.5 %collective-permute-start.6 = (bf16[256,384]{1,0:T(8,128)(2,1)S(1)}, bf16[256,384]{1,0:T(8,128)(2,1)S(1)}, u32[]{:S(2)}, u32[]{:S(2)}) collective-permute-start(bf16[256,384]{1,0:T(8,128)(2,1)S(1)} %get-tuple-element.24), channel_id=1, source_target_pairs={{0,5},{1,6},{2,7},{3,8},{4,9},{5,10},{6,11},{7,12},{8,13},{9,14},{... | collective-permute-start | bytes 589832 | tf_op jit(solution)/shard_map/ppermute | solution.py:279
  84.2 1.9 %collective-permute-start.5 = (bf16[256,384]{1,0:T(8,128)(2,1)S(1)}, bf16[256,384]{1,0:T(8,128)(2,1)S(1)}, u32[]{:S(2)}, u32[]{:S(2)}) collective-permute-start(bf16[256,384]{1,0:T(8,128)(2,1)S(1)} %get-tuple-element.23), channel_id=1, source_target_pairs={{0,1},{1,2},{2,3},{3,4},{4,5},{5,6},{6,7},{7,8},{8,9},{9,10},{10,1... | collective-permute-start | bytes 589832 | tf_op jit(solution)/shard_map/ppermute | solution.py:276
  86.7 0.3 fusion.49
  87.0 1.9 %collective-permute-start.12 = (bf16[256,384]{1,0:T(8,128)(2,1)S(1)}, bf16[256,384]{1,0:T(8,128)(2,1)S(1)}, u32[]{:S(2)}, u32[]{:S(2)}) collective-permute-start(bf16[256,384]{1,0:T(8,128)(2,1)S(1)} %get-tuple-element.38), channel_id=1, source_target_pairs={{0,512},{16,528},{32,544},{48,560},{64,576},{80,592},{96,608},{112... | collective-permute-start | bytes 589832 | tf_op jit(solution)/shard_map/ppermute | solution.py:282
  89.2 6.9 %collective-permute-done.12.other_ref = bf16[256,384]{1,0:T(8,128)(2,1)S(1)} collective-permute-done((bf16[256,384]{1,0:T(8,128)(2,1)S(1)}, bf16[256,384]{1,0:T(8,128)(2,1)S(1)}, u32[]{:S(2)}, u32[]{:S(2)}) %collective-permute-start.12) | collective-permute-done | bytes 196640 | tf_op jit(solution)/shard_map/ppermute | solution.py:282
  96.1 1.8 %collective-permute-done.5 = bf16[256,384]{1,0:T(8,128)(2,1)S(1)} collective-permute-done((bf16[256,384]{1,0:T(8,128)(2,1)S(1)}, bf16[256,384]{1,0:T(8,128)(2,1)S(1)}, u32[]{:S(2)}, u32[]{:S(2)}) %collective-permute-start.5) | collective-permute-done | bytes 196640 | tf_op jit(solution)/shard_map/ppermute | solution.py:276
  98.0 1.9 %collective-permute-start.13 = (bf16[256,384]{1,0:T(8,128)(2,1)S(1)}, bf16[256,384]{1,0:T(8,128)(2,1)S(1)}, u32[]{:S(2)}, u32[]{:S(2)}) collective-permute-start(bf16[256,384]{1,0:T(8,128)(2,1)S(1)} %get-tuple-element.30), channel_id=1, source_target_pairs={{0,512},{16,528},{32,544},{48,560},{64,576},{80,592},{96,608},{112... | collective-permute-start | bytes 589832 | tf_op jit(solution)/shard_map/ppermute | solution.py:282
  100.0 2.8 %attention_backward.1 = (bf16[256,384]{1,0:T(8,128)(2,1)}, bf16[256,384]{1,0:T(8,128)(2,1)}, bf16[256,384]{1,0:T(8,128)(2,1)}) custom-call(bf16[256,384]{1,0:T(8,128)(2,1)S(1)} %copy-done.1, bf16[256,384]{1,0:T(8,128)(2,1)S(1)} %copy-done.2, bf16[256,384]{1,0:T(8,128)(2,1)S(1)} %copy-done.3, f32[256,384]{1,0:T(8,128)S(1)} %get-tuple-element.39.partial_ref, ...), custom_call_target="tpu_custom_call" | custom-call | flops 301989888 | bytes 1771520 | tf_op jit(solution)/shard_map/attention_backward/pallas_call | solution.py:43
  102.8 4.3 %collective-permute-done.13.other_ref = bf16[256,384]{1,0:T(8,128)(2,1)S(1)} collective-permute-done((bf16[256,384]{1,0:T(8,128)(2,1)S(1)}, bf16[256,384]{1,0:T(8,128)(2,1)S(1)}, u32[]{:S(2)}, u32[]{:S(2)}) %collective-permute-start.13) | collective-permute-done | bytes 196640 | tf_op jit(solution)/shard_map/ppermute | solution.py:282
  107.1 0.9 finish_projected.1
  (31 shorter events, 2.7 us)
Async XLA Ops:
  0.6 11.3 %collective-permute-start.1 = (bf16[256,384]{1,0:T(8,128)(2,1)}, bf16[256,384]{1,0:T(8,128)(2,1)S(1)}, u32[]{:S(2)}, u32[]{:S(2)}) collective-permute-start(bf16[256,384]{1,0:T(8,128)(2,1)} %out_grad_hbm.1), channel_id=1, source_target_pairs={{0,512},{16,528},{32,544},{48,560},{64,576},{80,592},{96,608},{112... | collective-permute-start | bytes 589832 | tf_op jit(solution)/shard_map/ppermute | solution.py:282
  3.1 0.8 copy-start.5
  7.0 27.2 %collective-permute-start = (bf16[256,384]{1,0:T(8,128)(2,1)S(1)}, bf16[256,384]{1,0:T(8,128)(2,1)S(1)}, u32[]{:S(2)}, u32[]{:S(2)}) collective-permute-start(bf16[256,384]{1,0:T(8,128)(2,1)S(1)} %get-tuple-element.17.own_ref), channel_id=1, source_target_pairs={{0,512},{16,528},{32,544},{48,560},{64,576},{80,592},{96,608},{112... | collective-permute-start | bytes 589832 | tf_op jit(solution)/shard_map/ppermute | solution.py:282
  12.3 26.1 %collective-permute-start.7 = (bf16[256,384]{1,0:T(8,128)(2,1)S(1)}, bf16[256,384]{1,0:T(8,128)(2,1)S(1)}, u32[]{:S(2)}, u32[]{:S(2)}) collective-permute-start(bf16[256,384]{1,0:T(8,128)(2,1)S(1)} %pack_out_grad.1.earlier_ref), channel_id=1, source_target_pairs={{0,1},{1,2},{2,3},{3,4},{4,5},{5,6},{6,7},{7,8},{8,9},{9,10},{10,1... | collective-permute-start | bytes 589832 | tf_op jit(solution)/shard_map/ppermute | solution.py:276
  30.5 13.2 %collective-permute-start.8 = (bf16[256,384]{1,0:T(8,128)(2,1)S(1)}, bf16[256,384]{1,0:T(8,128)(2,1)S(1)}, u32[]{:S(2)}, u32[]{:S(2)}) collective-permute-start(bf16[256,384]{1,0:T(8,128)(2,1)S(1)} %pack_out_grad.1.earlier_ref), channel_id=1, source_target_pairs={{0,5},{1,6},{2,7},{3,8},{4,9},{5,10},{6,11},{7,12},{8,13},{9,14},{... | collective-permute-start | bytes 589832 | tf_op jit(solution)/shard_map/ppermute | solution.py:279
  34.2 1.1 copy-start.4
  35.9 16.0 %collective-permute-start.2 = (bf16[384,384]{1,0:T(8,128)(2,1)S(1)}, bf16[384,384]{1,0:T(8,128)(2,1)S(1)}, u32[]{:S(2)}, u32[]{:S(2)}) collective-permute-start(bf16[384,384]{1,0:T(8,128)(2,1)S(1)} %get-tuple-element.21.earlier_ref), channel_id=1, source_target_pairs={{0,1},{1,2},{2,3},{3,4},{4,5},{5,6},{6,7},{7,8},{8,9},{9,10},{10,1... | collective-permute-start | bytes 884744 | tf_op jit(solution)/shard_map/ppermute | solution.py:276
  43.7 13.7 %collective-permute-start.9 = (bf16[512,384]{1,0:T(8,128)(2,1)S(1)}, bf16[512,384]{1,0:T(8,128)(2,1)S(1)}, u32[]{:S(2)}, u32[]{:S(2)}) collective-permute-start(bf16[512,384]{1,0:T(8,128)(2,1)S(1)} %join_out_grad.1), channel_id=1, source_target_pairs={{0,1},{1,2},{2,3},{3,4},{4,5},{5,6},{6,7},{7,8},{8,9},{9,10},{10,1... | collective-permute-start | bytes 1179656 | tf_op jit(solution)/shard_map/ppermute | solution.py:276
  51.9 2.3 %copy-start = (bf16[384,6144]{1,0:T(8,128)(2,1)S(1)}, bf16[384,6144]{1,0:T(8,128)(2,1)}, u32[]{:S(2)}) copy-start(bf16[384,6144]{1,0:T(8,128)(2,1)} %weight_ref.5) | copy-start | bytes 14155780
  54.6 9.7 %collective-permute-start.3 = (bf16[512,384]{1,0:T(8,128)(2,1)S(1)}, bf16[512,384]{1,0:T(8,128)(2,1)S(1)}, u32[]{:S(2)}, u32[]{:S(2)}) collective-permute-start(bf16[512,384]{1,0:T(8,128)(2,1)S(1)} %add_terms.3), channel_id=1, source_target_pairs={{0,1},{1,2},{2,3},{3,4},{4,5},{5,6},{6,7},{7,8},{8,9},{9,10},{10,1... | collective-permute-start | bytes 1179656 | tf_op jit(solution)/shard_map/ppermute | solution.py:276
  57.4 11.3 %collective-permute-start.10 = (bf16[512,384]{1,0:T(8,128)(2,1)S(1)}, bf16[512,384]{1,0:T(8,128)(2,1)S(1)}, u32[]{:S(2)}, u32[]{:S(2)}) collective-permute-start(bf16[512,384]{1,0:T(8,128)(2,1)S(1)} %collective-permute-done.9), channel_id=1, source_target_pairs={{0,1},{1,2},{2,3},{3,4},{4,5},{5,6},{6,7},{7,8},{8,9},{9,10},{10,1... | collective-permute-start | bytes 1179656 | tf_op jit(solution)/shard_map/ppermute | solution.py:276
  64.7 9.7 %collective-permute-start.4 = (bf16[512,384]{1,0:T(8,128)(2,1)S(1)}, bf16[512,384]{1,0:T(8,128)(2,1)S(1)}, u32[]{:S(2)}, u32[]{:S(2)}) collective-permute-start(bf16[512,384]{1,0:T(8,128)(2,1)S(1)} %add_terms.4), channel_id=1, source_target_pairs={{0,1},{1,2},{2,3},{3,4},{4,5},{5,6},{6,7},{7,8},{8,9},{9,10},{10,1... | collective-permute-start | bytes 1179656 | tf_op jit(solution)/shard_map/ppermute | solution.py:276
  68.9 17.3 %collective-permute-start.11 = (bf16[384,384]{1,0:T(8,128)(2,1)S(1)}, bf16[384,384]{1,0:T(8,128)(2,1)S(1)}, u32[]{:S(2)}, u32[]{:S(2)}) collective-permute-start(bf16[384,384]{1,0:T(8,128)(2,1)S(1)} %pad_maximum_fusion), channel_id=1, source_target_pairs={{0,1},{1,2},{2,3},{3,4},{4,5},{5,6},{6,7},{7,8},{8,9},{9,10},{10,1... | collective-permute-start | bytes 884744 | tf_op jit(solution)/shard_map/ppermute | solution.py:276
  74.1 25.8 %copy-start.1 = (bf16[256,384]{1,0:T(8,128)(2,1)S(1)}, bf16[256,384]{1,0:T(8,128)(2,1)}, u32[]{:S(2)}) copy-start(bf16[256,384]{1,0:T(8,128)(2,1)} %query_ref.1) | copy-start | bytes 589828
  74.1 25.8 %copy-start.2 = (bf16[256,384]{1,0:T(8,128)(2,1)S(1)}, bf16[256,384]{1,0:T(8,128)(2,1)}, u32[]{:S(2)}) copy-start(bf16[256,384]{1,0:T(8,128)(2,1)} %key_ref.1) | copy-start | bytes 589828
  74.1 25.8 %copy-start.3 = (bf16[256,384]{1,0:T(8,128)(2,1)S(1)}, bf16[256,384]{1,0:T(8,128)(2,1)}, u32[]{:S(2)}) copy-start(bf16[256,384]{1,0:T(8,128)(2,1)} %value_ref.1) | copy-start | bytes 589828
  74.8 14.4 %collective-permute-start.6 = (bf16[256,384]{1,0:T(8,128)(2,1)S(1)}, bf16[256,384]{1,0:T(8,128)(2,1)S(1)}, u32[]{:S(2)}, u32[]{:S(2)}) collective-permute-start(bf16[256,384]{1,0:T(8,128)(2,1)S(1)} %get-tuple-element.24), channel_id=1, source_target_pairs={{0,5},{1,6},{2,7},{3,8},{4,9},{5,10},{6,11},{7,12},{8,13},{9,14},{... | collective-permute-start | bytes 589832 | tf_op jit(solution)/shard_map/ppermute | solution.py:279
  84.2 13.7 %collective-permute-start.5 = (bf16[256,384]{1,0:T(8,128)(2,1)S(1)}, bf16[256,384]{1,0:T(8,128)(2,1)S(1)}, u32[]{:S(2)}, u32[]{:S(2)}) collective-permute-start(bf16[256,384]{1,0:T(8,128)(2,1)S(1)} %get-tuple-element.23), channel_id=1, source_target_pairs={{0,1},{1,2},{2,3},{3,4},{4,5},{5,6},{6,7},{7,8},{8,9},{9,10},{10,1... | collective-permute-start | bytes 589832 | tf_op jit(solution)/shard_map/ppermute | solution.py:276
  87.0 9.1 %collective-permute-start.12 = (bf16[256,384]{1,0:T(8,128)(2,1)S(1)}, bf16[256,384]{1,0:T(8,128)(2,1)S(1)}, u32[]{:S(2)}, u32[]{:S(2)}) collective-permute-start(bf16[256,384]{1,0:T(8,128)(2,1)S(1)} %get-tuple-element.38), channel_id=1, source_target_pairs={{0,512},{16,528},{32,544},{48,560},{64,576},{80,592},{96,608},{112... | collective-permute-start | bytes 589832 | tf_op jit(solution)/shard_map/ppermute | solution.py:282
  98.0 9.1 %collective-permute-start.13 = (bf16[256,384]{1,0:T(8,128)(2,1)S(1)}, bf16[256,384]{1,0:T(8,128)(2,1)S(1)}, u32[]{:S(2)}, u32[]{:S(2)}) collective-permute-start(bf16[256,384]{1,0:T(8,128)(2,1)S(1)} %get-tuple-element.30), channel_id=1, source_target_pairs={{0,512},{16,528},{32,544},{48,560},{64,576},{80,592},{96,608},{112... | collective-permute-start | bytes 589832 | tf_op jit(solution)/shard_map/ppermute | solution.py:282

commit v6 on v5

--- a/solution.py
+++ b/solution.py
@@ -97,7 +97,16 @@
 
 
 def pack_terms_kernel(
-    dp_size, own_ref, other_ref, starts_ref, held_ref, earlier_ref, out_ref, terms_ref
+    dp_size,
+    mp_size,
+    distances,
+    own_ref,
+    other_ref,
+    starts_ref,
+    weight_ref,
+    earlier_ref,
+    out_ref,
+    terms_ref,
 ):
     del earlier_ref
     right = goes_right(lax.axis_index("dp"), dp_size)
@@ -105,9 +114,10 @@
     out_ref[:SLOT, :] = first
     out_ref[SLOT:, :] = second
     half = jnp.where(right, first, second)
-    terms_ref[:SLOT, :] = dot(first, held_ref[0]).astype(jnp.bfloat16)
-    terms_ref[SLOT:ROWS, :] = dot(second, held_ref[0]).astype(jnp.bfloat16)
-    terms_ref[ROWS:, :] = dot(half, held_ref[1]).astype(jnp.bfloat16)
+    near_weight, far_weight = weights_at(dp_size, mp_size, distances, weight_ref)
+    terms_ref[:SLOT, :] = dot(first, near_weight).astype(jnp.bfloat16)
+    terms_ref[SLOT:ROWS, :] = dot(second, near_weight).astype(jnp.bfloat16)
+    terms_ref[ROWS:, :] = dot(half, far_weight).astype(jnp.bfloat16)
 
 
 def weights_at(dp_size, mp_size, distances, weight_ref):
@@ -156,17 +166,13 @@
 
 def forward_kernel(
     dp_size,
-    mp_size,
-    distances,
     query_hbm,
     key_hbm,
     value_hbm,
     out_grad_hbm,
-    weight_hbm,
     starts_hbm,
     out_ref,
     out_grad_ref,
-    held_ref,
     pair_starts_ref,
     query_ref,
     key_ref,
@@ -175,8 +181,7 @@
     sems,
 ):
     width = query_ref.shape[1]
-    dp, z = lax.axis_index("dp"), lax.axis_index("mp")
-    right = goes_right(dp, dp_size)
+    dp = lax.axis_index("dp")
     moves = [
         (starts_hbm, starts_ref),
         (query_hbm, query_ref),
@@ -184,10 +189,6 @@
         (value_hbm, value_ref),
         (out_grad_hbm, out_grad_ref),
     ]
-    for slot, distance in enumerate(distances):
-        index = lax.rem(z + jnp.where(right, distance, mp_size - distance), mp_size)
-        columns = pl.ds(pl.multiple_of(index * width, 128), width)
-        moves.append((weight_hbm.at[:, columns], held_ref.at[slot]))
     copies = [pltpu.make_async_copy(*move, sems.at[at]) for at, move in enumerate(moves)]
     for copy in copies:
         copy.start()
@@ -295,18 +296,17 @@
     in_any = pl.BlockSpec(memory_space=pl.ANY)
     in_hbm = pl.BlockSpec(memory_space=pltpu.HBM)
     row_buffer = pltpu.VMEM((ROWS, width), jnp.bfloat16)
-    attended, own_out_grad, held, starts = call(
-        functools.partial(forward_kernel, dp_size, mp_size, (near, near + far - 1)),
+    attended, own_out_grad, starts = call(
+        functools.partial(forward_kernel, dp_size),
         [
             rows_type,
             rows_type,
-            jax.ShapeDtypeStruct((2, width, width), jnp.bfloat16),
             jax.ShapeDtypeStruct((2, ROWS), jnp.int32),
         ],
-        (query_rows, key_rows, value_rows, out_grad, proj_weight, image_starts),
-        specs=[in_hbm] * 6,
+        (query_rows, key_rows, value_rows, out_grad, image_starts),
+        specs=[in_hbm] * 5,
         scratch=[row_buffer] * 3
-        + [pltpu.VMEM(image_starts.shape, jnp.int32), pltpu.SemaphoreType.DMA((7,))],
+        + [pltpu.VMEM(image_starts.shape, jnp.int32), pltpu.SemaphoreType.DMA((5,))],
         flops=4 * ROWS * ROWS * width,
         name="attention_forward",
         limit=FRONT_LIMIT,
@@ -317,9 +317,9 @@
     )
     near_block, far_block = hop(pair_grad), jump(pair_grad)
     pair_attended, first_terms = call(
-        functools.partial(pack_terms_kernel, dp_size),
+        functools.partial(pack_terms_kernel, dp_size, mp_size, (near, near + far - 1)),
         [rows_type, half_type],
-        (attended, other_attended, starts, held, pair_grad),
+        (attended, other_attended, starts, proj_weight, pair_grad),
         specs=[IN_VMEM] * 4 + [in_any],
         name="pack_attended",
     )

time: 109 us -> 106 us (0.972)
  the two profiles are of different devices: /device:TPU:36 before, /device:TPU:42 now
where the time goes in v6:
time: 106 us; the launch traced here: 105 us
  starting transfers between devices  55.9 us (53%)
  waiting for transfers between devices  34.1 us (32%)
  Pallas kernels  8 us (8%)
  local copies, waits for them, and re-layouts  3.21 us (3%)
  matrix products  2.85 us (3%)
  between operations  1.07 us (1%)
    ppermute x8, starting transfers between devices, hop(): return lax.ppermute(rows, ('dp', 'mp'), hop_perm)  24.5 us
    ppermute x8, waiting for transfers between devices, hop(): return lax.ppermute(rows, ('dp', 'mp'), hop_perm)  19.8 us
    ppermute x4, starting transfers between devices, swap(): return lax.ppermute(rows, 'dp', swap_perm)  16.8 us
    ppermute x2, starting transfers between devices, jump(): return lax.ppermute(rows, ('dp', 'mp'), jump_perm)  14.6 us
    ppermute x2, waiting for transfers between devices, jump(): return lax.ppermute(rows, ('dp', 'mp'), jump_perm)  10.1 us
    pallas_call x9, Pallas kernels, call(): pl.pallas_call(kernel, out_shape=outs, in_specs=specs or [IN_VMEM] * len(...  8 us
    ppermute x4, waiting for transfers between devices, swap(): return lax.ppermute(rows, 'dp', swap_perm)  4.1 us
    unnamed x12, local copies, waits for them, and re-layouts  3.19 us
  transfers between devices with their start and end apart: 14, of which 9 were waited for; matrix products, arithmetic and copies ran while one was open for 3% of the time, Pallas kernels for 7%

profile of v6, /device:TPU:42, one launch (start us, length us, event | category | flops | bytes accessed | tf_op | source)
XLA Modules:
  0.0 105.2 jit_solution(8578050161412317591)
XLA Ops:
  0.6 4.0 %collective-permute-start.1 = (bf16[256,384]{1,0:T(8,128)(2,1)}, bf16[256,384]{1,0:T(8,128)(2,1)S(1)}, u32[]{:S(2)}, u32[]{:S(2)}) collective-permute-start(bf16[256,384]{1,0:T(8,128)(2,1)} %out_grad_hbm.1), channel_id=1, source_target_pairs={{0,512},{16,528},{32,544},{48,560},{64,576},{80,592},{96,608},{112... | collective-permute-start | bytes 589832 | tf_op jit(solution)/shard_map/ppermute | solution.py:283
  4.7 0.8 copy-done.5
  5.5 2.2 %attention_forward.1 = (bf16[256,384]{1,0:T(8,128)(2,1)S(1)}, bf16[256,384]{1,0:T(8,128)(2,1)S(1)}, s32[2,256]{1,0:T(2,128)S(1)}) custom-call(bf16[256,384]{1,0:T(8,128)(2,1)} %query_ref.1, bf16[256,384]{1,0:T(8,128)(2,1)} %key_ref.1, bf16[256,384]{1,0:T(8,128)(2,1)} %value_ref.1, bf16[256,384]{1,0:T(8,128)(2,1)} %out_grad_hbm.1, s32[64,256]{1,0:T(8,128)S(1)} %copy-done.5), custom_call_target="tpu_custom_call" | custom-call | flops 100663296 | bytes 1247232 | tf_op jit(solution)/shard_map/attention_forward/pallas_call | solution.py:43
  7.8 3.3 %collective-permute-start = (bf16[256,384]{1,0:T(8,128)(2,1)S(1)}, bf16[256,384]{1,0:T(8,128)(2,1)S(1)}, u32[]{:S(2)}, u32[]{:S(2)}) collective-permute-start(bf16[256,384]{1,0:T(8,128)(2,1)S(1)} %get-tuple-element.16.own_ref), channel_id=1, source_target_pairs={{0,512},{16,528},{32,544},{48,560},{64,576},{80,592},{96,608},{112... | collective-permute-start | bytes 589832 | tf_op jit(solution)/shard_map/ppermute | solution.py:283
  11.4 4.3 %collective-permute-start.7 = (bf16[256,384]{1,0:T(8,128)(2,1)S(1)}, bf16[256,384]{1,0:T(8,128)(2,1)S(1)}, u32[]{:S(2)}, u32[]{:S(2)}) collective-permute-start(bf16[256,384]{1,0:T(8,128)(2,1)S(1)} %pack_out_grad.1.earlier_ref), channel_id=1, source_target_pairs={{0,1},{1,2},{2,3},{3,4},{4,5},{5,6},{6,7},{7,8},{8,9},{9,10},{10,1... | collective-permute-start | bytes 589832 | tf_op jit(solution)/shard_map/ppermute | solution.py:277
  15.7 12.7 %collective-permute-start.8 = (bf16[256,384]{1,0:T(8,128)(2,1)S(1)}, bf16[256,384]{1,0:T(8,128)(2,1)S(1)}, u32[]{:S(2)}, u32[]{:S(2)}) collective-permute-start(bf16[256,384]{1,0:T(8,128)(2,1)S(1)} %pack_out_grad.1.earlier_ref), channel_id=1, source_target_pairs={{0,5},{1,6},{2,7},{3,8},{4,9},{5,10},{6,11},{7,12},{8,13},{9,14},{... | collective-permute-start | bytes 589832 | tf_op jit(solution)/shard_map/ppermute | solution.py:280
  28.5 2.3 %copy-done = bf16[384,6144]{1,0:T(8,128)(2,1)S(1)} copy-done((bf16[384,6144]{1,0:T(8,128)(2,1)S(1)}, bf16[384,6144]{1,0:T(8,128)(2,1)}, u32[]{:S(2)}) %copy-start) | copy-done | bytes 4718616
  30.9 0.6 pack_attended.1
  31.4 4.5 %collective-permute-start.2 = (bf16[384,384]{1,0:T(8,128)(2,1)S(1)}, bf16[384,384]{1,0:T(8,128)(2,1)S(1)}, u32[]{:S(2)}, u32[]{:S(2)}) collective-permute-start(bf16[384,384]{1,0:T(8,128)(2,1)S(1)} %get-tuple-element.19.earlier_ref), channel_id=1, source_target_pairs={{0,1},{1,2},{2,3},{3,4},{4,5},{5,6},{6,7},{7,8},{8,9},{9,10},{10,1... | collective-permute-start | bytes 884744 | tf_op jit(solution)/shard_map/ppermute | solution.py:277
  36.0 2.3 %collective-permute-done.8.far_ref = bf16[256,384]{1,0:T(8,128)(2,1)S(1)} collective-permute-done((bf16[256,384]{1,0:T(8,128)(2,1)S(1)}, bf16[256,384]{1,0:T(8,128)(2,1)S(1)}, u32[]{:S(2)}, u32[]{:S(2)}) %collective-permute-start.8) | collective-permute-done | bytes 196640 | tf_op jit(solution)/shard_map/ppermute | solution.py:280
  38.4 4.3 %collective-permute-start.9 = (bf16[512,384]{1,0:T(8,128)(2,1)S(1)}, bf16[512,384]{1,0:T(8,128)(2,1)S(1)}, u32[]{:S(2)}, u32[]{:S(2)}) collective-permute-start(bf16[512,384]{1,0:T(8,128)(2,1)S(1)} %join_out_grad.1), channel_id=1, source_target_pairs={{0,1},{1,2},{2,3},{3,4},{4,5},{5,6},{6,7},{7,8},{8,9},{9,10},{10,1... | collective-permute-start | bytes 1179656 | tf_op jit(solution)/shard_map/ppermute | solution.py:277
  43.3 4.1 %collective-permute-done.2.sums_ref = bf16[384,384]{1,0:T(8,128)(2,1)S(1)} collective-permute-done((bf16[384,384]{1,0:T(8,128)(2,1)S(1)}, bf16[384,384]{1,0:T(8,128)(2,1)S(1)}, u32[]{:S(2)}, u32[]{:S(2)}) %collective-permute-start.2) | collective-permute-done | bytes 294944 | tf_op jit(solution)/shard_map/ppermute | solution.py:277
  47.4 0.4 add_terms.3
  47.8 3.2 %collective-permute-start.3 = (bf16[512,384]{1,0:T(8,128)(2,1)S(1)}, bf16[512,384]{1,0:T(8,128)(2,1)S(1)}, u32[]{:S(2)}, u32[]{:S(2)}) collective-permute-start(bf16[512,384]{1,0:T(8,128)(2,1)S(1)} %add_terms.3), channel_id=1, source_target_pairs={{0,1},{1,2},{2,3},{3,4},{4,5},{5,6},{6,7},{7,8},{8,9},{9,10},{10,1... | collective-permute-start | bytes 1179656 | tf_op jit(solution)/shard_map/ppermute | solution.py:277
  51.0 7.3 %collective-permute-done.9 = bf16[512,384]{1,0:T(8,128)(2,1)S(1)} collective-permute-done((bf16[512,384]{1,0:T(8,128)(2,1)S(1)}, bf16[512,384]{1,0:T(8,128)(2,1)S(1)}, u32[]{:S(2)}, u32[]{:S(2)}) %collective-permute-start.9) | collective-permute-done | bytes 393248 | tf_op jit(solution)/shard_map/ppermute | solution.py:277
  58.2 1.9 %collective-permute-start.10 = (bf16[512,384]{1,0:T(8,128)(2,1)S(1)}, bf16[512,384]{1,0:T(8,128)(2,1)S(1)}, u32[]{:S(2)}, u32[]{:S(2)}) collective-permute-start(bf16[512,384]{1,0:T(8,128)(2,1)S(1)} %collective-permute-done.9), channel_id=1, source_target_pairs={{0,1},{1,2},{2,3},{3,4},{4,5},{5,6},{6,7},{7,8},{8,9},{9,10},{10,1... | collective-permute-start | bytes 1179656 | tf_op jit(solution)/shard_map/ppermute | solution.py:277
  60.8 1.7 %collective-permute-done.3.sums_ref = bf16[512,384]{1,0:T(8,128)(2,1)S(1)} collective-permute-done((bf16[512,384]{1,0:T(8,128)(2,1)S(1)}, bf16[512,384]{1,0:T(8,128)(2,1)S(1)}, u32[]{:S(2)}, u32[]{:S(2)}) %collective-permute-start.3) | collective-permute-done | bytes 393248 | tf_op jit(solution)/shard_map/ppermute | solution.py:277
  62.4 0.4 add_terms.4
  62.8 1.9 %collective-permute-start.4 = (bf16[512,384]{1,0:T(8,128)(2,1)S(1)}, bf16[512,384]{1,0:T(8,128)(2,1)S(1)}, u32[]{:S(2)}, u32[]{:S(2)}) collective-permute-start(bf16[512,384]{1,0:T(8,128)(2,1)S(1)} %add_terms.4), channel_id=1, source_target_pairs={{0,1},{1,2},{2,3},{3,4},{4,5},{5,6},{6,7},{7,8},{8,9},{9,10},{10,1... | collective-permute-start | bytes 1179656 | tf_op jit(solution)/shard_map/ppermute | solution.py:277
  64.8 4.3 %collective-permute-done.10 = bf16[512,384]{1,0:T(8,128)(2,1)S(1)} collective-permute-done((bf16[512,384]{1,0:T(8,128)(2,1)S(1)}, bf16[512,384]{1,0:T(8,128)(2,1)S(1)}, u32[]{:S(2)}, u32[]{:S(2)}) %collective-permute-start.10) | collective-permute-done | bytes 393248 | tf_op jit(solution)/shard_map/ppermute | solution.py:277
  69.2 1.9 %collective-permute-start.11 = (bf16[384,384]{1,0:T(8,128)(2,1)S(1)}, bf16[384,384]{1,0:T(8,128)(2,1)S(1)}, u32[]{:S(2)}, u32[]{:S(2)}) collective-permute-start(bf16[384,384]{1,0:T(8,128)(2,1)S(1)} %pad_maximum_fusion), channel_id=1, source_target_pairs={{0,1},{1,2},{2,3},{3,4},{4,5},{5,6},{6,7},{7,8},{8,9},{9,10},{10,1... | collective-permute-start | bytes 884744 | tf_op jit(solution)/shard_map/ppermute | solution.py:277
  71.8 1.9 %collective-permute-done.4.sums_ref = bf16[512,384]{1,0:T(8,128)(2,1)S(1)} collective-permute-done((bf16[512,384]{1,0:T(8,128)(2,1)S(1)}, bf16[512,384]{1,0:T(8,128)(2,1)S(1)}, u32[]{:S(2)}, u32[]{:S(2)}) %collective-permute-start.4) | collective-permute-done | bytes 393248 | tf_op jit(solution)/shard_map/ppermute | solution.py:277
  73.7 0.4 add_terms.5
  74.1 1.9 %collective-permute-start.6 = (bf16[256,384]{1,0:T(8,128)(2,1)S(1)}, bf16[256,384]{1,0:T(8,128)(2,1)S(1)}, u32[]{:S(2)}, u32[]{:S(2)}) collective-permute-start(bf16[256,384]{1,0:T(8,128)(2,1)S(1)} %get-tuple-element.22), channel_id=1, source_target_pairs={{0,5},{1,6},{2,7},{3,8},{4,9},{5,10},{6,11},{7,12},{8,13},{9,14},{... | collective-permute-start | bytes 589832 | tf_op jit(solution)/shard_map/ppermute | solution.py:280
  76.1 2.4 %collective-permute-start.5 = (bf16[256,384]{1,0:T(8,128)(2,1)S(1)}, bf16[256,384]{1,0:T(8,128)(2,1)S(1)}, u32[]{:S(2)}, u32[]{:S(2)}) collective-permute-start(bf16[256,384]{1,0:T(8,128)(2,1)S(1)} %get-tuple-element.21), channel_id=1, source_target_pairs={{0,1},{1,2},{2,3},{3,4},{4,5},{5,6},{6,7},{7,8},{8,9},{9,10},{10,1... | collective-permute-start | bytes 589832 | tf_op jit(solution)/shard_map/ppermute | solution.py:277
  78.5 0.5 collective-permute-done.11
  79.9 7.3 %collective-permute-start.12 = (bf16[256,384]{1,0:T(8,128)(2,1)S(1)}, bf16[256,384]{1,0:T(8,128)(2,1)S(1)}, u32[]{:S(2)}, u32[]{:S(2)}) collective-permute-start(bf16[256,384]{1,0:T(8,128)(2,1)S(1)} %get-tuple-element.36), channel_id=1, source_target_pairs={{0,512},{16,528},{32,544},{48,560},{64,576},{80,592},{96,608},{112... | collective-permute-start | bytes 589832 | tf_op jit(solution)/shard_map/ppermute | solution.py:283
  87.4 7.8 %collective-permute-done.6 = bf16[256,384]{1,0:T(8,128)(2,1)S(1)} collective-permute-done((bf16[256,384]{1,0:T(8,128)(2,1)S(1)}, bf16[256,384]{1,0:T(8,128)(2,1)S(1)}, u32[]{:S(2)}, u32[]{:S(2)}) %collective-permute-start.6) | collective-permute-done | bytes 196640 | tf_op jit(solution)/shard_map/ppermute | solution.py:280
  95.3 2.1 %collective-permute-start.13 = (bf16[256,384]{1,0:T(8,128)(2,1)S(1)}, bf16[256,384]{1,0:T(8,128)(2,1)S(1)}, u32[]{:S(2)}, u32[]{:S(2)}) collective-permute-start(bf16[256,384]{1,0:T(8,128)(2,1)S(1)} %get-tuple-element.28), channel_id=1, source_target_pairs={{0,512},{16,528},{32,544},{48,560},{64,576},{80,592},{96,608},{112... | collective-permute-start | bytes 589832 | tf_op jit(solution)/shard_map/ppermute | solution.py:283
  97.4 2.8 %attention_backward.1 = (bf16[256,384]{1,0:T(8,128)(2,1)}, bf16[256,384]{1,0:T(8,128)(2,1)}, bf16[256,384]{1,0:T(8,128)(2,1)}) custom-call(bf16[256,384]{1,0:T(8,128)(2,1)S(1)} %copy-done.2, bf16[256,384]{1,0:T(8,128)(2,1)S(1)} %copy-done.3, bf16[256,384]{1,0:T(8,128)(2,1)S(1)} %copy-done.4, f32[256,384]{1,0:T(8,128)S(1)} %get-tuple-element.37.partial_ref, ...), custom_call_target="tpu_custom_call" | custom-call | flops 301989888 | bytes 1771520 | tf_op jit(solution)/shard_map/attention_backward/pallas_call | solution.py:43
  100.3 4.1 %collective-permute-done.13.other_ref = bf16[256,384]{1,0:T(8,128)(2,1)S(1)} collective-permute-done((bf16[256,384]{1,0:T(8,128)(2,1)S(1)}, bf16[256,384]{1,0:T(8,128)(2,1)S(1)}, u32[]{:S(2)}, u32[]{:S(2)}) %collective-permute-start.13) | collective-permute-done | bytes 196640 | tf_op jit(solution)/shard_map/ppermute | solution.py:283
  104.3 0.9 finish_projected.1
  (31 shorter events, 3.4 us)
Async XLA Ops:
  0.6 10.4 %collective-permute-start.1 = (bf16[256,384]{1,0:T(8,128)(2,1)}, bf16[256,384]{1,0:T(8,128)(2,1)S(1)}, u32[]{:S(2)}, u32[]{:S(2)}) collective-permute-start(bf16[256,384]{1,0:T(8,128)(2,1)} %out_grad_hbm.1), channel_id=1, source_target_pairs={{0,512},{16,528},{32,544},{48,560},{64,576},{80,592},{96,608},{112... | collective-permute-start | bytes 589832 | tf_op jit(solution)/shard_map/ppermute | solution.py:283
  4.7 0.8 copy-start.5
  7.8 20.7 %collective-permute-start = (bf16[256,384]{1,0:T(8,128)(2,1)S(1)}, bf16[256,384]{1,0:T(8,128)(2,1)S(1)}, u32[]{:S(2)}, u32[]{:S(2)}) collective-permute-start(bf16[256,384]{1,0:T(8,128)(2,1)S(1)} %get-tuple-element.16.own_ref), channel_id=1, source_target_pairs={{0,512},{16,528},{32,544},{48,560},{64,576},{80,592},{96,608},{112... | collective-permute-start | bytes 589832 | tf_op jit(solution)/shard_map/ppermute | solution.py:283
  11.4 24.6 %collective-permute-start.7 = (bf16[256,384]{1,0:T(8,128)(2,1)S(1)}, bf16[256,384]{1,0:T(8,128)(2,1)S(1)}, u32[]{:S(2)}, u32[]{:S(2)}) collective-permute-start(bf16[256,384]{1,0:T(8,128)(2,1)S(1)} %pack_out_grad.1.earlier_ref), channel_id=1, source_target_pairs={{0,1},{1,2},{2,3},{3,4},{4,5},{5,6},{6,7},{7,8},{8,9},{9,10},{10,1... | collective-permute-start | bytes 589832 | tf_op jit(solution)/shard_map/ppermute | solution.py:277
  15.7 22.6 %collective-permute-start.8 = (bf16[256,384]{1,0:T(8,128)(2,1)S(1)}, bf16[256,384]{1,0:T(8,128)(2,1)S(1)}, u32[]{:S(2)}, u32[]{:S(2)}) collective-permute-start(bf16[256,384]{1,0:T(8,128)(2,1)S(1)} %pack_out_grad.1.earlier_ref), channel_id=1, source_target_pairs={{0,5},{1,6},{2,7},{3,8},{4,9},{5,10},{6,11},{7,12},{8,13},{9,14},{... | collective-permute-start | bytes 589832 | tf_op jit(solution)/shard_map/ppermute | solution.py:280
  28.5 2.3 %copy-start = (bf16[384,6144]{1,0:T(8,128)(2,1)S(1)}, bf16[384,6144]{1,0:T(8,128)(2,1)}, u32[]{:S(2)}) copy-start(bf16[384,6144]{1,0:T(8,128)(2,1)} %weight_ref.7) | copy-start | bytes 14155780
  30.8 11.9 %copy-start.1 = (bf16[384,6144]{1,0:T(8,128)(2,1)S(1)}, bf16[384,6144]{1,0:T(8,128)(2,1)}, u32[]{:S(2)}) copy-start(bf16[384,6144]{1,0:T(8,128)(2,1)} %weight_ref.7) | copy-start | bytes 14155780
  31.4 16.0 %collective-permute-start.2 = (bf16[384,384]{1,0:T(8,128)(2,1)S(1)}, bf16[384,384]{1,0:T(8,128)(2,1)S(1)}, u32[]{:S(2)}, u32[]{:S(2)}) collective-permute-start(bf16[384,384]{1,0:T(8,128)(2,1)S(1)} %get-tuple-element.19.earlier_ref), channel_id=1, source_target_pairs={{0,1},{1,2},{2,3},{3,4},{4,5},{5,6},{6,7},{7,8},{8,9},{9,10},{10,1... | collective-permute-start | bytes 884744 | tf_op jit(solution)/shard_map/ppermute | solution.py:277
  38.4 19.9 %collective-permute-start.9 = (bf16[512,384]{1,0:T(8,128)(2,1)S(1)}, bf16[512,384]{1,0:T(8,128)(2,1)S(1)}, u32[]{:S(2)}, u32[]{:S(2)}) collective-permute-start(bf16[512,384]{1,0:T(8,128)(2,1)S(1)} %join_out_grad.1), channel_id=1, source_target_pairs={{0,1},{1,2},{2,3},{3,4},{4,5},{5,6},{6,7},{7,8},{8,9},{9,10},{10,1... | collective-permute-start | bytes 1179656 | tf_op jit(solution)/shard_map/ppermute | solution.py:277
  47.8 14.7 %collective-permute-start.3 = (bf16[512,384]{1,0:T(8,128)(2,1)S(1)}, bf16[512,384]{1,0:T(8,128)(2,1)S(1)}, u32[]{:S(2)}, u32[]{:S(2)}) collective-permute-start(bf16[512,384]{1,0:T(8,128)(2,1)S(1)} %add_terms.3), channel_id=1, source_target_pairs={{0,1},{1,2},{2,3},{3,4},{4,5},{5,6},{6,7},{7,8},{8,9},{9,10},{10,1... | collective-permute-start | bytes 1179656 | tf_op jit(solution)/shard_map/ppermute | solution.py:277
  58.2 10.9 %collective-permute-start.10 = (bf16[512,384]{1,0:T(8,128)(2,1)S(1)}, bf16[512,384]{1,0:T(8,128)(2,1)S(1)}, u32[]{:S(2)}, u32[]{:S(2)}) collective-permute-start(bf16[512,384]{1,0:T(8,128)(2,1)S(1)} %collective-permute-done.9), channel_id=1, source_target_pairs={{0,1},{1,2},{2,3},{3,4},{4,5},{5,6},{6,7},{7,8},{8,9},{9,10},{10,1... | collective-permute-start | bytes 1179656 | tf_op jit(solution)/shard_map/ppermute | solution.py:277
  62.8 10.9 %collective-permute-start.4 = (bf16[512,384]{1,0:T(8,128)(2,1)S(1)}, bf16[512,384]{1,0:T(8,128)(2,1)S(1)}, u32[]{:S(2)}, u32[]{:S(2)}) collective-permute-start(bf16[512,384]{1,0:T(8,128)(2,1)S(1)} %add_terms.4), channel_id=1, source_target_pairs={{0,1},{1,2},{2,3},{3,4},{4,5},{5,6},{6,7},{7,8},{8,9},{9,10},{10,1... | collective-permute-start | bytes 1179656 | tf_op jit(solution)/shard_map/ppermute | solution.py:277
  69.2 9.8 %collective-permute-start.11 = (bf16[384,384]{1,0:T(8,128)(2,1)S(1)}, bf16[384,384]{1,0:T(8,128)(2,1)S(1)}, u32[]{:S(2)}, u32[]{:S(2)}) collective-permute-start(bf16[384,384]{1,0:T(8,128)(2,1)S(1)} %pad_maximum_fusion), channel_id=1, source_target_pairs={{0,1},{1,2},{2,3},{3,4},{4,5},{5,6},{6,7},{7,8},{8,9},{9,10},{10,1... | collective-permute-start | bytes 884744 | tf_op jit(solution)/shard_map/ppermute | solution.py:277
  71.8 25.6 %copy-start.2 = (bf16[256,384]{1,0:T(8,128)(2,1)S(1)}, bf16[256,384]{1,0:T(8,128)(2,1)}, u32[]{:S(2)}) copy-start(bf16[256,384]{1,0:T(8,128)(2,1)} %query_ref.1) | copy-start | bytes 589828
  71.8 25.6 %copy-start.3 = (bf16[256,384]{1,0:T(8,128)(2,1)S(1)}, bf16[256,384]{1,0:T(8,128)(2,1)}, u32[]{:S(2)}) copy-start(bf16[256,384]{1,0:T(8,128)(2,1)} %key_ref.1) | copy-start | bytes 589828
  71.8 25.6 %copy-start.4 = (bf16[256,384]{1,0:T(8,128)(2,1)S(1)}, bf16[256,384]{1,0:T(8,128)(2,1)}, u32[]{:S(2)}) copy-start(bf16[256,384]{1,0:T(8,128)(2,1)} %value_ref.1) | copy-start | bytes 589828
  74.1 21.1 %collective-permute-start.6 = (bf16[256,384]{1,0:T(8,128)(2,1)S(1)}, bf16[256,384]{1,0:T(8,128)(2,1)S(1)}, u32[]{:S(2)}, u32[]{:S(2)}) collective-permute-start(bf16[256,384]{1,0:T(8,128)(2,1)S(1)} %get-tuple-element.22), channel_id=1, source_target_pairs={{0,5},{1,6},{2,7},{3,8},{4,9},{5,10},{6,11},{7,12},{8,13},{9,14},{... | collective-permute-start | bytes 589832 | tf_op jit(solution)/shard_map/ppermute | solution.py:280
  76.1 19.2 %collective-permute-start.5 = (bf16[256,384]{1,0:T(8,128)(2,1)S(1)}, bf16[256,384]{1,0:T(8,128)(2,1)S(1)}, u32[]{:S(2)}, u32[]{:S(2)}) collective-permute-start(bf16[256,384]{1,0:T(8,128)(2,1)S(1)} %get-tuple-element.21), channel_id=1, source_target_pairs={{0,1},{1,2},{2,3},{3,4},{4,5},{5,6},{6,7},{7,8},{8,9},{9,10},{10,1... | collective-permute-start | bytes 589832 | tf_op jit(solution)/shard_map/ppermute | solution.py:277
  79.9 15.3 %collective-permute-start.12 = (bf16[256,384]{1,0:T(8,128)(2,1)S(1)}, bf16[256,384]{1,0:T(8,128)(2,1)S(1)}, u32[]{:S(2)}, u32[]{:S(2)}) collective-permute-start(bf16[256,384]{1,0:T(8,128)(2,1)S(1)} %get-tuple-element.36), channel_id=1, source_target_pairs={{0,512},{16,528},{32,544},{48,560},{64,576},{80,592},{96,608},{112... | collective-permute-start | bytes 589832 | tf_op jit(solution)/shard_map/ppermute | solution.py:283
  95.3 9.1 %collective-permute-start.13 = (bf16[256,384]{1,0:T(8,128)(2,1)S(1)}, bf16[256,384]{1,0:T(8,128)(2,1)S(1)}, u32[]{:S(2)}, u32[]{:S(2)}) collective-permute-start(bf16[256,384]{1,0:T(8,128)(2,1)S(1)} %get-tuple-element.28), channel_id=1, source_target_pairs={{0,512},{16,528},{32,544},{48,560},{64,576},{80,592},{96,608},{112... | collective-permute-start | bytes 589832 | tf_op jit(solution)/shard_map/ppermute | solution.py:283

commit v7 on v6

--- a/solution.py
+++ b/solution.py
@@ -149,6 +149,27 @@
     else:
         out_refs[0][:ROWS, :] = near_sum.astype(jnp.bfloat16)
         out_refs[0][ROWS:, :] = far_sum.astype(jnp.bfloat16)
+
+
+def total_kernel(
+    dp_size,
+    mp_size,
+    near_ref,
+    last_ref,
+    rows_ref,
+    weight_ref,
+    earlier_ref,
+    total_ref,
+    sent_ref,
+):
+    del earlier_ref
+    right = goes_right(lax.axis_index("dp"), dp_size)
+    (weight,) = weights_at(dp_size, mp_size, (0,), weight_ref)
+    own = dot(jnp.where(right, rows_ref[:SLOT, :], rows_ref[SLOT:, :]), weight)
+    total = near_ref[...].astype(jnp.float32) + last_ref[...].astype(jnp.float32)
+    total_ref[:SLOT, :] = total[:SLOT] + jnp.where(right, own, 0.0)
+    total_ref[SLOT:, :] = total[SLOT:] + jnp.where(right, 0.0, own)
+    sent_ref[...] = total_ref[...].astype(jnp.bfloat16)
 
 
 def join_kernel(near_ref, far_ref, earlier_ref, out_ref):
@@ -267,6 +288,7 @@
     dp, z = lax.axis_index("dp"), lax.axis_index("mp")
     hop_perm = ring_pairs(dp_size, mp_size, 1)
     jump_perm = ring_pairs(dp_size, mp_size, far)
+    gather_perm = ring_pairs(dp_size, mp_size, near)
     swap_perm = [(i, (i + dp_size // 2) % dp_size) for i in range(dp_size)]
     right = goes_right(dp, dp_size)
     delta = jnp.where(right, 1, mp_size - 1)
@@ -315,7 +337,8 @@
     (pair_grad,) = call(
         pack_kernel, [rows_type], (own_out_grad, other_out_grad, starts), name="pack_out_grad"
     )
-    near_block, far_block = hop(pair_grad), jump(pair_grad)
+    near_block = hop(pair_grad)
+    far_block = lax.ppermute(pair_grad, ("dp", "mp"), gather_perm)
     pair_attended, first_terms = call(
         functools.partial(pack_terms_kernel, dp_size, mp_size, (near, near + far - 1)),
         [rows_type, half_type],
@@ -355,20 +378,23 @@
     partial = place_half(product(half_of(pair_grad), 0))
     for step in range(1, near):
         near_block, far_block = moved[:ROWS], moved[ROWS:]
-        partial = partial + product(near_block, step) + product(far_block, far + step - 1)
-        if step == near - 1:
-            moved = jnp.concatenate([near_block, half_of(far_block)], 0)
-        moved = hop(moved)
-    near_block, far_block = moved[:ROWS], moved[ROWS:]
-    partial = partial + product(near_block, near) + place_half(product(far_block, near + far - 1))
+        partial = partial + product(near_block, step) + product(far_block, near + step - 1)
+        if step < near - 1:
+            moved = hop(moved)
+    far_block = hop(far_block)
+    partial = partial + product(far_block, 2 * near - 1)
+    far_block = hop(half_of(far_block))
+    partial = partial + place_half(product(far_block, 2 * near))
     other_partial = swap(partial.astype(jnp.bfloat16))
-    last_sum, other_partial = lax.optimization_barrier((last_sum, other_partial))
-    total = (
-        near_sum.astype(jnp.float32)
-        + last_sum.astype(jnp.float32)
-        + place_half(dot(half_of(pair_attended), block_of(proj_weight, z)))
-    )
-    other_total = swap(total.astype(jnp.bfloat16))
+    total, sent = call(
+        functools.partial(total_kernel, dp_size, mp_size),
+        [jax.ShapeDtypeStruct((ROWS, width), jnp.float32), rows_type],
+        (near_sum, last_sum, pair_attended, proj_weight, partial),
+        specs=[IN_VMEM] * 4 + [in_any],
+        flops=2 * SLOT * width * width,
+        name="total",
+    )
+    other_total = swap(sent)
     grads = call(
         backward_kernel,
         [rows_type] * 3,

time: 106 us -> 108 us (1.019)
  the two profiles are of different devices: /device:TPU:42 before, /device:TPU:40 now
where the time goes in v7:
time: 108 us
  starting transfers between devices  67.1 us (62%)
  waiting for transfers between devices  25.6 us (24%)
  Pallas kernels  8.26 us (8%)
  local copies, waits for them, and re-layouts  3.21 us (3%)
  matrix products  2.59 us (2%)
    ppermute x9, starting transfers between devices, hop(): return lax.ppermute(rows, ('dp', 'mp'), hop_perm)  34.9 us
    ppermute x9, waiting for transfers between devices, hop(): return lax.ppermute(rows, ('dp', 'mp'), hop_perm)  18.4 us
    ppermute x4, starting transfers between devices, swap(): return lax.ppermute(rows, 'dp', swap_perm)  16.7 us
    ppermute x1, starting transfers between devices, shards(): far_block = lax.ppermute(pair_grad, ('dp', 'mp'), gather_perm)  10.9 us
    pallas_call x10, Pallas kernels, call(): pl.pallas_call(kernel, out_shape=outs, in_specs=specs or [IN_VMEM] * len(...  8.26 us
    ppermute x1, starting transfers between devices, jump(): return lax.ppermute(rows, ('dp', 'mp'), jump_perm)  4.6 us
    ppermute x4, waiting for transfers between devices, swap(): return lax.ppermute(rows, 'dp', swap_perm)  4.3 us
    unnamed x12, local copies, waits for them, and re-layouts  3.19 us
  transfers between devices with their start and end apart: 15, of which 9 were waited for; matrix products, arithmetic and copies ran while one was open for 2% of the time, Pallas kernels for 7%

profile of v7, /device:TPU:40, one launch (start us, length us, event | category | flops | bytes accessed | tf_op | source)
XLA Modules:
  0.0 107.9 jit_solution(7747886919956364843)
XLA Ops:
  0.6 4.9 %collective-permute-start.1 = (bf16[256,384]{1,0:T(8,128)(2,1)}, bf16[256,384]{1,0:T(8,128)(2,1)S(1)}, u32[]{:S(2)}, u32[]{:S(2)}) collective-permute-start(bf16[256,384]{1,0:T(8,128)(2,1)} %out_grad_hbm.1), channel_id=1, source_target_pairs={{0,512},{16,528},{32,544},{48,560},{64,576},{80,592},{96,608},{112... | collective-permute-start | bytes 589832 | tf_op jit(solution)/shard_map/ppermute | solution.py:305
  5.6 0.8 copy-done.5
  6.4 2.2 %attention_forward.1 = (bf16[256,384]{1,0:T(8,128)(2,1)S(1)}, bf16[256,384]{1,0:T(8,128)(2,1)S(1)}, s32[2,256]{1,0:T(2,128)S(1)}) custom-call(bf16[256,384]{1,0:T(8,128)(2,1)} %query_ref.1, bf16[256,384]{1,0:T(8,128)(2,1)} %key_ref.1, bf16[256,384]{1,0:T(8,128)(2,1)} %value_ref.1, bf16[256,384]{1,0:T(8,128)(2,1)} %out_grad_hbm.1, s32[64,256]{1,0:T(8,128)S(1)} %copy-done.5), custom_call_target="tpu_custom_call" | custom-call | flops 100663296 | bytes 1247232 | tf_op jit(solution)/shard_map/attention_forward/pallas_call | solution.py:43
  8.7 2.4 %collective-permute-start = (bf16[256,384]{1,0:T(8,128)(2,1)S(1)}, bf16[256,384]{1,0:T(8,128)(2,1)S(1)}, u32[]{:S(2)}, u32[]{:S(2)}) collective-permute-start(bf16[256,384]{1,0:T(8,128)(2,1)S(1)} %get-tuple-element.16.own_ref), channel_id=1, source_target_pairs={{0,512},{16,528},{32,544},{48,560},{64,576},{80,592},{96,608},{112... | collective-permute-start | bytes 589832 | tf_op jit(solution)/shard_map/ppermute | solution.py:305
  11.4 4.3 %collective-permute-start.7 = (bf16[256,384]{1,0:T(8,128)(2,1)S(1)}, bf16[256,384]{1,0:T(8,128)(2,1)S(1)}, u32[]{:S(2)}, u32[]{:S(2)}) collective-permute-start(bf16[256,384]{1,0:T(8,128)(2,1)S(1)} %pack_out_grad.1.earlier_ref), channel_id=1, source_target_pairs={{0,1},{1,2},{2,3},{3,4},{4,5},{5,6},{6,7},{7,8},{8,9},{9,10},{10,1... | collective-permute-start | bytes 589832 | tf_op jit(solution)/shard_map/ppermute | solution.py:299
  15.7 10.9 %collective-permute-start.8 = (bf16[256,384]{1,0:T(8,128)(2,1)S(1)}, bf16[256,384]{1,0:T(8,128)(2,1)S(1)}, u32[]{:S(2)}, u32[]{:S(2)}) collective-permute-start(bf16[256,384]{1,0:T(8,128)(2,1)S(1)} %pack_out_grad.1.earlier_ref), channel_id=1, source_target_pairs={{0,4},{1,5},{2,6},{3,7},{4,8},{5,9},{6,10},{7,11},{8,12},{9,13},{1... | collective-permute-start | bytes 589832 | tf_op jit(solution)/shard_map/ppermute | solution.py:341
  26.7 2.3 %copy-done = bf16[384,6144]{1,0:T(8,128)(2,1)S(1)} copy-done((bf16[384,6144]{1,0:T(8,128)(2,1)S(1)}, bf16[384,6144]{1,0:T(8,128)(2,1)}, u32[]{:S(2)}) %copy-start) | copy-done | bytes 4718616
  29.0 0.6 pack_attended.1
  29.6 4.5 %collective-permute-start.2 = (bf16[384,384]{1,0:T(8,128)(2,1)S(1)}, bf16[384,384]{1,0:T(8,128)(2,1)S(1)}, u32[]{:S(2)}, u32[]{:S(2)}) collective-permute-start(bf16[384,384]{1,0:T(8,128)(2,1)S(1)} %get-tuple-element.19.earlier_ref), channel_id=1, source_target_pairs={{0,1},{1,2},{2,3},{3,4},{4,5},{5,6},{6,7},{7,8},{8,9},{9,10},{10,1... | collective-permute-start | bytes 884744 | tf_op jit(solution)/shard_map/ppermute | solution.py:299
  34.2 2.9 %collective-permute-done.8.far_ref = bf16[256,384]{1,0:T(8,128)(2,1)S(1)} collective-permute-done((bf16[256,384]{1,0:T(8,128)(2,1)S(1)}, bf16[256,384]{1,0:T(8,128)(2,1)S(1)}, u32[]{:S(2)}, u32[]{:S(2)}) %collective-permute-start.8) | collective-permute-done | bytes 196640 | tf_op jit(solution)/shard_map/ppermute | solution.py:341
  37.1 7.0 %collective-permute-start.9 = (bf16[512,384]{1,0:T(8,128)(2,1)S(1)}, bf16[512,384]{1,0:T(8,128)(2,1)S(1)}, u32[]{:S(2)}, u32[]{:S(2)}) collective-permute-start(bf16[512,384]{1,0:T(8,128)(2,1)S(1)} %join_out_grad.1), channel_id=1, source_target_pairs={{0,1},{1,2},{2,3},{3,4},{4,5},{5,6},{6,7},{7,8},{8,9},{9,10},{10,1... | collective-permute-start | bytes 1179656 | tf_op jit(solution)/shard_map/ppermute | solution.py:299
  44.6 1.1 %collective-permute-done.2.sums_ref = bf16[384,384]{1,0:T(8,128)(2,1)S(1)} collective-permute-done((bf16[384,384]{1,0:T(8,128)(2,1)S(1)}, bf16[384,384]{1,0:T(8,128)(2,1)S(1)}, u32[]{:S(2)}, u32[]{:S(2)}) %collective-permute-start.2) | collective-permute-done | bytes 294944 | tf_op jit(solution)/shard_map/ppermute | solution.py:299
  45.7 0.4 add_terms.3
  46.1 4.4 %collective-permute-start.3 = (bf16[512,384]{1,0:T(8,128)(2,1)S(1)}, bf16[512,384]{1,0:T(8,128)(2,1)S(1)}, u32[]{:S(2)}, u32[]{:S(2)}) collective-permute-start(bf16[512,384]{1,0:T(8,128)(2,1)S(1)} %add_terms.3), channel_id=1, source_target_pairs={{0,1},{1,2},{2,3},{3,4},{4,5},{5,6},{6,7},{7,8},{8,9},{9,10},{10,1... | collective-permute-start | bytes 1179656 | tf_op jit(solution)/shard_map/ppermute | solution.py:299
  50.6 1.6 %collective-permute-done.9 = bf16[512,384]{1,0:T(8,128)(2,1)S(1)} collective-permute-done((bf16[512,384]{1,0:T(8,128)(2,1)S(1)}, bf16[512,384]{1,0:T(8,128)(2,1)S(1)}, u32[]{:S(2)}, u32[]{:S(2)}) %collective-permute-start.9) | collective-permute-done | bytes 393248 | tf_op jit(solution)/shard_map/ppermute | solution.py:299
  52.2 2.6 %collective-permute-start.10 = (bf16[512,384]{1,0:T(8,128)(2,1)S(1)}, bf16[512,384]{1,0:T(8,128)(2,1)S(1)}, u32[]{:S(2)}, u32[]{:S(2)}) collective-permute-start(bf16[512,384]{1,0:T(8,128)(2,1)S(1)} %collective-permute-done.9), channel_id=1, source_target_pairs={{0,1},{1,2},{2,3},{3,4},{4,5},{5,6},{6,7},{7,8},{8,9},{9,10},{10,1... | collective-permute-start | bytes 1179656 | tf_op jit(solution)/shard_map/ppermute | solution.py:299
  55.5 1.6 %collective-permute-done.3.sums_ref = bf16[512,384]{1,0:T(8,128)(2,1)S(1)} collective-permute-done((bf16[512,384]{1,0:T(8,128)(2,1)S(1)}, bf16[512,384]{1,0:T(8,128)(2,1)S(1)}, u32[]{:S(2)}, u32[]{:S(2)}) %collective-permute-start.3) | collective-permute-done | bytes 393248 | tf_op jit(solution)/shard_map/ppermute | solution.py:299
  57.4 3.2 %collective-permute-start.4 = (bf16[512,384]{1,0:T(8,128)(2,1)S(1)}, bf16[512,384]{1,0:T(8,128)(2,1)S(1)}, u32[]{:S(2)}, u32[]{:S(2)}) collective-permute-start(bf16[512,384]{1,0:T(8,128)(2,1)S(1)} %add_terms.4), channel_id=1, source_target_pairs={{0,1},{1,2},{2,3},{3,4},{4,5},{5,6},{6,7},{7,8},{8,9},{9,10},{10,1... | collective-permute-start | bytes 1179656 | tf_op jit(solution)/shard_map/ppermute | solution.py:299
  61.0 4.0 %collective-permute-done.10 = bf16[512,384]{1,0:T(8,128)(2,1)S(1)} collective-permute-done((bf16[512,384]{1,0:T(8,128)(2,1)S(1)}, bf16[512,384]{1,0:T(8,128)(2,1)S(1)}, u32[]{:S(2)}, u32[]{:S(2)}) %collective-permute-start.10) | collective-permute-done | bytes 393248 | tf_op jit(solution)/shard_map/ppermute | solution.py:299
  65.0 1.9 %collective-permute-start.11 = (bf16[256,384]{1,0:T(8,128)(2,1)S(1)}, bf16[256,384]{1,0:T(8,128)(2,1)S(1)}, u32[]{:S(2)}, u32[]{:S(2)}) collective-permute-start(bf16[256,384]{1,0:T(8,128)(2,1)S(1)} %slice.47), channel_id=1, source_target_pairs={{0,1},{1,2},{2,3},{3,4},{4,5},{5,6},{6,7},{7,8},{8,9},{9,10},{10,1... | collective-permute-start | bytes 589832 | tf_op jit(solution)/shard_map/ppermute | solution.py:299
  67.2 2.4 %collective-permute-done.4.sums_ref = bf16[512,384]{1,0:T(8,128)(2,1)S(1)} collective-permute-done((bf16[512,384]{1,0:T(8,128)(2,1)S(1)}, bf16[512,384]{1,0:T(8,128)(2,1)S(1)}, u32[]{:S(2)}, u32[]{:S(2)}) %collective-permute-start.4) | collective-permute-done | bytes 393248 | tf_op jit(solution)/shard_map/ppermute | solution.py:299
  69.6 0.4 add_terms.5
  70.0 1.9 %collective-permute-start.5 = (bf16[256,384]{1,0:T(8,128)(2,1)S(1)}, bf16[256,384]{1,0:T(8,128)(2,1)S(1)}, u32[]{:S(2)}, u32[]{:S(2)}) collective-permute-start(bf16[256,384]{1,0:T(8,128)(2,1)S(1)} %get-tuple-element.21), channel_id=1, source_target_pairs={{0,1},{1,2},{2,3},{3,4},{4,5},{5,6},{6,7},{7,8},{8,9},{9,10},{10,1... | collective-permute-start | bytes 589832 | tf_op jit(solution)/shard_map/ppermute | solution.py:299
  71.9 4.6 %collective-permute-start.6 = (bf16[256,384]{1,0:T(8,128)(2,1)S(1)}, bf16[256,384]{1,0:T(8,128)(2,1)S(1)}, u32[]{:S(2)}, u32[]{:S(2)}) collective-permute-start(bf16[256,384]{1,0:T(8,128)(2,1)S(1)} %get-tuple-element.22), channel_id=1, source_target_pairs={{0,5},{1,6},{2,7},{3,8},{4,9},{5,10},{6,11},{7,12},{8,13},{9,14},{... | collective-permute-start | bytes 589832 | tf_op jit(solution)/shard_map/ppermute | solution.py:302
  76.6 4.9 %collective-permute-start.12 = (bf16[128,384]{1,0:T(8,128)(2,1)S(1)}, bf16[128,384]{1,0:T(8,128)(2,1)S(1)}, u32[]{:S(2)}, u32[]{:S(2)}) collective-permute-start(bf16[128,384]{1,0:T(8,128)(2,1)S(1)} %slice_select_fusion), channel_id=1, source_target_pairs={{0,1},{1,2},{2,3},{3,4},{4,5},{5,6},{6,7},{7,8},{8,9},{9,10},{10,1... | collective-permute-start | bytes 294920 | tf_op jit(solution)/shard_map/ppermute | solution.py:299
  81.8 7.7 %collective-permute-done.12 = bf16[128,384]{1,0:T(8,128)(2,1)S(1)} collective-permute-done((bf16[128,384]{1,0:T(8,128)(2,1)S(1)}, bf16[128,384]{1,0:T(8,128)(2,1)S(1)}, u32[]{:S(2)}, u32[]{:S(2)}) %collective-permute-start.12) | collective-permute-done | bytes 98336 | tf_op jit(solution)/shard_map/ppermute | solution.py:299
  90.2 7.5 %collective-permute-start.14 = (bf16[256,384]{1,0:T(8,128)(2,1)S(1)}, bf16[256,384]{1,0:T(8,128)(2,1)S(1)}, u32[]{:S(2)}, u32[]{:S(2)}) collective-permute-start(bf16[256,384]{1,0:T(8,128)(2,1)S(1)} %get-tuple-element.32), channel_id=1, source_target_pairs={{0,512},{16,528},{32,544},{48,560},{64,576},{80,592},{96,608},{112... | collective-permute-start | bytes 589832 | tf_op jit(solution)/shard_map/ppermute | solution.py:305
  97.9 1.9 %collective-permute-start.13 = (bf16[256,384]{1,0:T(8,128)(2,1)S(1)}, bf16[256,384]{1,0:T(8,128)(2,1)S(1)}, u32[]{:S(2)}, u32[]{:S(2)}) collective-permute-start(bf16[256,384]{1,0:T(8,128)(2,1)S(1)} %get-tuple-element.24), channel_id=1, source_target_pairs={{0,512},{16,528},{32,544},{48,560},{64,576},{80,592},{96,608},{112... | collective-permute-start | bytes 589832 | tf_op jit(solution)/shard_map/ppermute | solution.py:305
  99.8 1.4 %collective-permute-done.14.other_ref = bf16[256,384]{1,0:T(8,128)(2,1)S(1)} collective-permute-done((bf16[256,384]{1,0:T(8,128)(2,1)S(1)}, bf16[256,384]{1,0:T(8,128)(2,1)S(1)}, u32[]{:S(2)}, u32[]{:S(2)}) %collective-permute-start.14) | collective-permute-done | bytes 196640 | tf_op jit(solution)/shard_map/ppermute | solution.py:305
  101.3 2.8 %attention_backward.1 = (bf16[256,384]{1,0:T(8,128)(2,1)}, bf16[256,384]{1,0:T(8,128)(2,1)}, bf16[256,384]{1,0:T(8,128)(2,1)}) custom-call(bf16[256,384]{1,0:T(8,128)(2,1)S(1)} %copy-done.2, bf16[256,384]{1,0:T(8,128)(2,1)S(1)} %copy-done.3, bf16[256,384]{1,0:T(8,128)(2,1)S(1)} %copy-done.4, f32[256,384]{1,0:T(8,128)S(1)} %get-tuple-element.33.earlier_ref.partial_ref, ...), custom_call_target="tpu_custom_call" | custom-call | flops 301989888 | bytes 1771520 | tf_op jit(solution)/shard_map/attention_backward/pallas_call | solution.py:43
  104.1 2.9 %collective-permute-done.13.other_ref = bf16[256,384]{1,0:T(8,128)(2,1)S(1)} collective-permute-done((bf16[256,384]{1,0:T(8,128)(2,1)S(1)}, bf16[256,384]{1,0:T(8,128)(2,1)S(1)}, u32[]{:S(2)}, u32[]{:S(2)}) %collective-permute-start.13) | collective-permute-done | bytes 196640 | tf_op jit(solution)/shard_map/ppermute | solution.py:305
  107.0 0.9 finish_projected.1
  (31 shorter events, 3.7 us)
Async XLA Ops:
  0.6 10.4 %collective-permute-start.1 = (bf16[256,384]{1,0:T(8,128)(2,1)}, bf16[256,384]{1,0:T(8,128)(2,1)S(1)}, u32[]{:S(2)}, u32[]{:S(2)}) collective-permute-start(bf16[256,384]{1,0:T(8,128)(2,1)} %out_grad_hbm.1), channel_id=1, source_target_pairs={{0,512},{16,528},{32,544},{48,560},{64,576},{80,592},{96,608},{112... | collective-permute-start | bytes 589832 | tf_op jit(solution)/shard_map/ppermute | solution.py:305
  5.6 0.8 copy-start.5
  8.7 18.0 %collective-permute-start = (bf16[256,384]{1,0:T(8,128)(2,1)S(1)}, bf16[256,384]{1,0:T(8,128)(2,1)S(1)}, u32[]{:S(2)}, u32[]{:S(2)}) collective-permute-start(bf16[256,384]{1,0:T(8,128)(2,1)S(1)} %get-tuple-element.16.own_ref), channel_id=1, source_target_pairs={{0,512},{16,528},{32,544},{48,560},{64,576},{80,592},{96,608},{112... | collective-permute-start | bytes 589832 | tf_op jit(solution)/shard_map/ppermute | solution.py:305
  11.4 22.8 %collective-permute-start.7 = (bf16[256,384]{1,0:T(8,128)(2,1)S(1)}, bf16[256,384]{1,0:T(8,128)(2,1)S(1)}, u32[]{:S(2)}, u32[]{:S(2)}) collective-permute-start(bf16[256,384]{1,0:T(8,128)(2,1)S(1)} %pack_out_grad.1.earlier_ref), channel_id=1, source_target_pairs={{0,1},{1,2},{2,3},{3,4},{4,5},{5,6},{6,7},{7,8},{8,9},{9,10},{10,1... | collective-permute-start | bytes 589832 | tf_op jit(solution)/shard_map/ppermute | solution.py:299
  15.7 21.4 %collective-permute-start.8 = (bf16[256,384]{1,0:T(8,128)(2,1)S(1)}, bf16[256,384]{1,0:T(8,128)(2,1)S(1)}, u32[]{:S(2)}, u32[]{:S(2)}) collective-permute-start(bf16[256,384]{1,0:T(8,128)(2,1)S(1)} %pack_out_grad.1.earlier_ref), channel_id=1, source_target_pairs={{0,4},{1,5},{2,6},{3,7},{4,8},{5,9},{6,10},{7,11},{8,12},{9,13},{1... | collective-permute-start | bytes 589832 | tf_op jit(solution)/shard_map/ppermute | solution.py:341
  26.7 2.3 %copy-start = (bf16[384,6144]{1,0:T(8,128)(2,1)S(1)}, bf16[384,6144]{1,0:T(8,128)(2,1)}, u32[]{:S(2)}) copy-start(bf16[384,6144]{1,0:T(8,128)(2,1)} %weight_ref.9) | copy-start | bytes 14155780
  29.0 15.0 %copy-start.1 = (bf16[384,6144]{1,0:T(8,128)(2,1)S(1)}, bf16[384,6144]{1,0:T(8,128)(2,1)}, u32[]{:S(2)}) copy-start(bf16[384,6144]{1,0:T(8,128)(2,1)} %weight_ref.9) | copy-start | bytes 14155780
  29.6 16.1 %collective-permute-start.2 = (bf16[384,384]{1,0:T(8,128)(2,1)S(1)}, bf16[384,384]{1,0:T(8,128)(2,1)S(1)}, u32[]{:S(2)}, u32[]{:S(2)}) collective-permute-start(bf16[384,384]{1,0:T(8,128)(2,1)S(1)} %get-tuple-element.19.earlier_ref), channel_id=1, source_target_pairs={{0,1},{1,2},{2,3},{3,4},{4,5},{5,6},{6,7},{7,8},{8,9},{9,10},{10,1... | collective-permute-start | bytes 884744 | tf_op jit(solution)/shard_map/ppermute | solution.py:299
  37.1 15.1 %collective-permute-start.9 = (bf16[512,384]{1,0:T(8,128)(2,1)S(1)}, bf16[512,384]{1,0:T(8,128)(2,1)S(1)}, u32[]{:S(2)}, u32[]{:S(2)}) collective-permute-start(bf16[512,384]{1,0:T(8,128)(2,1)S(1)} %join_out_grad.1), channel_id=1, source_target_pairs={{0,1},{1,2},{2,3},{3,4},{4,5},{5,6},{6,7},{7,8},{8,9},{9,10},{10,1... | collective-permute-start | bytes 1179656 | tf_op jit(solution)/shard_map/ppermute | solution.py:299
  46.1 10.9 %collective-permute-start.3 = (bf16[512,384]{1,0:T(8,128)(2,1)S(1)}, bf16[512,384]{1,0:T(8,128)(2,1)S(1)}, u32[]{:S(2)}, u32[]{:S(2)}) collective-permute-start(bf16[512,384]{1,0:T(8,128)(2,1)S(1)} %add_terms.3), channel_id=1, source_target_pairs={{0,1},{1,2},{2,3},{3,4},{4,5},{5,6},{6,7},{7,8},{8,9},{9,10},{10,1... | collective-permute-start | bytes 1179656 | tf_op jit(solution)/shard_map/ppermute | solution.py:299
  52.2 12.8 %collective-permute-start.10 = (bf16[512,384]{1,0:T(8,128)(2,1)S(1)}, bf16[512,384]{1,0:T(8,128)(2,1)S(1)}, u32[]{:S(2)}, u32[]{:S(2)}) collective-permute-start(bf16[512,384]{1,0:T(8,128)(2,1)S(1)} %collective-permute-done.9), channel_id=1, source_target_pairs={{0,1},{1,2},{2,3},{3,4},{4,5},{5,6},{6,7},{7,8},{8,9},{9,10},{10,1... | collective-permute-start | bytes 1179656 | tf_op jit(solution)/shard_map/ppermute | solution.py:299
  57.4 12.2 %collective-permute-start.4 = (bf16[512,384]{1,0:T(8,128)(2,1)S(1)}, bf16[512,384]{1,0:T(8,128)(2,1)S(1)}, u32[]{:S(2)}, u32[]{:S(2)}) collective-permute-start(bf16[512,384]{1,0:T(8,128)(2,1)S(1)} %add_terms.4), channel_id=1, source_target_pairs={{0,1},{1,2},{2,3},{3,4},{4,5},{5,6},{6,7},{7,8},{8,9},{9,10},{10,1... | collective-permute-start | bytes 1179656 | tf_op jit(solution)/shard_map/ppermute | solution.py:299
  65.0 11.5 %collective-permute-start.11 = (bf16[256,384]{1,0:T(8,128)(2,1)S(1)}, bf16[256,384]{1,0:T(8,128)(2,1)S(1)}, u32[]{:S(2)}, u32[]{:S(2)}) collective-permute-start(bf16[256,384]{1,0:T(8,128)(2,1)S(1)} %slice.47), channel_id=1, source_target_pairs={{0,1},{1,2},{2,3},{3,4},{4,5},{5,6},{6,7},{7,8},{8,9},{9,10},{10,1... | collective-permute-start | bytes 589832 | tf_op jit(solution)/shard_map/ppermute | solution.py:299
  70.0 27.7 %collective-permute-start.5 = (bf16[256,384]{1,0:T(8,128)(2,1)S(1)}, bf16[256,384]{1,0:T(8,128)(2,1)S(1)}, u32[]{:S(2)}, u32[]{:S(2)}) collective-permute-start(bf16[256,384]{1,0:T(8,128)(2,1)S(1)} %get-tuple-element.21), channel_id=1, source_target_pairs={{0,1},{1,2},{2,3},{3,4},{4,5},{5,6},{6,7},{7,8},{8,9},{9,10},{10,1... | collective-permute-start | bytes 589832 | tf_op jit(solution)/shard_map/ppermute | solution.py:299
  71.9 25.7 %collective-permute-start.6 = (bf16[256,384]{1,0:T(8,128)(2,1)S(1)}, bf16[256,384]{1,0:T(8,128)(2,1)S(1)}, u32[]{:S(2)}, u32[]{:S(2)}) collective-permute-start(bf16[256,384]{1,0:T(8,128)(2,1)S(1)} %get-tuple-element.22), channel_id=1, source_target_pairs={{0,5},{1,6},{2,7},{3,8},{4,9},{5,10},{6,11},{7,12},{8,13},{9,14},{... | collective-permute-start | bytes 589832 | tf_op jit(solution)/shard_map/ppermute | solution.py:302
  76.6 13.0 %collective-permute-start.12 = (bf16[128,384]{1,0:T(8,128)(2,1)S(1)}, bf16[128,384]{1,0:T(8,128)(2,1)S(1)}, u32[]{:S(2)}, u32[]{:S(2)}) collective-permute-start(bf16[128,384]{1,0:T(8,128)(2,1)S(1)} %slice_select_fusion), channel_id=1, source_target_pairs={{0,1},{1,2},{2,3},{3,4},{4,5},{5,6},{6,7},{7,8},{8,9},{9,10},{10,1... | collective-permute-start | bytes 294920 | tf_op jit(solution)/shard_map/ppermute | solution.py:299
  81.8 19.5 %copy-start.2 = (bf16[256,384]{1,0:T(8,128)(2,1)S(1)}, bf16[256,384]{1,0:T(8,128)(2,1)}, u32[]{:S(2)}) copy-start(bf16[256,384]{1,0:T(8,128)(2,1)} %query_ref.1) | copy-start | bytes 589828
  81.8 19.5 %copy-start.3 = (bf16[256,384]{1,0:T(8,128)(2,1)S(1)}, bf16[256,384]{1,0:T(8,128)(2,1)}, u32[]{:S(2)}) copy-start(bf16[256,384]{1,0:T(8,128)(2,1)} %key_ref.1) | copy-start | bytes 589828
  81.8 19.5 %copy-start.4 = (bf16[256,384]{1,0:T(8,128)(2,1)S(1)}, bf16[256,384]{1,0:T(8,128)(2,1)}, u32[]{:S(2)}) copy-start(bf16[256,384]{1,0:T(8,128)(2,1)} %value_ref.1) | copy-start | bytes 589828
  90.2 11.1 %collective-permute-start.14 = (bf16[256,384]{1,0:T(8,128)(2,1)S(1)}, bf16[256,384]{1,0:T(8,128)(2,1)S(1)}, u32[]{:S(2)}, u32[]{:S(2)}) collective-permute-start(bf16[256,384]{1,0:T(8,128)(2,1)S(1)} %get-tuple-element.32), channel_id=1, source_target_pairs={{0,512},{16,528},{32,544},{48,560},{64,576},{80,592},{96,608},{112... | collective-permute-start | bytes 589832 | tf_op jit(solution)/shard_map/ppermute | solution.py:305
  97.9 9.1 %collective-permute-start.13 = (bf16[256,384]{1,0:T(8,128)(2,1)S(1)}, bf16[256,384]{1,0:T(8,128)(2,1)S(1)}, u32[]{:S(2)}, u32[]{:S(2)}) collective-permute-start(bf16[256,384]{1,0:T(8,128)(2,1)S(1)} %get-tuple-element.24), channel_id=1, source_target_pairs={{0,512},{16,528},{32,544},{48,560},{64,576},{80,592},{96,608},{112... | collective-permute-start | bytes 589832 | tf_op jit(solution)/shard_map/ppermute | solution.py:305

commit v8 on v6

--- a/solution.py
+++ b/solution.py
@@ -151,7 +151,7 @@
         out_refs[0][ROWS:, :] = far_sum.astype(jnp.bfloat16)
 
 
-def join_kernel(near_ref, far_ref, earlier_ref, out_ref):
+def join_kernel(far_ref, near_ref, earlier_ref, out_ref):
     del earlier_ref
     out_ref[:ROWS, :] = near_ref[...]
     out_ref[ROWS:, :] = far_ref[...]
@@ -315,7 +315,8 @@
     (pair_grad,) = call(
         pack_kernel, [rows_type], (own_out_grad, other_out_grad, starts), name="pack_out_grad"
     )
-    near_block, far_block = hop(pair_grad), jump(pair_grad)
+    far_block = jump(pair_grad)
+    near_block = hop(pair_grad)
     pair_attended, first_terms = call(
         functools.partial(pack_terms_kernel, dp_size, mp_size, (near, near + far - 1)),
         [rows_type, half_type],
@@ -345,7 +346,7 @@
             (moved,) = call(
                 join_kernel,
                 [jax.ShapeDtypeStruct((2 * ROWS, width), jnp.bfloat16)],
-                (near_block, far_block, first_terms),
+                (far_block, near_block, first_terms),
                 specs=[IN_VMEM] * 2 + [in_any],
                 name="join_out_grad",
             )

time: 106 us -> 103 us (0.972)
  the two profiles are of different devices: /device:TPU:42 before, /device:TPU:68 now
where the time goes in v8:
time: 103 us
  starting transfers between devices  70.4 us (68%)
  waiting for transfers between devices  17 us (17%)
  Pallas kernels  8.04 us (8%)
  local copies, waits for them, and re-layouts  3.21 us (3%)
  matrix products  2.85 us (3%)
  between operations  1.09 us (1%)
    ppermute x8, starting transfers between devices, hop(): return lax.ppermute(rows, ('dp', 'mp'), hop_perm)  33.6 us
    ppermute x2, starting transfers between devices, jump(): return lax.ppermute(rows, ('dp', 'mp'), jump_perm)  25.6 us
    ppermute x4, starting transfers between devices, swap(): return lax.ppermute(rows, 'dp', swap_perm)  11.2 us
    ppermute x4, waiting for transfers between devices, swap(): return lax.ppermute(rows, 'dp', swap_perm)  8.12 us
    pallas_call x9, Pallas kernels, call(): pl.pallas_call(kernel, out_shape=outs, in_specs=specs or [IN_VMEM] * len(...  8.04 us
    ppermute x2, waiting for transfers between devices, jump(): return lax.ppermute(rows, ('dp', 'mp'), jump_perm)  6.06 us
    unnamed x12, local copies, waits for them, and re-layouts  3.19 us
    dot_general x10, matrix products, dot(): lax.dot_general(a, b, (((dims[0],), (dims[1],)), ((), ())), preferred_ele...  2.85 us
  transfers between devices with their start and end apart: 14, of which 7 were waited for; matrix products, arithmetic and copies ran while one was open for 3% of the time, Pallas kernels for 7%

profile of v8, /device:TPU:68, one launch (start us, length us, event | category | flops | bytes accessed | tf_op | source)
XLA Modules:
  0.0 102.7 jit_solution(584812563861379113)
XLA Ops:
  0.6 2.4 %collective-permute-start.1 = (bf16[256,384]{1,0:T(8,128)(2,1)}, bf16[256,384]{1,0:T(8,128)(2,1)S(1)}, u32[]{:S(2)}, u32[]{:S(2)}) collective-permute-start(bf16[256,384]{1,0:T(8,128)(2,1)} %out_grad_hbm.1), channel_id=1, source_target_pairs={{0,512},{16,528},{32,544},{48,560},{64,576},{80,592},{96,608},{112... | collective-permute-start | bytes 589832 | tf_op jit(solution)/shard_map/ppermute | solution.py:283
  3.1 0.8 copy-done.5
  3.9 2.2 %attention_forward.1 = (bf16[256,384]{1,0:T(8,128)(2,1)S(1)}, bf16[256,384]{1,0:T(8,128)(2,1)S(1)}, s32[2,256]{1,0:T(2,128)S(1)}) custom-call(bf16[256,384]{1,0:T(8,128)(2,1)} %query_ref.1, bf16[256,384]{1,0:T(8,128)(2,1)} %key_ref.1, bf16[256,384]{1,0:T(8,128)(2,1)} %value_ref.1, bf16[256,384]{1,0:T(8,128)(2,1)} %out_grad_hbm.1, s32[64,256]{1,0:T(8,128)S(1)} %copy-done.5), custom_call_target="tpu_custom_call" | custom-call | flops 100663296 | bytes 1247232 | tf_op jit(solution)/shard_map/attention_forward/pallas_call | solution.py:43
  6.1 4.9 %collective-permute-start = (bf16[256,384]{1,0:T(8,128)(2,1)S(1)}, bf16[256,384]{1,0:T(8,128)(2,1)S(1)}, u32[]{:S(2)}, u32[]{:S(2)}) collective-permute-start(bf16[256,384]{1,0:T(8,128)(2,1)S(1)} %get-tuple-element.16.own_ref), channel_id=1, source_target_pairs={{0,512},{16,528},{32,544},{48,560},{64,576},{80,592},{96,608},{112... | collective-permute-start | bytes 589832 | tf_op jit(solution)/shard_map/ppermute | solution.py:283
  11.1 0.3 pack_out_grad.1.earlier_ref
  11.4 17.3 %collective-permute-start.7 = (bf16[256,384]{1,0:T(8,128)(2,1)S(1)}, bf16[256,384]{1,0:T(8,128)(2,1)S(1)}, u32[]{:S(2)}, u32[]{:S(2)}) collective-permute-start(bf16[256,384]{1,0:T(8,128)(2,1)S(1)} %pack_out_grad.1.earlier_ref), channel_id=1, source_target_pairs={{0,5},{1,6},{2,7},{3,8},{4,9},{5,10},{6,11},{7,12},{8,13},{9,14},{... | collective-permute-start | bytes 589832 | tf_op jit(solution)/shard_map/ppermute | solution.py:280
  28.7 3.7 %collective-permute-start.8 = (bf16[256,384]{1,0:T(8,128)(2,1)S(1)}, bf16[256,384]{1,0:T(8,128)(2,1)S(1)}, u32[]{:S(2)}, u32[]{:S(2)}) collective-permute-start(bf16[256,384]{1,0:T(8,128)(2,1)S(1)} %pack_out_grad.1.earlier_ref), channel_id=1, source_target_pairs={{0,1},{1,2},{2,3},{3,4},{4,5},{5,6},{6,7},{7,8},{8,9},{9,10},{10,1... | collective-permute-start | bytes 589832 | tf_op jit(solution)/shard_map/ppermute | solution.py:277
  32.5 2.3 %copy-done = bf16[384,6144]{1,0:T(8,128)(2,1)S(1)} copy-done((bf16[384,6144]{1,0:T(8,128)(2,1)S(1)}, bf16[384,6144]{1,0:T(8,128)(2,1)}, u32[]{:S(2)}) %copy-start) | copy-done | bytes 4718616
  34.8 0.6 pack_attended.1
  35.4 2.7 %collective-permute-start.2 = (bf16[384,384]{1,0:T(8,128)(2,1)S(1)}, bf16[384,384]{1,0:T(8,128)(2,1)S(1)}, u32[]{:S(2)}, u32[]{:S(2)}) collective-permute-start(bf16[384,384]{1,0:T(8,128)(2,1)S(1)} %get-tuple-element.19.earlier_ref), channel_id=1, source_target_pairs={{0,1},{1,2},{2,3},{3,4},{4,5},{5,6},{6,7},{7,8},{8,9},{9,10},{10,1... | collective-permute-start | bytes 884744 | tf_op jit(solution)/shard_map/ppermute | solution.py:277
  38.1 1.7 %collective-permute-done.7.far_ref = bf16[256,384]{1,0:T(8,128)(2,1)S(1)} collective-permute-done((bf16[256,384]{1,0:T(8,128)(2,1)S(1)}, bf16[256,384]{1,0:T(8,128)(2,1)S(1)}, u32[]{:S(2)}, u32[]{:S(2)}) %collective-permute-start.7) | collective-permute-done | bytes 196640 | tf_op jit(solution)/shard_map/ppermute | solution.py:280
  39.7 2.1 %collective-permute-done.8.near_ref = bf16[256,384]{1,0:T(8,128)(2,1)S(1)} collective-permute-done((bf16[256,384]{1,0:T(8,128)(2,1)S(1)}, bf16[256,384]{1,0:T(8,128)(2,1)S(1)}, u32[]{:S(2)}, u32[]{:S(2)}) %collective-permute-start.8) | collective-permute-done | bytes 196640 | tf_op jit(solution)/shard_map/ppermute | solution.py:277
  41.9 4.4 %collective-permute-start.9 = (bf16[512,384]{1,0:T(8,128)(2,1)S(1)}, bf16[512,384]{1,0:T(8,128)(2,1)S(1)}, u32[]{:S(2)}, u32[]{:S(2)}) collective-permute-start(bf16[512,384]{1,0:T(8,128)(2,1)S(1)} %join_out_grad.1), channel_id=1, source_target_pairs={{0,1},{1,2},{2,3},{3,4},{4,5},{5,6},{6,7},{7,8},{8,9},{9,10},{10,1... | collective-permute-start | bytes 1179656 | tf_op jit(solution)/shard_map/ppermute | solution.py:277
  46.9 0.4 add_terms.3
  47.3 5.4 %collective-permute-start.3 = (bf16[512,384]{1,0:T(8,128)(2,1)S(1)}, bf16[512,384]{1,0:T(8,128)(2,1)S(1)}, u32[]{:S(2)}, u32[]{:S(2)}) collective-permute-start(bf16[512,384]{1,0:T(8,128)(2,1)S(1)} %add_terms.3), channel_id=1, source_target_pairs={{0,1},{1,2},{2,3},{3,4},{4,5},{5,6},{6,7},{7,8},{8,9},{9,10},{10,1... | collective-permute-start | bytes 1179656 | tf_op jit(solution)/shard_map/ppermute | solution.py:277
  52.7 4.2 %collective-permute-start.10 = (bf16[512,384]{1,0:T(8,128)(2,1)S(1)}, bf16[512,384]{1,0:T(8,128)(2,1)S(1)}, u32[]{:S(2)}, u32[]{:S(2)}) collective-permute-start(bf16[512,384]{1,0:T(8,128)(2,1)S(1)} %collective-permute-done.9), channel_id=1, source_target_pairs={{0,1},{1,2},{2,3},{3,4},{4,5},{5,6},{6,7},{7,8},{8,9},{9,10},{10,1... | collective-permute-start | bytes 1179656 | tf_op jit(solution)/shard_map/ppermute | solution.py:277
  57.6 0.4 collective-permute-done.3.sums_ref
  58.0 0.4 add_terms.4
  58.4 5.2 %collective-permute-start.4 = (bf16[512,384]{1,0:T(8,128)(2,1)S(1)}, bf16[512,384]{1,0:T(8,128)(2,1)S(1)}, u32[]{:S(2)}, u32[]{:S(2)}) collective-permute-start(bf16[512,384]{1,0:T(8,128)(2,1)S(1)} %add_terms.4), channel_id=1, source_target_pairs={{0,1},{1,2},{2,3},{3,4},{4,5},{5,6},{6,7},{7,8},{8,9},{9,10},{10,1... | collective-permute-start | bytes 1179656 | tf_op jit(solution)/shard_map/ppermute | solution.py:277
  63.7 4.2 %collective-permute-start.11 = (bf16[384,384]{1,0:T(8,128)(2,1)S(1)}, bf16[384,384]{1,0:T(8,128)(2,1)S(1)}, u32[]{:S(2)}, u32[]{:S(2)}) collective-permute-start(bf16[384,384]{1,0:T(8,128)(2,1)S(1)} %pad_maximum_fusion), channel_id=1, source_target_pairs={{0,1},{1,2},{2,3},{3,4},{4,5},{5,6},{6,7},{7,8},{8,9},{9,10},{10,1... | collective-permute-start | bytes 884744 | tf_op jit(solution)/shard_map/ppermute | solution.py:277
  67.9 0.3 fusion.2
  68.9 0.4 add_terms.5
  69.3 8.3 %collective-permute-start.6 = (bf16[256,384]{1,0:T(8,128)(2,1)S(1)}, bf16[256,384]{1,0:T(8,128)(2,1)S(1)}, u32[]{:S(2)}, u32[]{:S(2)}) collective-permute-start(bf16[256,384]{1,0:T(8,128)(2,1)S(1)} %get-tuple-element.22), channel_id=1, source_target_pairs={{0,5},{1,6},{2,7},{3,8},{4,9},{5,10},{6,11},{7,12},{8,13},{9,14},{... | collective-permute-start | bytes 589832 | tf_op jit(solution)/shard_map/ppermute | solution.py:280
  77.6 3.8 %collective-permute-start.5 = (bf16[256,384]{1,0:T(8,128)(2,1)S(1)}, bf16[256,384]{1,0:T(8,128)(2,1)S(1)}, u32[]{:S(2)}, u32[]{:S(2)}) collective-permute-start(bf16[256,384]{1,0:T(8,128)(2,1)S(1)} %get-tuple-element.21), channel_id=1, source_target_pairs={{0,1},{1,2},{2,3},{3,4},{4,5},{5,6},{6,7},{7,8},{8,9},{9,10},{10,1... | collective-permute-start | bytes 589832 | tf_op jit(solution)/shard_map/ppermute | solution.py:277
  82.0 0.3 fusion.49
  82.3 1.9 %collective-permute-start.12 = (bf16[256,384]{1,0:T(8,128)(2,1)S(1)}, bf16[256,384]{1,0:T(8,128)(2,1)S(1)}, u32[]{:S(2)}, u32[]{:S(2)}) collective-permute-start(bf16[256,384]{1,0:T(8,128)(2,1)S(1)} %get-tuple-element.36), channel_id=1, source_target_pairs={{0,512},{16,528},{32,544},{48,560},{64,576},{80,592},{96,608},{112... | collective-permute-start | bytes 589832 | tf_op jit(solution)/shard_map/ppermute | solution.py:283
  84.5 4.4 %collective-permute-done.6 = bf16[256,384]{1,0:T(8,128)(2,1)S(1)} collective-permute-done((bf16[256,384]{1,0:T(8,128)(2,1)S(1)}, bf16[256,384]{1,0:T(8,128)(2,1)S(1)}, u32[]{:S(2)}, u32[]{:S(2)}) %collective-permute-start.6) | collective-permute-done | bytes 196640 | tf_op jit(solution)/shard_map/ppermute | solution.py:280
  88.9 3.8 %collective-permute-done.12.other_ref = bf16[256,384]{1,0:T(8,128)(2,1)S(1)} collective-permute-done((bf16[256,384]{1,0:T(8,128)(2,1)S(1)}, bf16[256,384]{1,0:T(8,128)(2,1)S(1)}, u32[]{:S(2)}, u32[]{:S(2)}) %collective-permute-start.12) | collective-permute-done | bytes 196640 | tf_op jit(solution)/shard_map/ppermute | solution.py:283
  92.8 1.9 %collective-permute-start.13 = (bf16[256,384]{1,0:T(8,128)(2,1)S(1)}, bf16[256,384]{1,0:T(8,128)(2,1)S(1)}, u32[]{:S(2)}, u32[]{:S(2)}) collective-permute-start(bf16[256,384]{1,0:T(8,128)(2,1)S(1)} %get-tuple-element.28), channel_id=1, source_target_pairs={{0,512},{16,528},{32,544},{48,560},{64,576},{80,592},{96,608},{112... | collective-permute-start | bytes 589832 | tf_op jit(solution)/shard_map/ppermute | solution.py:283
  94.7 2.8 %attention_backward.1 = (bf16[256,384]{1,0:T(8,128)(2,1)}, bf16[256,384]{1,0:T(8,128)(2,1)}, bf16[256,384]{1,0:T(8,128)(2,1)}) custom-call(bf16[256,384]{1,0:T(8,128)(2,1)S(1)} %copy-done.2, bf16[256,384]{1,0:T(8,128)(2,1)S(1)} %copy-done.3, bf16[256,384]{1,0:T(8,128)(2,1)S(1)} %copy-done.4, f32[256,384]{1,0:T(8,128)S(1)} %get-tuple-element.37.partial_ref, ...), custom_call_target="tpu_custom_call" | custom-call | flops 301989888 | bytes 1771520 | tf_op jit(solution)/shard_map/attention_backward/pallas_call | solution.py:43
  97.6 4.3 %collective-permute-done.13.other_ref = bf16[256,384]{1,0:T(8,128)(2,1)S(1)} collective-permute-done((bf16[256,384]{1,0:T(8,128)(2,1)S(1)}, bf16[256,384]{1,0:T(8,128)(2,1)S(1)}, u32[]{:S(2)}, u32[]{:S(2)}) %collective-permute-start.13) | collective-permute-done | bytes 196640 | tf_op jit(solution)/shard_map/ppermute | solution.py:283
  101.8 0.9 finish_projected.1
  (31 shorter events, 2.7 us)
Async XLA Ops:
  0.6 10.4 %collective-permute-start.1 = (bf16[256,384]{1,0:T(8,128)(2,1)}, bf16[256,384]{1,0:T(8,128)(2,1)S(1)}, u32[]{:S(2)}, u32[]{:S(2)}) collective-permute-start(bf16[256,384]{1,0:T(8,128)(2,1)} %out_grad_hbm.1), channel_id=1, source_target_pairs={{0,512},{16,528},{32,544},{48,560},{64,576},{80,592},{96,608},{112... | collective-permute-start | bytes 589832 | tf_op jit(solution)/shard_map/ppermute | solution.py:283
  3.1 0.8 copy-start.5
  6.1 26.3 %collective-permute-start = (bf16[256,384]{1,0:T(8,128)(2,1)S(1)}, bf16[256,384]{1,0:T(8,128)(2,1)S(1)}, u32[]{:S(2)}, u32[]{:S(2)}) collective-permute-start(bf16[256,384]{1,0:T(8,128)(2,1)S(1)} %get-tuple-element.16.own_ref), channel_id=1, source_target_pairs={{0,512},{16,528},{32,544},{48,560},{64,576},{80,592},{96,608},{112... | collective-permute-start | bytes 589832 | tf_op jit(solution)/shard_map/ppermute | solution.py:283
  11.4 28.4 %collective-permute-start.7 = (bf16[256,384]{1,0:T(8,128)(2,1)S(1)}, bf16[256,384]{1,0:T(8,128)(2,1)S(1)}, u32[]{:S(2)}, u32[]{:S(2)}) collective-permute-start(bf16[256,384]{1,0:T(8,128)(2,1)S(1)} %pack_out_grad.1.earlier_ref), channel_id=1, source_target_pairs={{0,5},{1,6},{2,7},{3,8},{4,9},{5,10},{6,11},{7,12},{8,13},{9,14},{... | collective-permute-start | bytes 589832 | tf_op jit(solution)/shard_map/ppermute | solution.py:280
  28.7 13.2 %collective-permute-start.8 = (bf16[256,384]{1,0:T(8,128)(2,1)S(1)}, bf16[256,384]{1,0:T(8,128)(2,1)S(1)}, u32[]{:S(2)}, u32[]{:S(2)}) collective-permute-start(bf16[256,384]{1,0:T(8,128)(2,1)S(1)} %pack_out_grad.1.earlier_ref), channel_id=1, source_target_pairs={{0,1},{1,2},{2,3},{3,4},{4,5},{5,6},{6,7},{7,8},{8,9},{9,10},{10,1... | collective-permute-start | bytes 589832 | tf_op jit(solution)/shard_map/ppermute | solution.py:277
  32.5 2.3 %copy-start = (bf16[384,6144]{1,0:T(8,128)(2,1)S(1)}, bf16[384,6144]{1,0:T(8,128)(2,1)}, u32[]{:S(2)}) copy-start(bf16[384,6144]{1,0:T(8,128)(2,1)} %weight_ref.7) | copy-start | bytes 14155780
  34.8 11.5 %copy-start.1 = (bf16[384,6144]{1,0:T(8,128)(2,1)S(1)}, bf16[384,6144]{1,0:T(8,128)(2,1)}, u32[]{:S(2)}) copy-start(bf16[384,6144]{1,0:T(8,128)(2,1)} %weight_ref.7) | copy-start | bytes 14155780
  35.4 11.5 %collective-permute-start.2 = (bf16[384,384]{1,0:T(8,128)(2,1)S(1)}, bf16[384,384]{1,0:T(8,128)(2,1)S(1)}, u32[]{:S(2)}, u32[]{:S(2)}) collective-permute-start(bf16[384,384]{1,0:T(8,128)(2,1)S(1)} %get-tuple-element.19.earlier_ref), channel_id=1, source_target_pairs={{0,1},{1,2},{2,3},{3,4},{4,5},{5,6},{6,7},{7,8},{8,9},{9,10},{10,1... | collective-permute-start | bytes 884744 | tf_op jit(solution)/shard_map/ppermute | solution.py:277
  41.9 10.8 %collective-permute-start.9 = (bf16[512,384]{1,0:T(8,128)(2,1)S(1)}, bf16[512,384]{1,0:T(8,128)(2,1)S(1)}, u32[]{:S(2)}, u32[]{:S(2)}) collective-permute-start(bf16[512,384]{1,0:T(8,128)(2,1)S(1)} %join_out_grad.1), channel_id=1, source_target_pairs={{0,1},{1,2},{2,3},{3,4},{4,5},{5,6},{6,7},{7,8},{8,9},{9,10},{10,1... | collective-permute-start | bytes 1179656 | tf_op jit(solution)/shard_map/ppermute | solution.py:277
  47.3 10.7 %collective-permute-start.3 = (bf16[512,384]{1,0:T(8,128)(2,1)S(1)}, bf16[512,384]{1,0:T(8,128)(2,1)S(1)}, u32[]{:S(2)}, u32[]{:S(2)}) collective-permute-start(bf16[512,384]{1,0:T(8,128)(2,1)S(1)} %add_terms.3), channel_id=1, source_target_pairs={{0,1},{1,2},{2,3},{3,4},{4,5},{5,6},{6,7},{7,8},{8,9},{9,10},{10,1... | collective-permute-start | bytes 1179656 | tf_op jit(solution)/shard_map/ppermute | solution.py:277
  52.7 10.9 %collective-permute-start.10 = (bf16[512,384]{1,0:T(8,128)(2,1)S(1)}, bf16[512,384]{1,0:T(8,128)(2,1)S(1)}, u32[]{:S(2)}, u32[]{:S(2)}) collective-permute-start(bf16[512,384]{1,0:T(8,128)(2,1)S(1)} %collective-permute-done.9), channel_id=1, source_target_pairs={{0,1},{1,2},{2,3},{3,4},{4,5},{5,6},{6,7},{7,8},{8,9},{9,10},{10,1... | collective-permute-start | bytes 1179656 | tf_op jit(solution)/shard_map/ppermute | solution.py:277
  58.4 10.5 %collective-permute-start.4 = (bf16[512,384]{1,0:T(8,128)(2,1)S(1)}, bf16[512,384]{1,0:T(8,128)(2,1)S(1)}, u32[]{:S(2)}, u32[]{:S(2)}) collective-permute-start(bf16[512,384]{1,0:T(8,128)(2,1)S(1)} %add_terms.4), channel_id=1, source_target_pairs={{0,1},{1,2},{2,3},{3,4},{4,5},{5,6},{6,7},{7,8},{8,9},{9,10},{10,1... | collective-permute-start | bytes 1179656 | tf_op jit(solution)/shard_map/ppermute | solution.py:277
  63.7 17.7 %collective-permute-start.11 = (bf16[384,384]{1,0:T(8,128)(2,1)S(1)}, bf16[384,384]{1,0:T(8,128)(2,1)S(1)}, u32[]{:S(2)}, u32[]{:S(2)}) collective-permute-start(bf16[384,384]{1,0:T(8,128)(2,1)S(1)} %pad_maximum_fusion), channel_id=1, source_target_pairs={{0,1},{1,2},{2,3},{3,4},{4,5},{5,6},{6,7},{7,8},{8,9},{9,10},{10,1... | collective-permute-start | bytes 884744 | tf_op jit(solution)/shard_map/ppermute | solution.py:277
  68.6 26.1 %copy-start.2 = (bf16[256,384]{1,0:T(8,128)(2,1)S(1)}, bf16[256,384]{1,0:T(8,128)(2,1)}, u32[]{:S(2)}) copy-start(bf16[256,384]{1,0:T(8,128)(2,1)} %query_ref.1) | copy-start | bytes 589828
  68.6 26.1 %copy-start.3 = (bf16[256,384]{1,0:T(8,128)(2,1)S(1)}, bf16[256,384]{1,0:T(8,128)(2,1)}, u32[]{:S(2)}) copy-start(bf16[256,384]{1,0:T(8,128)(2,1)} %key_ref.1) | copy-start | bytes 589828
  68.6 26.1 %copy-start.4 = (bf16[256,384]{1,0:T(8,128)(2,1)S(1)}, bf16[256,384]{1,0:T(8,128)(2,1)}, u32[]{:S(2)}) copy-start(bf16[256,384]{1,0:T(8,128)(2,1)} %value_ref.1) | copy-start | bytes 589828
  69.3 19.6 %collective-permute-start.6 = (bf16[256,384]{1,0:T(8,128)(2,1)S(1)}, bf16[256,384]{1,0:T(8,128)(2,1)S(1)}, u32[]{:S(2)}, u32[]{:S(2)}) collective-permute-start(bf16[256,384]{1,0:T(8,128)(2,1)S(1)} %get-tuple-element.22), channel_id=1, source_target_pairs={{0,5},{1,6},{2,7},{3,8},{4,9},{5,10},{6,11},{7,12},{8,13},{9,14},{... | collective-permute-start | bytes 589832 | tf_op jit(solution)/shard_map/ppermute | solution.py:280
  77.6 15.1 %collective-permute-start.5 = (bf16[256,384]{1,0:T(8,128)(2,1)S(1)}, bf16[256,384]{1,0:T(8,128)(2,1)S(1)}, u32[]{:S(2)}, u32[]{:S(2)}) collective-permute-start(bf16[256,384]{1,0:T(8,128)(2,1)S(1)} %get-tuple-element.21), channel_id=1, source_target_pairs={{0,1},{1,2},{2,3},{3,4},{4,5},{5,6},{6,7},{7,8},{8,9},{9,10},{10,1... | collective-permute-start | bytes 589832 | tf_op jit(solution)/shard_map/ppermute | solution.py:277
  82.3 10.4 %collective-permute-start.12 = (bf16[256,384]{1,0:T(8,128)(2,1)S(1)}, bf16[256,384]{1,0:T(8,128)(2,1)S(1)}, u32[]{:S(2)}, u32[]{:S(2)}) collective-permute-start(bf16[256,384]{1,0:T(8,128)(2,1)S(1)} %get-tuple-element.36), channel_id=1, source_target_pairs={{0,512},{16,528},{32,544},{48,560},{64,576},{80,592},{96,608},{112... | collective-permute-start | bytes 589832 | tf_op jit(solution)/shard_map/ppermute | solution.py:283
  92.8 9.1 %collective-permute-start.13 = (bf16[256,384]{1,0:T(8,128)(2,1)S(1)}, bf16[256,384]{1,0:T(8,128)(2,1)S(1)}, u32[]{:S(2)}, u32[]{:S(2)}) collective-permute-start(bf16[256,384]{1,0:T(8,128)(2,1)S(1)} %get-tuple-element.28), channel_id=1, source_target_pairs={{0,512},{16,528},{32,544},{48,560},{64,576},{80,592},{96,608},{112... | collective-permute-start | bytes 589832 | tf_op jit(solution)/shard_map/ppermute | solution.py:283

commit v9 on v7

--- a/solution.py
+++ b/solution.py
@@ -154,8 +154,8 @@
 def total_kernel(
     dp_size,
     mp_size,
+    last_ref,
     near_ref,
-    last_ref,
     rows_ref,
     weight_ref,
     earlier_ref,
@@ -172,7 +172,7 @@
     sent_ref[...] = total_ref[...].astype(jnp.bfloat16)
 
 
-def join_kernel(near_ref, far_ref, earlier_ref, out_ref):
+def join_kernel(far_ref, near_ref, earlier_ref, out_ref):
     del earlier_ref
     out_ref[:ROWS, :] = near_ref[...]
     out_ref[ROWS:, :] = far_ref[...]
@@ -288,7 +288,6 @@
     dp, z = lax.axis_index("dp"), lax.axis_index("mp")
     hop_perm = ring_pairs(dp_size, mp_size, 1)
     jump_perm = ring_pairs(dp_size, mp_size, far)
-    gather_perm = ring_pairs(dp_size, mp_size, near)
     swap_perm = [(i, (i + dp_size // 2) % dp_size) for i in range(dp_size)]
     right = goes_right(dp, dp_size)
     delta = jnp.where(right, 1, mp_size - 1)
@@ -337,8 +336,8 @@
     (pair_grad,) = call(
         pack_kernel, [rows_type], (own_out_grad, other_out_grad, starts), name="pack_out_grad"
     )
+    far_block = jump(pair_grad)
     near_block = hop(pair_grad)
-    far_block = lax.ppermute(pair_grad, ("dp", "mp"), gather_perm)
     pair_attended, first_terms = call(
         functools.partial(pack_terms_kernel, dp_size, mp_size, (near, near + far - 1)),
         [rows_type, half_type],
@@ -368,7 +367,7 @@
             (moved,) = call(
                 join_kernel,
                 [jax.ShapeDtypeStruct((2 * ROWS, width), jnp.bfloat16)],
-                (near_block, far_block, first_terms),
+                (far_block, near_block, first_terms),
                 specs=[IN_VMEM] * 2 + [in_any],
                 name="join_out_grad",
             )
@@ -378,18 +377,17 @@
     partial = place_half(product(half_of(pair_grad), 0))
     for step in range(1, near):
         near_block, far_block = moved[:ROWS], moved[ROWS:]
-        partial = partial + product(near_block, step) + product(far_block, near + step - 1)
-        if step < near - 1:
-            moved = hop(moved)
-    far_block = hop(far_block)
-    partial = partial + product(far_block, 2 * near - 1)
-    far_block = hop(half_of(far_block))
-    partial = partial + place_half(product(far_block, 2 * near))
+        partial = partial + product(near_block, step) + product(far_block, far + step - 1)
+        if step == near - 1:
+            moved = jnp.concatenate([near_block, half_of(far_block)], 0)
+        moved = hop(moved)
+    near_block, far_block = moved[:ROWS], moved[ROWS:]
+    partial = partial + product(near_block, near) + place_half(product(far_block, near + far - 1))
     other_partial = swap(partial.astype(jnp.bfloat16))
     total, sent = call(
         functools.partial(total_kernel, dp_size, mp_size),
         [jax.ShapeDtypeStruct((ROWS, width), jnp.float32), rows_type],
-        (near_sum, last_sum, pair_attended, proj_weight, partial),
+        (last_sum, near_sum, pair_attended, proj_weight, partial),
         specs=[IN_VMEM] * 4 + [in_any],
         flops=2 * SLOT * width * width,
         name="total",

time: 108 us -> 103 us (0.954)
  the two profiles are of different devices: /device:TPU:40 before, /device:TPU:4 now
where the time goes in v9:
time: 103 us; the launch traced here: 102 us
  starting transfers between devices  67.2 us (65%)
  waiting for transfers between devices  19.9 us (19%)
  Pallas kernels  8.31 us (8%)
  local copies, waits for them, and re-layouts  3.21 us (3%)
  matrix products  2.6 us (3%)
  between operations  1.09 us (1%)
    ppermute x8, starting transfers between devices, hop(): return lax.ppermute(rows, ('dp', 'mp'), hop_perm)  29.8 us
    ppermute x4, starting transfers between devices, swap(): return lax.ppermute(rows, 'dp', swap_perm)  20.8 us
    ppermute x2, starting transfers between devices, jump(): return lax.ppermute(rows, ('dp', 'mp'), jump_perm)  16.6 us
    ppermute x2, waiting for transfers between devices, jump(): return lax.ppermute(rows, ('dp', 'mp'), jump_perm)  10.9 us
    pallas_call x10, Pallas kernels, call(): pl.pallas_call(kernel, out_shape=outs, in_specs=specs or [IN_VMEM] * len(...  8.31 us
    ppermute x8, waiting for transfers between devices, hop(): return lax.ppermute(rows, ('dp', 'mp'), hop_perm)  4.7 us
    ppermute x4, waiting for transfers between devices, swap(): return lax.ppermute(rows, 'dp', swap_perm)  4.28 us
    unnamed x12, local copies, waits for them, and re-layouts  3.19 us
  transfers between devices with their start and end apart: 14, of which 6 were waited for; matrix products, arithmetic and copies ran while one was open for 3% of the time, Pallas kernels for 7%

profile of v9, /device:TPU:4, one launch (start us, length us, event | category | flops | bytes accessed | tf_op | source)
XLA Modules:
  0.0 102.3 jit_solution(4332201791249571176)
XLA Ops:
  0.6 15.1 %collective-permute-start.1 = (bf16[256,384]{1,0:T(8,128)(2,1)}, bf16[256,384]{1,0:T(8,128)(2,1)S(1)}, u32[]{:S(2)}, u32[]{:S(2)}) collective-permute-start(bf16[256,384]{1,0:T(8,128)(2,1)} %out_grad_hbm.1), channel_id=1, source_target_pairs={{0,512},{16,528},{32,544},{48,560},{64,576},{80,592},{96,608},{112... | collective-permute-start | bytes 589832 | tf_op jit(solution)/shard_map/ppermute | solution.py:304
  15.7 0.8 copy-done.5
  16.5 2.2 %attention_forward.1 = (bf16[256,384]{1,0:T(8,128)(2,1)S(1)}, bf16[256,384]{1,0:T(8,128)(2,1)S(1)}, s32[2,256]{1,0:T(2,128)S(1)}) custom-call(bf16[256,384]{1,0:T(8,128)(2,1)} %query_ref.1, bf16[256,384]{1,0:T(8,128)(2,1)} %key_ref.1, bf16[256,384]{1,0:T(8,128)(2,1)} %value_ref.1, bf16[256,384]{1,0:T(8,128)(2,1)} %out_grad_hbm.1, s32[64,256]{1,0:T(8,128)S(1)} %copy-done.5), custom_call_target="tpu_custom_call" | custom-call | flops 100663296 | bytes 1247232 | tf_op jit(solution)/shard_map/attention_forward/pallas_call | solution.py:43
  18.8 1.9 %collective-permute-start = (bf16[256,384]{1,0:T(8,128)(2,1)S(1)}, bf16[256,384]{1,0:T(8,128)(2,1)S(1)}, u32[]{:S(2)}, u32[]{:S(2)}) collective-permute-start(bf16[256,384]{1,0:T(8,128)(2,1)S(1)} %get-tuple-element.16.own_ref), channel_id=1, source_target_pairs={{0,512},{16,528},{32,544},{48,560},{64,576},{80,592},{96,608},{112... | collective-permute-start | bytes 589832 | tf_op jit(solution)/shard_map/ppermute | solution.py:304
  20.7 0.3 pack_out_grad.1.earlier_ref
  21.0 9.8 %collective-permute-start.7 = (bf16[256,384]{1,0:T(8,128)(2,1)S(1)}, bf16[256,384]{1,0:T(8,128)(2,1)S(1)}, u32[]{:S(2)}, u32[]{:S(2)}) collective-permute-start(bf16[256,384]{1,0:T(8,128)(2,1)S(1)} %pack_out_grad.1.earlier_ref), channel_id=1, source_target_pairs={{0,5},{1,6},{2,7},{3,8},{4,9},{5,10},{6,11},{7,12},{8,13},{9,14},{... | collective-permute-start | bytes 589832 | tf_op jit(solution)/shard_map/ppermute | solution.py:301
  30.8 2.5 %collective-permute-start.8 = (bf16[256,384]{1,0:T(8,128)(2,1)S(1)}, bf16[256,384]{1,0:T(8,128)(2,1)S(1)}, u32[]{:S(2)}, u32[]{:S(2)}) collective-permute-start(bf16[256,384]{1,0:T(8,128)(2,1)S(1)} %pack_out_grad.1.earlier_ref), channel_id=1, source_target_pairs={{0,1},{1,2},{2,3},{3,4},{4,5},{5,6},{6,7},{7,8},{8,9},{9,10},{10,1... | collective-permute-start | bytes 589832 | tf_op jit(solution)/shard_map/ppermute | solution.py:298
  33.4 2.3 %copy-done = bf16[384,6144]{1,0:T(8,128)(2,1)S(1)} copy-done((bf16[384,6144]{1,0:T(8,128)(2,1)S(1)}, bf16[384,6144]{1,0:T(8,128)(2,1)}, u32[]{:S(2)}) %copy-start) | copy-done | bytes 4718616
  35.7 0.6 pack_attended.1
  36.3 2.7 %collective-permute-start.2 = (bf16[384,384]{1,0:T(8,128)(2,1)S(1)}, bf16[384,384]{1,0:T(8,128)(2,1)S(1)}, u32[]{:S(2)}, u32[]{:S(2)}) collective-permute-start(bf16[384,384]{1,0:T(8,128)(2,1)S(1)} %get-tuple-element.19.earlier_ref), channel_id=1, source_target_pairs={{0,1},{1,2},{2,3},{3,4},{4,5},{5,6},{6,7},{7,8},{8,9},{9,10},{10,1... | collective-permute-start | bytes 884744 | tf_op jit(solution)/shard_map/ppermute | solution.py:298
  39.0 3.4 %collective-permute-done.7.far_ref = bf16[256,384]{1,0:T(8,128)(2,1)S(1)} collective-permute-done((bf16[256,384]{1,0:T(8,128)(2,1)S(1)}, bf16[256,384]{1,0:T(8,128)(2,1)S(1)}, u32[]{:S(2)}, u32[]{:S(2)}) %collective-permute-start.7) | collective-permute-done | bytes 196640 | tf_op jit(solution)/shard_map/ppermute | solution.py:301
  42.4 2.3 %collective-permute-done.8.near_ref = bf16[256,384]{1,0:T(8,128)(2,1)S(1)} collective-permute-done((bf16[256,384]{1,0:T(8,128)(2,1)S(1)}, bf16[256,384]{1,0:T(8,128)(2,1)S(1)}, u32[]{:S(2)}, u32[]{:S(2)}) %collective-permute-start.8) | collective-permute-done | bytes 196640 | tf_op jit(solution)/shard_map/ppermute | solution.py:298
  44.7 5.4 %collective-permute-start.9 = (bf16[512,384]{1,0:T(8,128)(2,1)S(1)}, bf16[512,384]{1,0:T(8,128)(2,1)S(1)}, u32[]{:S(2)}, u32[]{:S(2)}) collective-permute-start(bf16[512,384]{1,0:T(8,128)(2,1)S(1)} %join_out_grad.1), channel_id=1, source_target_pairs={{0,1},{1,2},{2,3},{3,4},{4,5},{5,6},{6,7},{7,8},{8,9},{9,10},{10,1... | collective-permute-start | bytes 1179656 | tf_op jit(solution)/shard_map/ppermute | solution.py:298
  50.7 0.4 add_terms.3
  51.1 2.5 %collective-permute-start.3 = (bf16[512,384]{1,0:T(8,128)(2,1)S(1)}, bf16[512,384]{1,0:T(8,128)(2,1)S(1)}, u32[]{:S(2)}, u32[]{:S(2)}) collective-permute-start(bf16[512,384]{1,0:T(8,128)(2,1)S(1)} %add_terms.3), channel_id=1, source_target_pairs={{0,1},{1,2},{2,3},{3,4},{4,5},{5,6},{6,7},{7,8},{8,9},{9,10},{10,1... | collective-permute-start | bytes 1179656 | tf_op jit(solution)/shard_map/ppermute | solution.py:298
  53.6 1.8 %collective-permute-done.9 = bf16[512,384]{1,0:T(8,128)(2,1)S(1)} collective-permute-done((bf16[512,384]{1,0:T(8,128)(2,1)S(1)}, bf16[512,384]{1,0:T(8,128)(2,1)S(1)}, u32[]{:S(2)}, u32[]{:S(2)}) %collective-permute-start.9) | collective-permute-done | bytes 393248 | tf_op jit(solution)/shard_map/ppermute | solution.py:298
  55.4 5.6 %collective-permute-start.10 = (bf16[512,384]{1,0:T(8,128)(2,1)S(1)}, bf16[512,384]{1,0:T(8,128)(2,1)S(1)}, u32[]{:S(2)}, u32[]{:S(2)}) collective-permute-start(bf16[512,384]{1,0:T(8,128)(2,1)S(1)} %collective-permute-done.9), channel_id=1, source_target_pairs={{0,1},{1,2},{2,3},{3,4},{4,5},{5,6},{6,7},{7,8},{8,9},{9,10},{10,1... | collective-permute-start | bytes 1179656 | tf_op jit(solution)/shard_map/ppermute | solution.py:298
  61.6 0.4 add_terms.4
  62.0 3.6 %collective-permute-start.4 = (bf16[512,384]{1,0:T(8,128)(2,1)S(1)}, bf16[512,384]{1,0:T(8,128)(2,1)S(1)}, u32[]{:S(2)}, u32[]{:S(2)}) collective-permute-start(bf16[512,384]{1,0:T(8,128)(2,1)S(1)} %add_terms.4), channel_id=1, source_target_pairs={{0,1},{1,2},{2,3},{3,4},{4,5},{5,6},{6,7},{7,8},{8,9},{9,10},{10,1... | collective-permute-start | bytes 1179656 | tf_op jit(solution)/shard_map/ppermute | solution.py:298
  65.6 0.7 collective-permute-done.10
  66.3 5.6 %collective-permute-start.11 = (bf16[384,384]{1,0:T(8,128)(2,1)S(1)}, bf16[384,384]{1,0:T(8,128)(2,1)S(1)}, u32[]{:S(2)}, u32[]{:S(2)}) collective-permute-start(bf16[384,384]{1,0:T(8,128)(2,1)S(1)} %pad_maximum_fusion), channel_id=1, source_target_pairs={{0,1},{1,2},{2,3},{3,4},{4,5},{5,6},{6,7},{7,8},{8,9},{9,10},{10,1... | collective-permute-start | bytes 884744 | tf_op jit(solution)/shard_map/ppermute | solution.py:298
  72.0 0.3 fusion.2
  72.6 0.4 add_terms.5
  73.0 6.8 %collective-permute-start.5 = (bf16[256,384]{1,0:T(8,128)(2,1)S(1)}, bf16[256,384]{1,0:T(8,128)(2,1)S(1)}, u32[]{:S(2)}, u32[]{:S(2)}) collective-permute-start(bf16[256,384]{1,0:T(8,128)(2,1)S(1)} %get-tuple-element.21), channel_id=1, source_target_pairs={{0,5},{1,6},{2,7},{3,8},{4,9},{5,10},{6,11},{7,12},{8,13},{9,14},{... | collective-permute-start | bytes 589832 | tf_op jit(solution)/shard_map/ppermute | solution.py:301
  79.9 1.9 %collective-permute-start.6 = (bf16[256,384]{1,0:T(8,128)(2,1)S(1)}, bf16[256,384]{1,0:T(8,128)(2,1)S(1)}, u32[]{:S(2)}, u32[]{:S(2)}) collective-permute-start(bf16[256,384]{1,0:T(8,128)(2,1)S(1)} %get-tuple-element.22), channel_id=1, source_target_pairs={{0,1},{1,2},{2,3},{3,4},{4,5},{5,6},{6,7},{7,8},{8,9},{9,10},{10,1... | collective-permute-start | bytes 589832 | tf_op jit(solution)/shard_map/ppermute | solution.py:298
  82.4 0.3 fusion.41
  82.7 1.9 %collective-permute-start.13 = (bf16[256,384]{1,0:T(8,128)(2,1)S(1)}, bf16[256,384]{1,0:T(8,128)(2,1)S(1)}, u32[]{:S(2)}, u32[]{:S(2)}) collective-permute-start(bf16[256,384]{1,0:T(8,128)(2,1)S(1)} %get-tuple-element.32), channel_id=1, source_target_pairs={{0,512},{16,528},{32,544},{48,560},{64,576},{80,592},{96,608},{112... | collective-permute-start | bytes 589832 | tf_op jit(solution)/shard_map/ppermute | solution.py:304
  84.6 7.5 %collective-permute-done.5.last_ref = bf16[256,384]{1,0:T(8,128)(2,1)S(1)} collective-permute-done((bf16[256,384]{1,0:T(8,128)(2,1)S(1)}, bf16[256,384]{1,0:T(8,128)(2,1)S(1)}, u32[]{:S(2)}, u32[]{:S(2)}) %collective-permute-start.5) | collective-permute-done | bytes 196640 | tf_op jit(solution)/shard_map/ppermute | solution.py:301
  92.4 1.9 %collective-permute-start.12 = (bf16[256,384]{1,0:T(8,128)(2,1)S(1)}, bf16[256,384]{1,0:T(8,128)(2,1)S(1)}, u32[]{:S(2)}, u32[]{:S(2)}) collective-permute-start(bf16[256,384]{1,0:T(8,128)(2,1)S(1)} %get-tuple-element.24), channel_id=1, source_target_pairs={{0,512},{16,528},{32,544},{48,560},{64,576},{80,592},{96,608},{112... | collective-permute-start | bytes 589832 | tf_op jit(solution)/shard_map/ppermute | solution.py:304
  94.3 2.8 %attention_backward.1 = (bf16[256,384]{1,0:T(8,128)(2,1)}, bf16[256,384]{1,0:T(8,128)(2,1)}, bf16[256,384]{1,0:T(8,128)(2,1)}) custom-call(bf16[256,384]{1,0:T(8,128)(2,1)S(1)} %copy-done.2, bf16[256,384]{1,0:T(8,128)(2,1)S(1)} %copy-done.3, bf16[256,384]{1,0:T(8,128)(2,1)S(1)} %copy-done.4, f32[256,384]{1,0:T(8,128)S(1)} %get-tuple-element.33.earlier_ref.partial_ref, ...), custom_call_target="tpu_custom_call" | custom-call | flops 301989888 | bytes 1771520 | tf_op jit(solution)/shard_map/attention_backward/pallas_call | solution.py:43
  97.2 4.3 %collective-permute-done.12.other_ref = bf16[256,384]{1,0:T(8,128)(2,1)S(1)} collective-permute-done((bf16[256,384]{1,0:T(8,128)(2,1)S(1)}, bf16[256,384]{1,0:T(8,128)(2,1)S(1)}, u32[]{:S(2)}, u32[]{:S(2)}) %collective-permute-start.12) | collective-permute-done | bytes 196640 | tf_op jit(solution)/shard_map/ppermute | solution.py:304
  101.4 0.9 finish_projected.1
  (30 shorter events, 2.3 us)
Async XLA Ops:
  0.6 20.1 %collective-permute-start.1 = (bf16[256,384]{1,0:T(8,128)(2,1)}, bf16[256,384]{1,0:T(8,128)(2,1)S(1)}, u32[]{:S(2)}, u32[]{:S(2)}) collective-permute-start(bf16[256,384]{1,0:T(8,128)(2,1)} %out_grad_hbm.1), channel_id=1, source_target_pairs={{0,512},{16,528},{32,544},{48,560},{64,576},{80,592},{96,608},{112... | collective-permute-start | bytes 589832 | tf_op jit(solution)/shard_map/ppermute | solution.py:304
  15.7 0.8 copy-start.5
  18.8 14.6 %collective-permute-start = (bf16[256,384]{1,0:T(8,128)(2,1)S(1)}, bf16[256,384]{1,0:T(8,128)(2,1)S(1)}, u32[]{:S(2)}, u32[]{:S(2)}) collective-permute-start(bf16[256,384]{1,0:T(8,128)(2,1)S(1)} %get-tuple-element.16.own_ref), channel_id=1, source_target_pairs={{0,512},{16,528},{32,544},{48,560},{64,576},{80,592},{96,608},{112... | collective-permute-start | bytes 589832 | tf_op jit(solution)/shard_map/ppermute | solution.py:304
  21.0 21.4 %collective-permute-start.7 = (bf16[256,384]{1,0:T(8,128)(2,1)S(1)}, bf16[256,384]{1,0:T(8,128)(2,1)S(1)}, u32[]{:S(2)}, u32[]{:S(2)}) collective-permute-start(bf16[256,384]{1,0:T(8,128)(2,1)S(1)} %pack_out_grad.1.earlier_ref), channel_id=1, source_target_pairs={{0,5},{1,6},{2,7},{3,8},{4,9},{5,10},{6,11},{7,12},{8,13},{9,14},{... | collective-permute-start | bytes 589832 | tf_op jit(solution)/shard_map/ppermute | solution.py:301
  30.8 13.9 %collective-permute-start.8 = (bf16[256,384]{1,0:T(8,128)(2,1)S(1)}, bf16[256,384]{1,0:T(8,128)(2,1)S(1)}, u32[]{:S(2)}, u32[]{:S(2)}) collective-permute-start(bf16[256,384]{1,0:T(8,128)(2,1)S(1)} %pack_out_grad.1.earlier_ref), channel_id=1, source_target_pairs={{0,1},{1,2},{2,3},{3,4},{4,5},{5,6},{6,7},{7,8},{8,9},{9,10},{10,1... | collective-permute-start | bytes 589832 | tf_op jit(solution)/shard_map/ppermute | solution.py:298
  33.4 2.3 %copy-start = (bf16[384,6144]{1,0:T(8,128)(2,1)S(1)}, bf16[384,6144]{1,0:T(8,128)(2,1)}, u32[]{:S(2)}) copy-start(bf16[384,6144]{1,0:T(8,128)(2,1)} %weight_ref.9) | copy-start | bytes 14155780
  35.7 14.4 %copy-start.1 = (bf16[384,6144]{1,0:T(8,128)(2,1)S(1)}, bf16[384,6144]{1,0:T(8,128)(2,1)}, u32[]{:S(2)}) copy-start(bf16[384,6144]{1,0:T(8,128)(2,1)} %weight_ref.9) | copy-start | bytes 14155780
  36.3 14.4 %collective-permute-start.2 = (bf16[384,384]{1,0:T(8,128)(2,1)S(1)}, bf16[384,384]{1,0:T(8,128)(2,1)S(1)}, u32[]{:S(2)}, u32[]{:S(2)}) collective-permute-start(bf16[384,384]{1,0:T(8,128)(2,1)S(1)} %get-tuple-element.19.earlier_ref), channel_id=1, source_target_pairs={{0,1},{1,2},{2,3},{3,4},{4,5},{5,6},{6,7},{7,8},{8,9},{9,10},{10,1... | collective-permute-start | bytes 884744 | tf_op jit(solution)/shard_map/ppermute | solution.py:298
  44.7 10.7 %collective-permute-start.9 = (bf16[512,384]{1,0:T(8,128)(2,1)S(1)}, bf16[512,384]{1,0:T(8,128)(2,1)S(1)}, u32[]{:S(2)}, u32[]{:S(2)}) collective-permute-start(bf16[512,384]{1,0:T(8,128)(2,1)S(1)} %join_out_grad.1), channel_id=1, source_target_pairs={{0,1},{1,2},{2,3},{3,4},{4,5},{5,6},{6,7},{7,8},{8,9},{9,10},{10,1... | collective-permute-start | bytes 1179656 | tf_op jit(solution)/shard_map/ppermute | solution.py:298
  51.1 10.5 %collective-permute-start.3 = (bf16[512,384]{1,0:T(8,128)(2,1)S(1)}, bf16[512,384]{1,0:T(8,128)(2,1)S(1)}, u32[]{:S(2)}, u32[]{:S(2)}) collective-permute-start(bf16[512,384]{1,0:T(8,128)(2,1)S(1)} %add_terms.3), channel_id=1, source_target_pairs={{0,1},{1,2},{2,3},{3,4},{4,5},{5,6},{6,7},{7,8},{8,9},{9,10},{10,1... | collective-permute-start | bytes 1179656 | tf_op jit(solution)/shard_map/ppermute | solution.py:298
  55.4 10.9 %collective-permute-start.10 = (bf16[512,384]{1,0:T(8,128)(2,1)S(1)}, bf16[512,384]{1,0:T(8,128)(2,1)S(1)}, u32[]{:S(2)}, u32[]{:S(2)}) collective-permute-start(bf16[512,384]{1,0:T(8,128)(2,1)S(1)} %collective-permute-done.9), channel_id=1, source_target_pairs={{0,1},{1,2},{2,3},{3,4},{4,5},{5,6},{6,7},{7,8},{8,9},{9,10},{10,1... | collective-permute-start | bytes 1179656 | tf_op jit(solution)/shard_map/ppermute | solution.py:298
  62.0 10.6 %collective-permute-start.4 = (bf16[512,384]{1,0:T(8,128)(2,1)S(1)}, bf16[512,384]{1,0:T(8,128)(2,1)S(1)}, u32[]{:S(2)}, u32[]{:S(2)}) collective-permute-start(bf16[512,384]{1,0:T(8,128)(2,1)S(1)} %add_terms.4), channel_id=1, source_target_pairs={{0,1},{1,2},{2,3},{3,4},{4,5},{5,6},{6,7},{7,8},{8,9},{9,10},{10,1... | collective-permute-start | bytes 1179656 | tf_op jit(solution)/shard_map/ppermute | solution.py:298
  66.3 15.4 %collective-permute-start.11 = (bf16[384,384]{1,0:T(8,128)(2,1)S(1)}, bf16[384,384]{1,0:T(8,128)(2,1)S(1)}, u32[]{:S(2)}, u32[]{:S(2)}) collective-permute-start(bf16[384,384]{1,0:T(8,128)(2,1)S(1)} %pad_maximum_fusion), channel_id=1, source_target_pairs={{0,1},{1,2},{2,3},{3,4},{4,5},{5,6},{6,7},{7,8},{8,9},{9,10},{10,1... | collective-permute-start | bytes 884744 | tf_op jit(solution)/shard_map/ppermute | solution.py:298
  73.0 19.1 %collective-permute-start.5 = (bf16[256,384]{1,0:T(8,128)(2,1)S(1)}, bf16[256,384]{1,0:T(8,128)(2,1)S(1)}, u32[]{:S(2)}, u32[]{:S(2)}) collective-permute-start(bf16[256,384]{1,0:T(8,128)(2,1)S(1)} %get-tuple-element.21), channel_id=1, source_target_pairs={{0,5},{1,6},{2,7},{3,8},{4,9},{5,10},{6,11},{7,12},{8,13},{9,14},{... | collective-permute-start | bytes 589832 | tf_op jit(solution)/shard_map/ppermute | solution.py:301
  79.9 12.3 %collective-permute-start.6 = (bf16[256,384]{1,0:T(8,128)(2,1)S(1)}, bf16[256,384]{1,0:T(8,128)(2,1)S(1)}, u32[]{:S(2)}, u32[]{:S(2)}) collective-permute-start(bf16[256,384]{1,0:T(8,128)(2,1)S(1)} %get-tuple-element.22), channel_id=1, source_target_pairs={{0,1},{1,2},{2,3},{3,4},{4,5},{5,6},{6,7},{7,8},{8,9},{9,10},{10,1... | collective-permute-start | bytes 589832 | tf_op jit(solution)/shard_map/ppermute | solution.py:298
  82.0 12.3 %copy-start.2 = (bf16[256,384]{1,0:T(8,128)(2,1)S(1)}, bf16[256,384]{1,0:T(8,128)(2,1)}, u32[]{:S(2)}) copy-start(bf16[256,384]{1,0:T(8,128)(2,1)} %query_ref.1) | copy-start | bytes 589828
  82.1 12.3 %copy-start.3 = (bf16[256,384]{1,0:T(8,128)(2,1)S(1)}, bf16[256,384]{1,0:T(8,128)(2,1)}, u32[]{:S(2)}) copy-start(bf16[256,384]{1,0:T(8,128)(2,1)} %key_ref.1) | copy-start | bytes 589828
  82.1 12.3 %copy-start.4 = (bf16[256,384]{1,0:T(8,128)(2,1)S(1)}, bf16[256,384]{1,0:T(8,128)(2,1)}, u32[]{:S(2)}) copy-start(bf16[256,384]{1,0:T(8,128)(2,1)} %value_ref.1) | copy-start | bytes 589828
  82.7 11.6 %collective-permute-start.13 = (bf16[256,384]{1,0:T(8,128)(2,1)S(1)}, bf16[256,384]{1,0:T(8,128)(2,1)S(1)}, u32[]{:S(2)}, u32[]{:S(2)}) collective-permute-start(bf16[256,384]{1,0:T(8,128)(2,1)S(1)} %get-tuple-element.32), channel_id=1, source_target_pairs={{0,512},{16,528},{32,544},{48,560},{64,576},{80,592},{96,608},{112... | collective-permute-start | bytes 589832 | tf_op jit(solution)/shard_map/ppermute | solution.py:304
  92.4 9.1 %collective-permute-start.12 = (bf16[256,384]{1,0:T(8,128)(2,1)S(1)}, bf16[256,384]{1,0:T(8,128)(2,1)S(1)}, u32[]{:S(2)}, u32[]{:S(2)}) collective-permute-start(bf16[256,384]{1,0:T(8,128)(2,1)S(1)} %get-tuple-element.24), channel_id=1, source_target_pairs={{0,512},{16,528},{32,544},{48,560},{64,576},{80,592},{96,608},{112... | collective-permute-start | bytes 589832 | tf_op jit(solution)/shard_map/ppermute | solution.py:304
